TPU v7x, 512 devices: a whole 4x4x16 slice. The times are simulated.
512 devices in a mesh: dp: 16 (over z_hi, y, core), loop: 32 (over z_lo, x).
Axes of the slice: x: 4, y: 4, z: 16 (z_hi: 2, z_lo: 8; z = z_hi * 8 + z_lo), core: 2. Of those that a mesh axis runs over, the one named last changes fastest.
Arguments:
- image_embeds: bfloat16 [65536, 1152], P(('dp', 'loop')), may hold values from -0.6 to 0.6
- text_embeds: bfloat16 [65536, 1152], P(('dp', 'loop')), may hold values from -0.6 to 0.6
- log_scale: float32 [1], replicated, may hold values from 2 to 2.7
- logit_bias: float32 [1], replicated, may hold values from -8 to -5
Outputs:
- loss: float32 [1], replicated
- image_grad: bfloat16 [65536, 1152], P(('dp', 'loop'))
- text_grad: bfloat16 [65536, 1152], P(('dp', 'loop'))
- grad_log_scale: float32 [1], replicated
- grad_bias: float32 [1], replicated
All inputs are finite; a program needn't handle non-finite values.
Results may differ from a plain program's by a relative error of at most 0.0065.
Values may be sent and summed in bfloat16 or wider, within the bound.
No kernel may reach another device: no remote copies, remote signals or barrier semaphores. Data moves between devices by JAX's collectives and lax.ppermute only.
A program may use at most 64 MiB of HBM per device.

v0:
```python
import jax
import jax.numpy as jnp
from jax import lax
from jax.sharding import PartitionSpec as P

EPSILON = 1e-06


def unit_rows(matrix):
    floats = matrix.astype(jnp.float32)
    return floats * lax.rsqrt(jnp.sum(floats * floats, axis=1, keepdims=True) + EPSILON)


def unit_pull(matrix, cotangent):
    _, pullback = jax.vjp(unit_rows, matrix.astype(jnp.float32))
    return pullback(cotangent)[0]


def pair_terms(image_block, text_block, row_first, col_first, temper, offset):
    products = lax.dot_general(
        image_block, text_block, (((1,), (1,)), ((), ())), preferred_element_type=jnp.float32
    )
    scaled = temper * products
    logits = scaled + offset
    row_ids = row_first + jnp.arange(image_block.shape[0], dtype=jnp.int32)
    col_ids = col_first + jnp.arange(text_block.shape[0], dtype=jnp.int32)
    positive = row_ids[:, None] == col_ids[None, :]
    signs = jnp.where(positive, jnp.float32(-1.0), jnp.float32(1.0))
    losses = jax.nn.softplus(signs * logits)
    coef = jax.nn.sigmoid(logits) - positive.astype(jnp.float32)
    return (coef, jnp.sum(losses), jnp.sum(coef * scaled), jnp.sum(coef))


def on_device(image_embeds, text_embeds, log_scale, logit_bias):
    row_count = image_embeds.shape[0]
    temper = jnp.exp(log_scale[0])
    offset = logit_bias[0]
    image_unit = unit_rows(image_embeds).astype(jnp.bfloat16)
    text_unit = unit_rows(text_embeds).astype(jnp.bfloat16)
    dp_index = lax.axis_index("dp")
    dp_count = lax.axis_size("dp")
    own_first = dp_index * row_count
    images_all, texts_all = (
        lax.all_gather(image_unit, "dp", axis=0, tiled=True),
        lax.all_gather(text_unit, "dp", axis=0, tiled=True),
    )
    coef_rows, loss_part, scale_part, bias_part = pair_terms(
        image_unit, texts_all, own_first, 0, temper, offset
    )
    image_cot = temper * jnp.dot(
        coef_rows.astype(jnp.bfloat16), texts_all, preferred_element_type=jnp.float32
    )
    coef_cols, _, _, _ = pair_terms(images_all, text_unit, 0, own_first, temper, offset)
    text_cot = temper * lax.dot_general(
        coef_cols.astype(jnp.bfloat16),
        images_all,
        (((0,), (0,)), ((), ())),
        preferred_element_type=jnp.float32,
    )
    loss_total, scale_total, bias_total = lax.psum(
        (loss_part, scale_part, bias_part), ("dp", "loop")
    )
    batch_total = row_count * dp_count * lax.axis_size("loop")
    image_grad = unit_pull(image_embeds, image_cot).astype(jnp.bfloat16)
    text_grad = unit_pull(text_embeds, text_cot).astype(jnp.bfloat16)
    return (
        jnp.reshape(loss_total / batch_total, (1,)),
        image_grad,
        text_grad,
        jnp.reshape(scale_total, (1,)),
        jnp.reshape(bias_total, (1,)),
    )


def solution(mesh):
    return jax.shard_map(
        on_device,
        mesh=mesh,
        in_specs=(P(("dp", "loop"), None), P(("dp", "loop"), None), P(), P()),
        out_specs=(P(), P(("dp", "loop"), None), P(("dp", "loop"), None), P(), P()),
        check_vma=False,
    )
```

profile of v0, /device:TPU:1, one launch (start us, length us, event | category | flops | bytes accessed | tf_op | source)
XLA Modules:
  0.0 387.2 jit_solution(7892680599499120050)
XLA Ops:
  7.2 0.0 all-gather.5.cloned.1.call-start
  7.2 1.1 fusion.10
  8.3 1.8 fusion.11
  10.1 0.0 all-gather.5.cloned.1.call-update
  10.1 0.0 all-gather.3.cloned.1.call-start
  10.2 1.1 fusion.13
  11.3 1.8 fusion.14
  13.1 0.0 all-gather.3.cloned.1.call-update
  14.5 130.9 %all-gather.5.cloned.1.call-done = bf16[2048,1152]{1,0:T(8,128)(2,1)} async-done(((bf16[128,1152]{1,0:T(8,128)(2,1)}), bf16[2048,1152]{1,0:T(8,128)(2,1)}) %all-gather.5.cloned.1.call-update) | async-done | bytes 4718608 | tf_op jit(solution)/shard_map/all_gather | solution.py:44
  145.4 0.0 copy-start.2
  145.4 7.2 %fusion.15 = (f32[128]{0:T(128)S(1)}, f32[128,1152]{1,0:T(8,128)S(1)}) fusion(bf16[128,1152]{1,0:T(8,128)(2,1)} %param.5, bf16[2048,1152]{1,0:T(8,128)(2,1)} %all-gather.5.cloned.1.call-done, s32[128]{0:T(128)S(1)} %iota_add_fusion, f32[]{:T(128)} %bitcast.11, f32[]{:T(128)} %bitcast, f32[128]{0:T(128)S(1)} %add_rsqrt_fusion), kind=kOutput, calls=%fused_computation.34 | convolution fusion | flops 1211350912 | bytes 5604872 | tf_op jit(solution)/shard_map/dot_general | solution.py:54
  152.6 116.3 %all-gather.3.cloned.1.call-done = bf16[2048,1152]{1,0:T(8,128)(2,1)} async-done(((bf16[128,1152]{1,0:T(8,128)(2,1)}), bf16[2048,1152]{1,0:T(8,128)(2,1)}) %all-gather.3.cloned.1.call-update) | async-done | bytes 4718608 | tf_op jit(solution)/shard_map/all_gather | solution.py:45
  268.9 0.0 copy-done.2
  268.9 0.0 copy-start.1
  268.9 0.0 copy-start.3
  268.9 5.5 %fusion.22 = (f32[]{:T(128)}, f32[]{:T(128)}, f32[]{:T(128)}, f32[128,2048]{1,0:T(8,128)S(1)}) fusion(s32[128]{0:T(128)S(1)} %iota_add_fusion, f32[]{:T(128)} %bitcast.10, bf16[128,1152]{1,0:T(8,128)(2,1)S(1)} %copy-done.2, bf16[2048,1152]{1,0:T(8,128)(2,1)} %all-gather.3.cloned.1.call-done, f32[]{:T(128)} %bitcast), kind=kOutput, calls=%fused_computation.46 | convolution fusion | flops 609222656 | bytes 6062612 | tf_op jit(solution)/shard_map/dot_general | solution.py:20
  274.4 0.0 copy-done.1
  274.4 0.0 copy-done.3
  274.4 0.0 copy-start
  274.4 1.1 fusion.12
  275.5 0.0 copy-done
  275.5 0.9 fusion.9
  276.4 0.9 fusion.8
  277.3 101.3 %all-reduce = (f32[]{:T(128)}, f32[1]{0:T(128)}, f32[1]{0:T(128)}) all-reduce(f32[]{:T(128)} %get-tuple-element.7, f32[1]{0:T(128)} %bitcast.3, f32[1]{0:T(128)} %bitcast.4), channel_id=1, replica_groups=mesh['dp'=16,'loop'=32] {'dp','loop'}, use_global_device_ids=true, to_apply=%region_3.4 | all-reduce | flops 3 | bytes 24 | tf_op jit(solution)/shard_map/psum | solution.py:60
  (5 shorter events, 0.0 us)
Async XLA Ops:
  7.2 138.2 %all-gather.5.cloned.1.call-start = ((), (), s32[]{:S(2)}) async-start(), calls=%async_computation.1 | async-start | bytes 5013504 | tf_op jit(solution)/shard_map/all_gather | solution.py:44
  10.1 258.8 %all-gather.3.cloned.1.call-start = ((), (), s32[]{:S(2)}) async-start(), calls=%async_computation | async-start | bytes 5013504 | tf_op jit(solution)/shard_map/all_gather | solution.py:45
  145.4 123.6 %copy-start.2 = (bf16[128,1152]{1,0:T(8,128)(2,1)S(1)}, bf16[128,1152]{1,0:T(8,128)(2,1)}, u32[]{:S(2)}) copy-start(bf16[128,1152]{1,0:T(8,128)(2,1)} %fusion.11) | copy-start | bytes 884740
  268.9 5.5 %copy-start.1 = (bf16[128,1152]{1,0:T(8,128)(2,1)S(1)}, bf16[128,1152]{1,0:T(8,128)(2,1)}, u32[]{:S(2)}) copy-start(bf16[128,1152]{1,0:T(8,128)(2,1)} %param.4) | copy-start | bytes 884740
  268.9 5.5 %copy-start.3 = (bf16[2048,1152]{1,0:T(8,128)(2,1)S(1)}, bf16[2048,1152]{1,0:T(8,128)(2,1)}, u32[]{:S(2)}) copy-start(bf16[2048,1152]{1,0:T(8,128)(2,1)} %all-gather.3.cloned.1.call-done) | copy-start | bytes 14155780
  274.4 1.1 copy-start
Sparse Core Ops, SparseCore 0:
  11.9 133.4 all-gather.4
  149.2 119.6 all-gather.2
where the time goes:
time: 388 us; the launch traced here: 387 us
  waiting for transfers between devices  247 us (64%)
  blocking collectives  101 us (26%)
  between operations  17.2 us (4%)
  matrix products  13.7 us (4%)
  other arithmetic  7.62 us (2%)
    all_gather x1, waiting for transfers between devices, on_device(): lax.all_gather(image_unit, 'dp', axis=0, tiled=True)  131 us
    all_gather x1, waiting for transfers between devices, on_device(): lax.all_gather(text_unit, 'dp', axis=0, tiled=True)  116 us
    psum x1, blocking collectives, on_device(): lax.psum((loss_part, scale_part, bias_part), ('dp', 'loop'))  101 us
  transfers between devices with their start and end apart: 2, of which 2 were waited for; matrix products, arithmetic and copies ran while one was open for 3% of the time, Pallas kernels for 0%

commit v1 on v0

v1 whole, which is shorter than its diff:
```python
import jax
import jax.numpy as jnp
from jax import lax
from jax.experimental import pallas as pl
from jax.experimental.pallas import tpu as pltpu
from jax.sharding import Mesh, PartitionSpec as P

EPSILON = 1e-06
F32 = jnp.float32
BF16 = jnp.bfloat16
AXES = ("zh", "y", "c", "zl", "x")
SIZES = (2, 4, 2, 8, 4)

VMEM = pl.BlockSpec(memory_space=pltpu.VMEM)
SMEM = pl.BlockSpec(memory_space=pltpu.SMEM)
PARAMS = pltpu.CompilerParams(vmem_limit_bytes=40 * 1024 * 1024)
SWAP = ((0, 1), (1, 0))
CHUNK = 256


def call(kernel, outs, in_specs, args):
    return pl.pallas_call(
        kernel,
        out_shape=[jax.ShapeDtypeStruct(shape, dtype) for shape, dtype in outs],
        in_specs=in_specs,
        out_specs=[VMEM] * len(outs),
        compiler_params=PARAMS,
    )(*args)


def unit(matrix):
    floats = matrix.astype(F32)
    return (floats * lax.rsqrt(jnp.sum(floats * floats, axis=1, keepdims=True) + EPSILON)).astype(BF16)


def norm_kernel(image_ref, text_ref, image_out, text_out):
    image_out[...] = unit(image_ref[...])
    text = unit(text_ref[...])
    for k in range(text_out.shape[0]):
        text_out[k] = text


def fold(values):
    rows, cols = values.shape
    total = jnp.sum(values.reshape(rows // 8, 8, cols), axis=0)
    return sum(total[:, k * 128 : (k + 1) * 128] for k in range(cols // 128))


def pair_chunk(image, text, temper, offset, positive):
    products = lax.dot_general(image, text, (((1,), (1,)), ((), ())), preferred_element_type=F32)
    scaled = temper * products
    logits = scaled + offset
    small = jnp.exp(-jnp.abs(logits))
    part = 1.0 / (1.0 + small)
    coef = jnp.where(logits >= 0.0, 1.0, small) * part
    signed = logits
    if positive is not None:
        coef = coef - jnp.where(positive, 1.0, 0.0)
        signed = jnp.where(positive, -logits, logits)
    losses = jnp.maximum(signed, 0.0) + jnp.log1p(small)
    return coef, (fold(losses), fold(coef * scaled), fold(coef))


def rows_of(ref, chunk):
    per = CHUNK // 128
    return ref[chunk * per : (chunk + 1) * per].reshape(CHUNK, ref.shape[2])


def pairs(scale_ref, bias_ref, image, mine_ref, sib_ref, coef_mine, coef_sib, y=None):
    temper = jnp.exp(jnp.full((1, CHUNK), scale_ref[0], F32))
    offset = bias_ref[0]
    sums, cot = None, None
    for ref, out in ((mine_ref, coef_mine), (sib_ref, coef_sib)):
        for chunk in range(ref.shape[0] * 128 // CHUNK):
            text = rows_of(ref, chunk)
            positive = None
            if y is not None and ref is mine_ref:
                rows = lax.broadcasted_iota(jnp.int32, (128, CHUNK), 0)
                cols = lax.broadcasted_iota(jnp.int32, (128, CHUNK), 1)
                positive = cols + chunk * CHUNK == rows + y * 128
            coef, terms = pair_chunk(image, text, temper, offset, positive)
            half = coef.astype(BF16)
            out[:, chunk * CHUNK : (chunk + 1) * CHUNK] = half
            part = jnp.dot(half, text, preferred_element_type=F32)
            cot = part if cot is None else cot + part
            sums = terms if sums is None else tuple(a + b for a, b in zip(sums, terms))
    return cot, sums


def own_kernel(scale_ref, bias_ref, y_ref, image_ref, mine_ref, sib_ref, coef_mine, coef_sib, cot_ref, sums_ref):
    cot, sums = pairs(
        scale_ref, bias_ref, image_ref[...], mine_ref, sib_ref, coef_mine, coef_sib, y_ref[0]
    )
    cot_ref[...] = cot
    for k in range(3):
        sums_ref[k] = sums[k]


def cross_kernel(scale_ref, bias_ref, image_ref, mine_ref, sib_ref, before_ref, coef_mine, coef_sib, cot_ref, sums_ref):
    cot, sums = pairs(scale_ref, bias_ref, image_ref[...], mine_ref, sib_ref, coef_mine, coef_sib)
    cot_ref[...] = cot.astype(BF16)
    sums_ref[...] = jnp.zeros_like(sums_ref)
    for k in range(3):
        sums_ref[k : k + 1, :] = jnp.sum(sums[k] + before_ref[k], axis=0, keepdims=True)


def text_part(own_ref, cross_ref, image_ref, image_far_ref, k):
    cols = slice(k * 128, (k + 1) * 128)
    dims = (((0,), (0,)), ((), ()))
    return lax.dot_general(own_ref[:, cols], image_ref[...], dims, preferred_element_type=F32) + lax.dot_general(
        cross_ref[:, cols], image_far_ref[...], dims, preferred_element_type=F32
    )


def text_sib_kernel(own_ref, cross_ref, image_ref, image_far_ref, out_ref):
    for k in range(out_ref.shape[0]):
        out_ref[k] = text_part(own_ref, cross_ref, image_ref, image_far_ref, k).astype(BF16)


def text_mine_kernel(y_ref, own_ref, cross_ref, image_ref, image_far_ref, got_ref, out_ref, kept_ref):
    for k in range(out_ref.shape[0]):
        total = text_part(own_ref, cross_ref, image_ref, image_far_ref, k) + got_ref[k].astype(F32)
        out_ref[k] = total.astype(BF16)

        @pl.when(y_ref[0] == k)
        def _():
            kept_ref[...] = total


def pull(embeds, cot, scale):
    floats = embeds.astype(F32)
    cot = jnp.exp(jnp.full((1, floats.shape[1]), scale, F32)) * cot
    inverse = lax.rsqrt(jnp.sum(floats * floats, axis=1, keepdims=True) + EPSILON)
    along = jnp.sum(cot * floats, axis=1, keepdims=True)
    return (inverse * cot - (inverse * inverse * inverse * along) * floats).astype(BF16)


def image_kernel(scale_ref, embeds_ref, cot_ref, got_ref, out_ref):
    out_ref[...] = pull(embeds_ref[...], cot_ref[...] + got_ref[...].astype(F32), scale_ref[0])


def text_kernel(scale_ref, y_ref, embeds_ref, kept_ref, got_ref, out_ref):
    total = kept_ref[...]
    for k in range(got_ref.shape[0]):
        total = total + jnp.where(y_ref[0] == k, 0.0, got_ref[k].astype(F32))
    out_ref[...] = pull(embeds_ref[...], total, scale_ref[0])


def everyone(values, axes):
    count = lax.axis_size(axes)
    spread = jnp.broadcast_to(values[None], (count,) + values.shape)
    return jnp.sum(lax.all_to_all(spread, axes, 0, 0, tiled=True), axis=0)


def on_device(image_embeds, text_embeds, log_scale, logit_bias):
    rows, width = image_embeds.shape
    y_count = lax.axis_size("y")
    y = jnp.reshape(lax.axis_index("y"), (1,))
    block, blocks = (rows, width), (y_count, rows, width)
    half = (rows, y_count * rows)

    image, text = call(norm_kernel, [(block, BF16), (blocks, BF16)], [VMEM] * 2, (image_embeds, text_embeds))
    image_far = lax.ppermute(image, "zh", SWAP)
    mine = lax.all_to_all(text, "y", 0, 0, tiled=True)
    sib = lax.ppermute(mine, "c", SWAP)

    own_mine, own_sib, image_cot, sums = call(
        own_kernel,
        [(half, BF16), (half, BF16), (block, F32), ((3, 8, 128), F32)],
        [SMEM] * 3 + [VMEM] * 3,
        (log_scale, logit_bias, y, image, mine, sib),
    )
    far_mine, far_sib, far_cot, sums = call(
        cross_kernel,
        [(half, BF16), (half, BF16), (block, BF16), ((8, 128), F32)],
        [SMEM] * 2 + [VMEM] * 4,
        (log_scale, logit_bias, image_far, mine, sib, sums),
    )
    far_got = lax.ppermute(far_cot, "zh", SWAP)

    (text_sib,) = call(text_sib_kernel, [(blocks, BF16)], [VMEM] * 4, (own_sib, far_sib, image, image_far))
    text_got = lax.ppermute(text_sib, "c", SWAP)
    text_send, text_kept = call(
        text_mine_kernel,
        [(blocks, BF16), (block, F32)],
        [SMEM] + [VMEM] * 5,
        (y, own_mine, far_mine, image, image_far, text_got),
    )
    text_parts = lax.all_to_all(text_send, "y", 0, 0, tiled=True)

    totals = everyone(everyone(sums, ("y", "c", "x")), ("zh", "zl"))
    totals = jnp.sum(totals[:3], axis=1)

    (text_grad,) = call(
        text_kernel, [(block, BF16)], [SMEM] * 2 + [VMEM] * 3, (log_scale, y, text_embeds, text_kept, text_parts)
    )
    (image_grad,) = call(
        image_kernel, [(block, BF16)], [SMEM] + [VMEM] * 3, (log_scale, image_embeds, image_cot, far_got)
    )
    batch = rows * lax.axis_size(AXES)
    return totals[0:1] / batch, image_grad, text_grad, totals[1:2], totals[2:3]


def solution(mesh):
    fine = Mesh(mesh.devices.reshape(SIZES), AXES)
    return jax.shard_map(
        on_device,
        mesh=fine,
        in_specs=(P(AXES, None), P(AXES, None), P(), P()),
        out_specs=(P(), P(AXES, None), P(AXES, None), P(), P()),
        check_vma=False,
    )
```

time: 388 us -> 154 us (0.40)
  the two profiles are of different devices: /device:TPU:1 before, /device:TPU:10 now
where the time goes in v1:
time: 154 us; the launch traced here: 153 us
  starting transfers between devices  53.7 us (35%)
  waiting for transfers between devices  46.6 us (30%)
  blocking collectives  31.8 us (21%)
  Pallas kernels  10.1 us (7%)
  local copies, waits for them, and re-layouts  4.99 us (3%)
  between operations  3.89 us (3%)
  other arithmetic  1.91 us (1%)
    ppermute x1, waiting for transfers between devices, on_device(): far_got = lax.ppermute(far_cot, 'zh', SWAP)  29.1 us
    all_to_all x1, starting transfers between devices, everyone(): return jnp.sum(lax.all_to_all(spread, axes, 0, 0, tiled=True), axis=0)  25.4 us
    all_to_all x1, blocking collectives, on_device(): mine = lax.all_to_all(text, 'y', 0, 0, tiled=True)  19.8 us
    ppermute x1, starting transfers between devices, on_device(): image_far = lax.ppermute(image, 'zh', SWAP)  15.7 us
    all_to_all x1, blocking collectives, everyone(): return jnp.sum(lax.all_to_all(spread, axes, 0, 0, tiled=True), axis=0)  12.1 us
    pallas_call x7, Pallas kernels, call(): pl.pallas_call(kernel, out_shape=[jax.ShapeDtypeStruct(shape, dtype) for...  10.1 us
    all_to_all x1, waiting for transfers between devices, everyone(): return jnp.sum(lax.all_to_all(spread, axes, 0, 0, tiled=True), axis=0)  8.85 us
    ppermute x1, waiting for transfers between devices, on_device(): image_far = lax.ppermute(image, 'zh', SWAP)  8.64 us
  transfers between devices with their start and end apart: 6, of which 3 were waited for; matrix products, arithmetic and copies ran while one was open for 2% of the time, Pallas kernels for 4%

profile of v1, /device:TPU:10, one launch (start us, length us, event | category | flops | bytes accessed | tf_op | source)
XLA Modules:
  0.0 153.0 jit_solution(18405985958609575761)
XLA Ops:
  0.6 0.0 copy-start
  0.6 1.0 copy-done
  1.6 0.0 copy-start.2
  1.6 1.0 copy-done.2
  2.6 0.2 shard_map.83
  2.8 19.8 %all_to_all.20.mine_ref = bf16[4,128,1152]{2,1,0:T(8,128)(2,1)S(1)} all-to-all(bf16[4,128,1152]{2,1,0:T(8,128)(2,1)S(1)} %get-tuple-element.18), channel_id=1, replica_groups=mesh['zh'=2,'y'=4,'c'=2,'zl'=8,'x'=4] {'y'}, dimensions={0} | all-to-all | bytes 2359296 | tf_op jit(solution)/shard_map/all_to_all | solution.py:164
  22.6 1.9 %collective-permute-start.1 = (bf16[4,128,1152]{2,1,0:T(8,128)(2,1)S(1)}, bf16[4,128,1152]{2,1,0:T(8,128)(2,1)S(1)}, u32[]{:S(2)}, u32[]{:S(2)}) collective-permute-start(bf16[4,128,1152]{2,1,0:T(8,128)(2,1)S(1)} %all_to_all.20.mine_ref), channel_id=1, source_target_pairs={{0,32},{32,0},{1,33},{33,1},{2,34},{34,2},{3,35},{35,3},{4,36},{36... | collective-permute-start | bytes 3538952 | tf_op jit(solution)/shard_map/ppermute | solution.py:165
  24.5 15.7 %collective-permute-start = (bf16[128,1152]{1,0:T(8,128)(2,1)S(1)}, bf16[128,1152]{1,0:T(8,128)(2,1)S(1)}, u32[]{:S(2)}, u32[]{:S(2)}) collective-permute-start(bf16[128,1152]{1,0:T(8,128)(2,1)S(1)} %get-tuple-element.17.image_ref), channel_id=1, source_target_pairs={{0,256},{256,0},{1,257},{257,1},{2,258},{258,2},{3,259},{259,3},{4... | collective-permute-start | bytes 884744 | tf_op jit(solution)/shard_map/ppermute | solution.py:163
  41.5 0.0 collective-permute-done.1.sib_ref
  41.5 2.2 %shard_map.84 = (bf16[128,512]{1,0:T(8,128)(2,1)S(1)}, bf16[128,512]{1,0:T(8,128)(2,1)S(1)}, f32[128,1152]{1,0:T(8,128)S(1)}, f32[3,8,128]{2,1,0:T(8,128)S(1)}) custom-call(f32[1]{0:T(128)S(6)} %copy.9.scale_ref, f32[1]{0:T(128)S(6)} %copy.10.bias_ref, s32[1]{0:T(128)} %bitcast.y_ref, bf16[128,1152]{1,0:T(8,128)(2,1)S(1)} %get-tuple-element.17.image_ref, ...), custom_call_target="tpu_custom_call" | custom-call | tf_op jit(solution)/shard_map/pallas_call | solution.py:22
  43.8 0.0 copy-start.4
  43.8 8.6 %collective-permute-done.image_ref.image_far_ref = bf16[128,1152]{1,0:T(8,128)(2,1)S(1)} collective-permute-done((bf16[128,1152]{1,0:T(8,128)(2,1)S(1)}, bf16[128,1152]{1,0:T(8,128)(2,1)S(1)}, u32[]{:S(2)}, u32[]{:S(2)}) %collective-permute-start) | collective-permute-done | bytes 294944 | tf_op jit(solution)/shard_map/ppermute | solution.py:163
  52.4 2.2 %shard_map.85 = (bf16[128,512]{1,0:T(8,128)(2,1)S(1)}, bf16[128,512]{1,0:T(8,128)(2,1)S(1)}, bf16[128,1152]{1,0:T(8,128)(2,1)S(1)}, f32[8,128]{1,0:T(8,128)S(1)}) custom-call(f32[1]{0:T(128)S(6)} %copy.9.scale_ref, f32[1]{0:T(128)S(6)} %copy.10.bias_ref, bf16[128,1152]{1,0:T(8,128)(2,1)S(1)} %collective-permute-done.image_ref.image_far_ref, ...), custom_call_target="tpu_custom_call" | custom-call | tf_op jit(solution)/shard_map/pallas_call | solution.py:22
  54.6 0.0 copy-done.4
  54.6 0.0 copy-start.6
  54.6 0.0 copy-start.8
  54.6 0.8 shard_map.87
  55.4 1.9 %collective-permute-start.3 = (bf16[4,128,1152]{2,1,0:T(8,128)(2,1)S(1)}, bf16[4,128,1152]{2,1,0:T(8,128)(2,1)S(1)}, u32[]{:S(2)}, u32[]{:S(2)}) collective-permute-start(bf16[4,128,1152]{2,1,0:T(8,128)(2,1)S(1)} %shard_map.87), channel_id=1, source_target_pairs={{0,32},{32,0},{1,33},{33,1},{2,34},{34,2},{3,35},{35,3},{4,36},{36... | collective-permute-start | bytes 3538952 | tf_op jit(solution)/shard_map/ppermute | solution.py:182
  57.4 0.0 copy-done.6
  57.4 0.0 copy-done.8
  57.4 12.1 %all_to_all.21 = f32[32,8,128]{2,1,0:T(8,128)} all-to-all(f32[32,8,128]{2,1,0:T(8,128)S(1)} %broadcast_in_dim.4), channel_id=1, replica_groups=mesh['zh'=2,'y'=4,'c'=2,'zl'=8,'x'=4] {'y','c','x'}, dimensions={0} | all-to-all | bytes 262144 | tf_op jit(solution)/shard_map/all_to_all | solution.py:152
  69.5 0.9 reduce_sum.27
  70.4 0.6 broadcast_in_dim.5
  71.1 25.4 %all-to-all-start.2 = ((f32[16,8,128]{2,1,0:T(8,128)}), f32[16,8,128]{2,1,0:T(8,128)}, u32[]{:S(2)}, u32[]{:S(2)}) async-start(f32[16,8,128]{2,1,0:T(8,128)} %broadcast_in_dim.5), calls=%async_computation.2 | async-start | bytes 131072 | tf_op jit(solution)/shard_map/all_to_all | solution.py:152
  96.4 0.0 collective-permute-done.3.got_ref
  96.4 0.0 copy-start.5
  96.4 0.9 copy-done.5
  97.3 0.0 copy-start.7
  97.3 0.9 copy-done.7
  98.2 2.5 %shard_map.88 = (bf16[4,128,1152]{2,1,0:T(8,128)(2,1)}, f32[128,1152]{1,0:T(8,128)S(1)}) custom-call(s32[1]{0:T(128)} %bitcast.y_ref, bf16[128,512]{1,0:T(8,128)(2,1)S(1)} %copy-done.5, bf16[128,512]{1,0:T(8,128)(2,1)S(1)} %copy-done.7, bf16[128,1152]{1,0:T(8,128)(2,1)S(1)} %get-tuple-element.17.image_ref, ...), custom_call_target="tpu_custom_call" | custom-call | tf_op jit(solution)/shard_map/pallas_call | solution.py:22
  100.7 8.8 %all-to-all-done.2 = f32[16,8,128]{2,1,0:T(8,128)} async-done(((f32[16,8,128]{2,1,0:T(8,128)}), f32[16,8,128]{2,1,0:T(8,128)}, u32[]{:S(2)}, u32[]{:S(2)}) %all-to-all-start.2) | async-done | bytes 65568 | tf_op jit(solution)/shard_map/all_to_all | solution.py:152
  109.6 0.0 copy-start.9
  109.6 0.0 copy-start.1
  109.6 5.0 %all-to-all-start.3 = ((bf16[4,128,1152]{2,1,0:T(8,128)(2,1)}), bf16[4,128,1152]{2,1,0:T(8,128)(2,1)S(1)}, u32[]{:S(2)}, u32[]{:S(2)}) async-start(bf16[4,128,1152]{2,1,0:T(8,128)(2,1)} %get-tuple-element.28), calls=%async_computation.3 | async-start | bytes 2359296 | tf_op jit(solution)/shard_map/all_to_all | solution.py:189
  114.6 0.0 copy-start.3
  114.6 0.0 copy-done.9
  114.6 3.8 %collective-permute-start.2 = (bf16[128,1152]{1,0:T(8,128)(2,1)S(1)}, bf16[128,1152]{1,0:T(8,128)(2,1)S(1)}, u32[]{:S(2)}, u32[]{:S(2)}) collective-permute-start(bf16[128,1152]{1,0:T(8,128)(2,1)S(1)} %copy-done.9), channel_id=1, source_target_pairs={{0,256},{256,0},{1,257},{257,1},{2,258},{258,2},{3,259},{259,3},{4... | collective-permute-start | bytes 884744 | tf_op jit(solution)/shard_map/ppermute | solution.py:179
  118.4 29.1 %collective-permute-done.2.got_ref = bf16[128,1152]{1,0:T(8,128)(2,1)S(1)} collective-permute-done((bf16[128,1152]{1,0:T(8,128)(2,1)S(1)}, bf16[128,1152]{1,0:T(8,128)(2,1)S(1)}, u32[]{:S(2)}, u32[]{:S(2)}) %collective-permute-start.2) | collective-permute-done | bytes 294944 | tf_op jit(solution)/shard_map/ppermute | solution.py:179
  147.5 0.0 copy-done.1
  147.5 1.0 shard_map.86
  148.4 0.9 reduce_sum.28
  149.3 0.1 slice_reduce_fusion
  149.4 0.6 fusion
  150.7 0.0 all-to-all-done.3.got_ref
  150.7 0.0 copy-done.3
  150.7 1.1 shard_map.89
  (1 shorter events, 0.0 us)
Async XLA Ops:
  0.6 1.0 copy-start
  1.6 1.0 copy-start.2
  22.6 18.9 %collective-permute-start.1 = (bf16[4,128,1152]{2,1,0:T(8,128)(2,1)S(1)}, bf16[4,128,1152]{2,1,0:T(8,128)(2,1)S(1)}, u32[]{:S(2)}, u32[]{:S(2)}) collective-permute-start(bf16[4,128,1152]{2,1,0:T(8,128)(2,1)S(1)} %all_to_all.20.mine_ref), channel_id=1, source_target_pairs={{0,32},{32,0},{1,33},{33,1},{2,34},{34,2},{3,35},{35,3},{4,36},{36... | collective-permute-start | bytes 3538952 | tf_op jit(solution)/shard_map/ppermute | solution.py:165
  24.5 27.9 %collective-permute-start = (bf16[128,1152]{1,0:T(8,128)(2,1)S(1)}, bf16[128,1152]{1,0:T(8,128)(2,1)S(1)}, u32[]{:S(2)}, u32[]{:S(2)}) collective-permute-start(bf16[128,1152]{1,0:T(8,128)(2,1)S(1)} %get-tuple-element.17.image_ref), channel_id=1, source_target_pairs={{0,256},{256,0},{1,257},{257,1},{2,258},{258,2},{3,259},{259,3},{4... | collective-permute-start | bytes 884744 | tf_op jit(solution)/shard_map/ppermute | solution.py:163
  43.8 10.9 %copy-start.4 = (bf16[128,512]{1,0:T(8,128)(2,1)}, bf16[128,512]{1,0:T(8,128)(2,1)S(1)}, u32[]{:S(2)}) copy-start(bf16[128,512]{1,0:T(8,128)(2,1)S(1)} %get-tuple-element.23.own_ref) | copy-start | bytes 393220
  54.6 2.8 %copy-start.6 = (bf16[128,512]{1,0:T(8,128)(2,1)}, bf16[128,512]{1,0:T(8,128)(2,1)S(1)}, u32[]{:S(2)}) copy-start(bf16[128,512]{1,0:T(8,128)(2,1)S(1)} %get-tuple-element.24.cross_ref) | copy-start | bytes 393220
  54.6 2.8 %copy-start.8 = (bf16[128,1152]{1,0:T(8,128)(2,1)}, bf16[128,1152]{1,0:T(8,128)(2,1)S(1)}, u32[]{:S(2)}) copy-start(bf16[128,1152]{1,0:T(8,128)(2,1)S(1)} %get-tuple-element.22) | copy-start | bytes 884740
  55.4 41.0 %collective-permute-start.3 = (bf16[4,128,1152]{2,1,0:T(8,128)(2,1)S(1)}, bf16[4,128,1152]{2,1,0:T(8,128)(2,1)S(1)}, u32[]{:S(2)}, u32[]{:S(2)}) collective-permute-start(bf16[4,128,1152]{2,1,0:T(8,128)(2,1)S(1)} %shard_map.87), channel_id=1, source_target_pairs={{0,32},{32,0},{1,33},{33,1},{2,34},{34,2},{3,35},{35,3},{4,36},{36... | collective-permute-start | bytes 3538952 | tf_op jit(solution)/shard_map/ppermute | solution.py:182
  71.1 38.5 %all-to-all-start.2 = ((f32[16,8,128]{2,1,0:T(8,128)}), f32[16,8,128]{2,1,0:T(8,128)}, u32[]{:S(2)}, u32[]{:S(2)}) async-start(f32[16,8,128]{2,1,0:T(8,128)} %broadcast_in_dim.5), calls=%async_computation.2 | async-start | bytes 131072 | tf_op jit(solution)/shard_map/all_to_all | solution.py:152
  96.4 0.9 copy-start.5
  97.3 0.9 copy-start.7
  109.6 5.0 %copy-start.9 = (bf16[128,1152]{1,0:T(8,128)(2,1)S(1)}, bf16[128,1152]{1,0:T(8,128)(2,1)}, u32[]{:S(2)}) copy-start(bf16[128,1152]{1,0:T(8,128)(2,1)} %copy-done.8) | copy-start | bytes 884740
  109.6 37.9 %copy-start.1 = (bf16[128,1152]{1,0:T(8,128)(2,1)S(1)}, bf16[128,1152]{1,0:T(8,128)(2,1)}, u32[]{:S(2)}) copy-start(bf16[128,1152]{1,0:T(8,128)(2,1)} %embeds_ref.2) | copy-start | bytes 884740
  109.6 41.1 %all-to-all-start.3 = ((bf16[4,128,1152]{2,1,0:T(8,128)(2,1)}), bf16[4,128,1152]{2,1,0:T(8,128)(2,1)S(1)}, u32[]{:S(2)}, u32[]{:S(2)}) async-start(bf16[4,128,1152]{2,1,0:T(8,128)(2,1)} %get-tuple-element.28), calls=%async_computation.3 | async-start | bytes 2359296 | tf_op jit(solution)/shard_map/all_to_all | solution.py:189
  114.6 36.1 %copy-start.3 = (bf16[128,1152]{1,0:T(8,128)(2,1)S(1)}, bf16[128,1152]{1,0:T(8,128)(2,1)}, u32[]{:S(2)}) copy-start(bf16[128,1152]{1,0:T(8,128)(2,1)} %embeds_ref.3) | copy-start | bytes 884740
  114.6 32.9 %collective-permute-start.2 = (bf16[128,1152]{1,0:T(8,128)(2,1)S(1)}, bf16[128,1152]{1,0:T(8,128)(2,1)S(1)}, u32[]{:S(2)}, u32[]{:S(2)}) collective-permute-start(bf16[128,1152]{1,0:T(8,128)(2,1)S(1)} %copy-done.9), channel_id=1, source_target_pairs={{0,256},{256,0},{1,257},{257,1},{2,258},{258,2},{3,259},{259,3},{4... | collective-permute-start | bytes 884744 | tf_op jit(solution)/shard_map/ppermute | solution.py:179

commit v2 on v1

v2 whole, which is shorter than its diff:
```python
import jax
import jax.numpy as jnp
from jax import lax
from jax.experimental import pallas as pl
from jax.experimental.pallas import tpu as pltpu
from jax.sharding import Mesh, PartitionSpec as P

EPSILON = 1e-06
F32 = jnp.float32
BF16 = jnp.bfloat16
AXES = ("zh", "y", "c", "zl", "x")
SIZES = (2, 4, 2, 8, 4)

VMEM = pl.BlockSpec(memory_space=pltpu.VMEM)
SMEM = pl.BlockSpec(memory_space=pltpu.SMEM)
HBM = pl.BlockSpec(memory_space=pltpu.HBM)
PARAMS = pltpu.CompilerParams(vmem_limit_bytes=16 * 1024 * 1024)
SWAP = ((0, 1), (1, 0))
CHUNK = 256
EXTRA = 16


def call(kernel, outs, in_specs, args, scratch=(), out_specs=None):
    return pl.pallas_call(
        kernel,
        out_shape=[jax.ShapeDtypeStruct(shape, dtype) for shape, dtype in outs],
        in_specs=in_specs,
        out_specs=out_specs or [VMEM] * len(outs),
        scratch_shapes=scratch,
        compiler_params=PARAMS,
    )(*args)


def unit(matrix):
    floats = matrix.astype(F32)
    return (floats * lax.rsqrt(jnp.sum(floats * floats, axis=1, keepdims=True) + EPSILON)).astype(BF16)


def norm_kernel(image_ref, text_ref, image_out, text_out, image_in, text_in, sems):
    copies = [
        pltpu.make_async_copy(image_ref, image_in, sems.at[0]),
        pltpu.make_async_copy(text_ref, text_in, sems.at[1]),
    ]
    for copy in copies:
        copy.start()
    copies[0].wait()
    image_out[...] = unit(image_in[...])
    copies[1].wait()
    text = unit(text_in[...])
    for k in range(text_out.shape[0]):
        text_out[k] = text


def fold(values):
    rows, cols = values.shape
    total = jnp.sum(values.reshape(rows // 8, 8, cols), axis=0)
    return sum(total[:, k * 128 : (k + 1) * 128] for k in range(cols // 128))


def pair_chunk(image, text, temper, offset, positive):
    products = lax.dot_general(image, text, (((1,), (1,)), ((), ())), preferred_element_type=F32)
    scaled = temper * products
    logits = scaled + offset
    small = jnp.exp(-jnp.abs(logits))
    part = 1.0 / (1.0 + small)
    coef = jnp.where(logits >= 0.0, 1.0, small) * part
    signed = logits
    if positive is not None:
        coef = coef - jnp.where(positive, 1.0, 0.0)
        signed = jnp.where(positive, -logits, logits)
    losses = jnp.maximum(signed, 0.0) + jnp.log1p(small)
    return coef, (fold(losses), fold(coef * scaled), fold(coef))


def pairs(scale_ref, bias_ref, image, mine_ref, sib_ref, coef_mine, coef_sib, y=None):
    per = CHUNK // 128
    temper = jnp.exp(jnp.full((1, CHUNK), scale_ref[0], F32))
    offset = bias_ref[0]
    sums, cot = None, None
    for ref, out in ((mine_ref, coef_mine), (sib_ref, coef_sib)):
        for first in range(0, ref.shape[0], per):
            text = ref[first : first + per].reshape(CHUNK, ref.shape[2])
            positive = None
            if y is not None and ref is mine_ref:
                rows = lax.broadcasted_iota(jnp.int32, (128, CHUNK), 0)
                cols = lax.broadcasted_iota(jnp.int32, (128, CHUNK), 1)
                positive = cols + first * 128 == rows + y * 128
            coef, terms = pair_chunk(image, text, temper, offset, positive)
            half = coef.astype(BF16)
            out[:, first * 128 : first * 128 + CHUNK] = half
            part = jnp.dot(half, text, preferred_element_type=F32)
            cot = part if cot is None else cot + part
            sums = terms if sums is None else tuple(a + b for a, b in zip(sums, terms))
    return cot, sums


def own_kernel(scale_ref, bias_ref, y_ref, image_ref, mine_ref, sib_ref, coef_mine, coef_sib, cot_ref, sums_ref):
    cot, sums = pairs(scale_ref, bias_ref, image_ref[...], mine_ref, sib_ref, coef_mine, coef_sib, y_ref[0])
    cot_ref[...] = cot
    for k in range(3):
        sums_ref[k] = sums[k]


def cross_kernel(scale_ref, bias_ref, image_ref, mine_ref, sib_ref, before_ref, coef_mine, coef_sib, cot_ref, sums_ref):
    cot, sums = pairs(scale_ref, bias_ref, image_ref[...], mine_ref, sib_ref, coef_mine, coef_sib)
    cot_ref[...] = cot.astype(BF16)
    lane = lax.broadcasted_iota(jnp.int32, (1, 128), 1)
    row = jnp.zeros((1, 128), F32)
    for k in range(3):
        row = row + jnp.where(lane == k, jnp.sum(sums[k] + before_ref[k]), 0.0)
    sums_ref[...] = row


def text_part(own_ref, cross_ref, image_ref, image_far_ref, block):
    cols = pl.ds(pl.multiple_of(block * 128, 128), 128)
    dims = (((0,), (0,)), ((), ()))
    return lax.dot_general(own_ref[:, cols], image_ref[...], dims, preferred_element_type=F32) + lax.dot_general(
        cross_ref[:, cols], image_far_ref[...], dims, preferred_element_type=F32
    )


def text_sib_kernel(own_ref, cross_ref, image_ref, image_far_ref, sums_ref, out_ref):
    count = (out_ref.shape[0] - EXTRA) // 128
    for k in range(count):
        out_ref[k * 128 : (k + 1) * 128, :] = text_part(own_ref, cross_ref, image_ref, image_far_ref, k).astype(BF16)
    rest = sums_ref[...]
    tail = jnp.zeros((EXTRA, 128), F32)
    row = lax.broadcasted_iota(jnp.int32, (EXTRA, 128), 0)
    for k in range(3):
        term = rest.astype(BF16).astype(F32)
        tail = tail + jnp.where(row == k, term, 0.0)
        rest = rest - term
    out_ref[count * 128 :, 0:128] = tail.astype(BF16)
    out_ref[count * 128 :, 128:] = jnp.zeros((EXTRA, out_ref.shape[1] - 128), BF16)


def text_mine_kernel(y_ref, own_ref, cross_ref, image_ref, image_far_ref, sums_ref, got_ref, spread_ref, *out_refs):
    count = len(out_refs)
    for k in range(count):
        block = lax.rem(y_ref[0] + k, count)
        got = got_ref[pl.ds(pl.multiple_of(block * 128, 128), 128), :]
        total = text_part(own_ref, cross_ref, image_ref, image_far_ref, block) + got.astype(F32)
        out_refs[k][...] = total.astype(out_refs[k].dtype)
    tail = got_ref[count * 128 :, 0:128].astype(F32)
    row = sums_ref[...] + jnp.sum(tail, axis=0, keepdims=True)
    spread_ref[...] = jnp.broadcast_to(row[None], spread_ref.shape)


def pull(embeds, cot, scale):
    floats = embeds.astype(F32)
    cot = jnp.exp(jnp.full((1, floats.shape[1]), scale, F32)) * cot
    inverse = lax.rsqrt(jnp.sum(floats * floats, axis=1, keepdims=True) + EPSILON)
    along = jnp.sum(cot * floats, axis=1, keepdims=True)
    return (inverse * cot - (inverse * inverse * inverse * along) * floats).astype(BF16)


def last_kernel(scale_ref, image_ref, text_ref, image_cot_ref, far_ref, text_cot_ref, *refs):
    *got_refs, totals_ref, image_grad, text_grad, loss_ref, scale_grad, bias_grad = refs
    image_grad[...] = pull(image_ref[...], image_cot_ref[...] + far_ref[...].astype(F32), scale_ref[0])
    cot = text_cot_ref[...]
    for got_ref in got_refs:
        cot = cot + got_ref[...].astype(F32)
    text_grad[...] = pull(text_ref[...], cot, scale_ref[0])
    totals = jnp.sum(totals_ref[...], axis=0)
    lane = lax.broadcasted_iota(jnp.int32, (1, 128), 1)
    batch = 2 * totals_ref.shape[0] * image_ref.shape[0]
    loss, scale, bias = (jnp.sum(jnp.where(lane == k, totals, 0.0)) for k in range(3))
    loss_ref[0] = loss / batch
    scale_grad[0] = scale
    bias_grad[0] = bias


def region(body, inside, *args):
    outs = jax.eval_shape(body, *args)
    return lax.cond(inside, body, lambda *_: jax.tree.map(lambda o: jnp.zeros(o.shape, o.dtype), outs), *args)


def on_device(image_embeds, text_embeds, log_scale, logit_bias):
    rows, width = image_embeds.shape
    y_count = lax.axis_size("y")
    y = jnp.reshape(lax.axis_index("y"), (1,))
    inside = y[0] < y_count
    block, blocks = (rows, width), (y_count, rows, width)
    half = (rows, y_count * rows)
    sum_axes = ("zh", "y", "zl", "x")

    image, text = call(
        norm_kernel,
        [(block, BF16), (blocks, BF16)],
        [HBM] * 2,
        (image_embeds, text_embeds),
        [pltpu.VMEM(block, BF16), pltpu.VMEM(block, BF16), pltpu.SemaphoreType.DMA((2,))],
    )
    image_far = lax.ppermute(image, "zh", SWAP)

    def gather(text):
        mine = lax.all_to_all(text, "y", 0, 0, tiled=True)
        return mine, lax.ppermute(mine, "c", SWAP)

    mine, sib = region(gather, inside, text)
    own_mine, own_sib, image_cot, sums = call(
        own_kernel,
        [(half, BF16), (half, BF16), (block, F32), ((3, 8, 128), F32)],
        [SMEM] * 3 + [VMEM] * 3,
        (log_scale, logit_bias, y, image, mine, sib),
    )
    far_mine, far_sib, far_cot, sums = call(
        cross_kernel,
        [(half, BF16), (half, BF16), (block, BF16), ((1, 128), F32)],
        [SMEM] * 2 + [VMEM] * 4,
        (log_scale, logit_bias, image_far, mine, sib, sums),
    )
    far_got = lax.ppermute(far_cot, "zh", SWAP)

    def text_side(own_mine, own_sib, far_mine, far_sib, image, image_far, y, sums):
        (text_sib,) = call(
            text_sib_kernel,
            [((y_count * rows + EXTRA, width), BF16)],
            [VMEM] * 5,
            (own_sib, far_sib, image, image_far, sums),
        )
        text_got = lax.ppermute(text_sib, "c", SWAP)
        spread, text_kept, *text_send = call(
            text_mine_kernel,
            [((lax.axis_size(sum_axes), 1, 128), F32), (block, F32)] + [(block, BF16)] * (y_count - 1),
            [SMEM] + [VMEM] * 6,
            (y, own_mine, far_mine, image, image_far, sums, text_got),
        )
        got = [
            lax.ppermute(part, "y", [(i, (i + k) % y_count) for i in range(y_count)])
            for k, part in enumerate(text_send, 1)
        ]
        return text_kept, *got, lax.all_to_all(spread, sum_axes, 0, 0, tiled=True)

    text_cots = region(text_side, inside, own_mine, own_sib, far_mine, far_sib, image, image_far, y, sums)
    image_grad, text_grad, loss, scale_grad, bias_grad = call(
        last_kernel,
        [(block, BF16)] * 2 + [((1,), F32)] * 3,
        [SMEM] + [VMEM] * (4 + len(text_cots)),
        (log_scale, image_embeds, text_embeds, image_cot, far_got, *text_cots),
        out_specs=[VMEM] * 2 + [SMEM] * 3,
    )
    return loss, image_grad, text_grad, scale_grad, bias_grad


def solution(mesh):
    fine = Mesh(mesh.devices.reshape(SIZES), AXES)
    return jax.shard_map(
        on_device,
        mesh=fine,
        in_specs=(P(AXES, None), P(AXES, None), P(), P()),
        out_specs=(P(), P(AXES, None), P(AXES, None), P(), P()),
        check_vma=False,
    )
```

time: 154 us -> 109 us (0.71)
  the two profiles are of different devices: /device:TPU:10 before, /device:TPU:1 now
where the time goes in v2:
time: 109 us; the launch traced here: 108 us
  starting transfers between devices  54.7 us (50%)
  blocking collectives  19.1 us (18%)
  waiting for transfers between devices  16.8 us (15%)
  Pallas kernels  13.5 us (12%)
  between operations  2.01 us (2%)
  local copies, waits for them, and re-layouts  1.93 us (2%)
    all_to_all x1, starting transfers between devices, text_side(): return (text_kept, *got, lax.all_to_all(spread, sum_axes, 0, 0, tiled=True))  20.3 us
    all_to_all x1, blocking collectives, gather(): mine = lax.all_to_all(text, 'y', 0, 0, tiled=True)  19.1 us
    ppermute x1, starting transfers between devices, on_device(): image_far = lax.ppermute(image, 'zh', SWAP)  16.3 us
    pallas_call x6, Pallas kernels, call(): pl.pallas_call(kernel, out_shape=[jax.ShapeDtypeStruct(shape, dtype) for...  13.5 us
    ppermute x3, waiting for transfers between devices, text_side(): lax.ppermute(part, 'y', [(i, (i + k) % y_count) for i in range(y_count)])  11.5 us
    ppermute x3, starting transfers between devices, text_side(): lax.ppermute(part, 'y', [(i, (i + k) % y_count) for i in range(y_count)])  9.25 us
    ppermute x1, starting transfers between devices, gather(): return (mine, lax.ppermute(mine, 'c', SWAP))  4.35 us
    ppermute x1, waiting for transfers between devices, gather(): return (mine, lax.ppermute(mine, 'c', SWAP))  2.79 us
  transfers between devices with their start and end apart: 8, of which 5 were waited for; matrix products, arithmetic and copies ran while one was open for 0% of the time, Pallas kernels for 6%

profile of v2, /device:TPU:1, one launch (start us, length us, event | category | flops | bytes accessed | tf_op | source)
XLA Modules:
  0.0 108.1 jit_solution(16314811275463229203)
XLA Ops:
  0.6 0.0 copy-start
  0.6 1.0 copy-done
  1.6 0.0 copy-start.2
  1.6 1.0 copy-done.2
  2.6 0.5 shard_map.83
  3.0 16.3 %collective-permute-start.5 = (bf16[128,1152]{1,0:T(8,128)(2,1)S(1)}, bf16[128,1152]{1,0:T(8,128)(2,1)S(1)}, u32[]{:S(2)}, u32[]{:S(2)}) collective-permute-start(bf16[128,1152]{1,0:T(8,128)(2,1)S(1)} %get-tuple-element.57.image_ref), channel_id=1, source_target_pairs={{0,256},{256,0},{1,257},{257,1},{2,258},{258,2},{3,259},{259,3},{4... | collective-permute-start | bytes 884744 | tf_op jit(solution)/shard_map/ppermute | solution.py:194
  20.6 26.3 %conditional.2 = (bf16[4,128,1152]{2,1,0:T(8,128)(2,1)}, bf16[4,128,1152]{2,1,0:T(8,128)(2,1)}) conditional(s32[]{:T(128)} %convert_element_type.4, () %tuple.24, bf16[4,128,1152]{2,1,0:T(8,128)(2,1)S(1)} %get-tuple-element.58), branch_computations={%region_0.0_spmd, %region_1.0_spmd} | conditional | bytes 7077944 | solution.py:175
  20.6 19.1 %all_to_all.8 = bf16[4,128,1152]{2,1,0:T(8,128)(2,1)} all-to-all(bf16[4,128,1152]{2,1,0:T(8,128)(2,1)S(1)} %param.1), channel_id=1, replica_groups=mesh['zh'=2,'y'=4,'c'=2,'zl'=8,'x'=4] {'y'}, dimensions={0} | all-to-all | bytes 2359296 | tf_op jit(solution)/shard_map/cond/branch_1_fun/all_to_all | solution.py:197
  39.7 4.4 %collective-permute-start = (bf16[4,128,1152]{2,1,0:T(8,128)(2,1)}, bf16[4,128,1152]{2,1,0:T(8,128)(2,1)}, u32[]{:S(2)}, u32[]{:S(2)}) collective-permute-start(bf16[4,128,1152]{2,1,0:T(8,128)(2,1)} %all_to_all.8), channel_id=1, source_target_pairs={{0,32},{32,0},{1,33},{33,1},{2,34},{34,2},{3,35},{35,3},{4,36},{36... | collective-permute-start | bytes 3538952 | tf_op jit(solution)/shard_map/cond/branch_1_fun/ppermute | solution.py:198
  44.1 2.8 %collective-permute-done = bf16[4,128,1152]{2,1,0:T(8,128)(2,1)} collective-permute-done((bf16[4,128,1152]{2,1,0:T(8,128)(2,1)}, bf16[4,128,1152]{2,1,0:T(8,128)(2,1)}, u32[]{:S(2)}, u32[]{:S(2)}) %collective-permute-start) | collective-permute-done | bytes 1179680 | tf_op jit(solution)/shard_map/cond/branch_1_fun/ppermute | solution.py:198
  46.9 3.9 %shard_map.84 = (bf16[128,512]{1,0:T(8,128)(2,1)S(1)}, bf16[128,512]{1,0:T(8,128)(2,1)S(1)}, f32[128,1152]{1,0:T(8,128)S(1)}, f32[3,8,128]{2,1,0:T(8,128)S(1)}) custom-call(f32[1]{0:T(128)S(6)} %copy.23.scale_ref, f32[1]{0:T(128)S(6)} %copy.24.bias_ref, s32[1]{0:T(128)} %bitcast.y_ref, bf16[128,1152]{1,0:T(8,128)(2,1)S(1)} %get-tuple-element.57.image_ref, ...), custom_call_target="tpu_custom_call" | custom-call | tf_op jit(solution)/shard_map/pallas_call | solution.py:24
  50.7 0.0 collective-permute-done.5.image_ref
  50.7 3.8 %shard_map.85 = (bf16[128,512]{1,0:T(8,128)(2,1)S(1)}, bf16[128,512]{1,0:T(8,128)(2,1)S(1)}, bf16[128,1152]{1,0:T(8,128)(2,1)S(1)}, f32[1,128]{1,0:T(1,128)S(1)}) custom-call(f32[1]{0:T(128)S(6)} %copy.23.scale_ref, f32[1]{0:T(128)S(6)} %copy.24.bias_ref, bf16[128,1152]{1,0:T(8,128)(2,1)S(1)} %collective-permute-done.5.image_ref, ...), custom_call_target="tpu_custom_call" | custom-call | tf_op jit(solution)/shard_map/pallas_call | solution.py:24
  54.6 1.9 %collective-permute-start.6 = (bf16[128,1152]{1,0:T(8,128)(2,1)S(1)}, bf16[128,1152]{1,0:T(8,128)(2,1)S(1)}, u32[]{:S(2)}, u32[]{:S(2)}) collective-permute-start(bf16[128,1152]{1,0:T(8,128)(2,1)S(1)} %get-tuple-element.63), channel_id=1, source_target_pairs={{0,256},{256,0},{1,257},{257,1},{2,258},{258,2},{3,259},{259,3},{4... | collective-permute-start | bytes 884744 | tf_op jit(solution)/shard_map/ppermute | solution.py:213
  56.5 0.0 copy-start.1
  56.5 0.0 copy-start.3
  56.5 48.7 %conditional.3 = (f32[128,1152]{1,0:T(8,128)}, bf16[128,1152]{1,0:T(8,128)(2,1)}, bf16[128,1152]{1,0:T(8,128)(2,1)}, bf16[128,1152]{1,0:T(8,128)(2,1)}, f32[256,1,128]{2,1,0:T(1,128)}) conditional(s32[]{:T(128)} %convert_element_type.4, () %tuple.25, (bf16[128,512]{1,0:T(8,128)(2,1)S(1)}, bf16[128,512]{1,0:T(8,128)(2,1)S(1)}, ...), branch_computations={%region_2.0_spmd, %region_3.0_spmd} | conditional | bytes 8798440 | solution.py:175
  56.5 0.8 branch_1_fun.2
  57.3 2.6 %collective-permute-start.1 = (bf16[528,1152]{1,0:T(8,128)(2,1)S(1)}, bf16[528,1152]{1,0:T(8,128)(2,1)S(1)}, u32[]{:S(2)}, u32[]{:S(2)}) collective-permute-start(bf16[528,1152]{1,0:T(8,128)(2,1)S(1)} %branch_1_fun.2), channel_id=1, source_target_pairs={{0,32},{32,0},{1,33},{33,1},{2,34},{34,2},{3,35},{35,3},{4,36},{36... | collective-permute-start | bytes 3649544 | tf_op jit(solution)/shard_map/cond/branch_1_fun/ppermute | solution.py:222
  59.9 2.5 %collective-permute-done.1.got_ref = bf16[528,1152]{1,0:T(8,128)(2,1)S(1)} collective-permute-done((bf16[528,1152]{1,0:T(8,128)(2,1)S(1)}, bf16[528,1152]{1,0:T(8,128)(2,1)S(1)}, u32[]{:S(2)}, u32[]{:S(2)}) %collective-permute-start.1) | collective-permute-done | bytes 1216544 | tf_op jit(solution)/shard_map/cond/branch_1_fun/ppermute | solution.py:222
  62.4 1.7 %branch_1_fun.3 = (f32[256,1,128]{2,1,0:T(1,128)}, f32[128,1152]{1,0:T(8,128)}, bf16[128,1152]{1,0:T(8,128)(2,1)S(1)}, bf16[128,1152]{1,0:T(8,128)(2,1)S(1)}, bf16[128,1152]{1,0:T(8,128)(2,1)S(1)}) custom-call(s32[1]{0:T(128)} %get-tuple-element.17.y_ref, bf16[128,512]{1,0:T(8,128)(2,1)S(1)} %get-tuple-element.18.own_ref, ...), custom_call_target="tpu_custom_call" | custom-call | tf_op jit(solution)/shard_map/cond/branch_1_fun/pallas_call | solution.py:24
  64.1 20.3 %all-to-all-start.1 = ((f32[256,1,128]{2,1,0:T(1,128)}), f32[256,1,128]{2,1,0:T(1,128)}, u32[]{:S(2)}, u32[]{:S(2)}) async-start(f32[256,1,128]{2,1,0:T(1,128)} %get-tuple-element.29), calls=%async_computation.1 | async-start | bytes 262144 | tf_op jit(solution)/shard_map/cond/branch_1_fun/all_to_all | solution.py:233
  84.4 1.9 %collective-permute-start.2 = (bf16[128,1152]{1,0:T(8,128)(2,1)S(1)}, bf16[128,1152]{1,0:T(8,128)(2,1)}, u32[]{:S(2)}, u32[]{:S(2)}) collective-permute-start(bf16[128,1152]{1,0:T(8,128)(2,1)S(1)} %get-tuple-element.26), channel_id=1, source_target_pairs={{0,64},{64,128},{128,192},{192,0},{1,65},{65,129},{129,193},{193,1... | collective-permute-start | bytes 884744 | tf_op jit(solution)/shard_map/cond/branch_1_fun/ppermute | solution.py:230
  86.4 4.5 %collective-permute-start.3 = (bf16[128,1152]{1,0:T(8,128)(2,1)S(1)}, bf16[128,1152]{1,0:T(8,128)(2,1)}, u32[]{:S(2)}, u32[]{:S(2)}) collective-permute-start(bf16[128,1152]{1,0:T(8,128)(2,1)S(1)} %get-tuple-element.27), channel_id=1, source_target_pairs={{0,128},{64,192},{128,0},{192,64},{1,129},{65,193},{129,1},{193,65... | collective-permute-start | bytes 884744 | tf_op jit(solution)/shard_map/cond/branch_1_fun/ppermute | solution.py:230
  90.8 2.9 %collective-permute-start.4 = (bf16[128,1152]{1,0:T(8,128)(2,1)S(1)}, bf16[128,1152]{1,0:T(8,128)(2,1)}, u32[]{:S(2)}, u32[]{:S(2)}) collective-permute-start(bf16[128,1152]{1,0:T(8,128)(2,1)S(1)} %get-tuple-element.28), channel_id=1, source_target_pairs={{0,192},{64,0},{128,64},{192,128},{1,193},{65,1},{129,65},{193,129... | collective-permute-start | bytes 884744 | tf_op jit(solution)/shard_map/cond/branch_1_fun/ppermute | solution.py:230
  93.7 3.1 %collective-permute-done.2 = bf16[128,1152]{1,0:T(8,128)(2,1)} collective-permute-done((bf16[128,1152]{1,0:T(8,128)(2,1)S(1)}, bf16[128,1152]{1,0:T(8,128)(2,1)}, u32[]{:S(2)}, u32[]{:S(2)}) %collective-permute-start.2) | collective-permute-done | bytes 294944 | tf_op jit(solution)/shard_map/cond/branch_1_fun/ppermute | solution.py:230
  96.8 5.9 %collective-permute-done.3 = bf16[128,1152]{1,0:T(8,128)(2,1)} collective-permute-done((bf16[128,1152]{1,0:T(8,128)(2,1)S(1)}, bf16[128,1152]{1,0:T(8,128)(2,1)}, u32[]{:S(2)}, u32[]{:S(2)}) %collective-permute-start.3) | collective-permute-done | bytes 294944 | tf_op jit(solution)/shard_map/cond/branch_1_fun/ppermute | solution.py:230
  102.7 2.5 %collective-permute-done.4 = bf16[128,1152]{1,0:T(8,128)(2,1)} collective-permute-done((bf16[128,1152]{1,0:T(8,128)(2,1)S(1)}, bf16[128,1152]{1,0:T(8,128)(2,1)}, u32[]{:S(2)}, u32[]{:S(2)}) %collective-permute-start.4) | collective-permute-done | bytes 294944 | tf_op jit(solution)/shard_map/cond/branch_1_fun/ppermute | solution.py:230
  105.2 0.0 all-to-all-done.1
  105.2 0.0 collective-permute-done.6.far_ref
  105.2 0.0 copy-done.1
  105.2 0.0 copy-done.3
  105.2 2.9 %shard_map.86 = (bf16[128,1152]{1,0:T(8,128)(2,1)}, bf16[128,1152]{1,0:T(8,128)(2,1)}, f32[1]{0:T(128)}, f32[1]{0:T(128)}, f32[1]{0:T(128)}) custom-call(f32[1]{0:T(128)S(6)} %copy.23.scale_ref, bf16[128,1152]{1,0:T(8,128)(2,1)S(1)} %copy-done.1, bf16[128,1152]{1,0:T(8,128)(2,1)S(1)} %copy-done.3, f32[128,1152]{1,0:T(8,128)S(1)} %get-tuple-element.61.image_cot_ref, ...), custom_call_target="tpu_custom_call" | custom-call | tf_op jit(solution)/shard_map/pallas_call | solution.py:24
Async XLA Ops:
  0.6 1.0 copy-start
  1.6 1.0 copy-start.2
  3.0 47.7 %collective-permute-start.5 = (bf16[128,1152]{1,0:T(8,128)(2,1)S(1)}, bf16[128,1152]{1,0:T(8,128)(2,1)S(1)}, u32[]{:S(2)}, u32[]{:S(2)}) collective-permute-start(bf16[128,1152]{1,0:T(8,128)(2,1)S(1)} %get-tuple-element.57.image_ref), channel_id=1, source_target_pairs={{0,256},{256,0},{1,257},{257,1},{2,258},{258,2},{3,259},{259,3},{4... | collective-permute-start | bytes 884744 | tf_op jit(solution)/shard_map/ppermute | solution.py:194
  39.7 7.2 %collective-permute-start = (bf16[4,128,1152]{2,1,0:T(8,128)(2,1)}, bf16[4,128,1152]{2,1,0:T(8,128)(2,1)}, u32[]{:S(2)}, u32[]{:S(2)}) collective-permute-start(bf16[4,128,1152]{2,1,0:T(8,128)(2,1)} %all_to_all.8), channel_id=1, source_target_pairs={{0,32},{32,0},{1,33},{33,1},{2,34},{34,2},{3,35},{35,3},{4,36},{36... | collective-permute-start | bytes 3538952 | tf_op jit(solution)/shard_map/cond/branch_1_fun/ppermute | solution.py:198
  54.6 50.7 %collective-permute-start.6 = (bf16[128,1152]{1,0:T(8,128)(2,1)S(1)}, bf16[128,1152]{1,0:T(8,128)(2,1)S(1)}, u32[]{:S(2)}, u32[]{:S(2)}) collective-permute-start(bf16[128,1152]{1,0:T(8,128)(2,1)S(1)} %get-tuple-element.63), channel_id=1, source_target_pairs={{0,256},{256,0},{1,257},{257,1},{2,258},{258,2},{3,259},{259,3},{4... | collective-permute-start | bytes 884744 | tf_op jit(solution)/shard_map/ppermute | solution.py:213
  56.5 48.7 %copy-start.1 = (bf16[128,1152]{1,0:T(8,128)(2,1)S(1)}, bf16[128,1152]{1,0:T(8,128)(2,1)}, u32[]{:S(2)}) copy-start(bf16[128,1152]{1,0:T(8,128)(2,1)} %image_ref.3) | copy-start | bytes 884740
  56.5 48.7 %copy-start.3 = (bf16[128,1152]{1,0:T(8,128)(2,1)S(1)}, bf16[128,1152]{1,0:T(8,128)(2,1)}, u32[]{:S(2)}) copy-start(bf16[128,1152]{1,0:T(8,128)(2,1)} %text_ref.3) | copy-start | bytes 884740
  57.3 5.1 %collective-permute-start.1 = (bf16[528,1152]{1,0:T(8,128)(2,1)S(1)}, bf16[528,1152]{1,0:T(8,128)(2,1)S(1)}, u32[]{:S(2)}, u32[]{:S(2)}) collective-permute-start(bf16[528,1152]{1,0:T(8,128)(2,1)S(1)} %branch_1_fun.2), channel_id=1, source_target_pairs={{0,32},{32,0},{1,33},{33,1},{2,34},{34,2},{3,35},{35,3},{4,36},{36... | collective-permute-start | bytes 3649544 | tf_op jit(solution)/shard_map/cond/branch_1_fun/ppermute | solution.py:222
  64.1 41.1 %all-to-all-start.1 = ((f32[256,1,128]{2,1,0:T(1,128)}), f32[256,1,128]{2,1,0:T(1,128)}, u32[]{:S(2)}, u32[]{:S(2)}) async-start(f32[256,1,128]{2,1,0:T(1,128)} %get-tuple-element.29), calls=%async_computation.1 | async-start | bytes 262144 | tf_op jit(solution)/shard_map/cond/branch_1_fun/all_to_all | solution.py:233
  84.4 12.4 %collective-permute-start.2 = (bf16[128,1152]{1,0:T(8,128)(2,1)S(1)}, bf16[128,1152]{1,0:T(8,128)(2,1)}, u32[]{:S(2)}, u32[]{:S(2)}) collective-permute-start(bf16[128,1152]{1,0:T(8,128)(2,1)S(1)} %get-tuple-element.26), channel_id=1, source_target_pairs={{0,64},{64,128},{128,192},{192,0},{1,65},{65,129},{129,193},{193,1... | collective-permute-start | bytes 884744 | tf_op jit(solution)/shard_map/cond/branch_1_fun/ppermute | solution.py:230
  86.4 16.4 %collective-permute-start.3 = (bf16[128,1152]{1,0:T(8,128)(2,1)S(1)}, bf16[128,1152]{1,0:T(8,128)(2,1)}, u32[]{:S(2)}, u32[]{:S(2)}) collective-permute-start(bf16[128,1152]{1,0:T(8,128)(2,1)S(1)} %get-tuple-element.27), channel_id=1, source_target_pairs={{0,128},{64,192},{128,0},{192,64},{1,129},{65,193},{129,1},{193,65... | collective-permute-start | bytes 884744 | tf_op jit(solution)/shard_map/cond/branch_1_fun/ppermute | solution.py:230
  90.8 14.4 %collective-permute-start.4 = (bf16[128,1152]{1,0:T(8,128)(2,1)S(1)}, bf16[128,1152]{1,0:T(8,128)(2,1)}, u32[]{:S(2)}, u32[]{:S(2)}) collective-permute-start(bf16[128,1152]{1,0:T(8,128)(2,1)S(1)} %get-tuple-element.28), channel_id=1, source_target_pairs={{0,192},{64,0},{128,64},{192,128},{1,193},{65,1},{129,65},{193,129... | collective-permute-start | bytes 884744 | tf_op jit(solution)/shard_map/cond/branch_1_fun/ppermute | solution.py:230

commit v3 on v2

--- a/solution.py
+++ b/solution.py
@@ -1,3 +1,5 @@
+import functools
+
 import jax
 import jax.numpy as jnp
 from jax import lax
@@ -17,7 +19,6 @@
 PARAMS = pltpu.CompilerParams(vmem_limit_bytes=16 * 1024 * 1024)
 SWAP = ((0, 1), (1, 0))
 CHUNK = 256
-EXTRA = 16
 
 
 def call(kernel, outs, in_specs, args, scratch=(), out_specs=None):
@@ -36,19 +37,14 @@
     return (floats * lax.rsqrt(jnp.sum(floats * floats, axis=1, keepdims=True) + EPSILON)).astype(BF16)
 
 
-def norm_kernel(image_ref, text_ref, image_out, text_out, image_in, text_in, sems):
-    copies = [
-        pltpu.make_async_copy(image_ref, image_in, sems.at[0]),
-        pltpu.make_async_copy(text_ref, text_in, sems.at[1]),
-    ]
-    for copy in copies:
-        copy.start()
-    copies[0].wait()
-    image_out[...] = unit(image_in[...])
-    copies[1].wait()
-    text = unit(text_in[...])
-    for k in range(text_out.shape[0]):
-        text_out[k] = text
+def norm_kernel(matrix_ref, *out_refs):
+    rows = unit(matrix_ref[...])
+    for out_ref in out_refs:
+        if len(out_ref.shape) == 2:
+            out_ref[...] = rows
+        else:
+            for k in range(out_ref.shape[0]):
+                out_ref[k] = rows
 
 
 def fold(values):
@@ -94,7 +90,11 @@
     return cot, sums
 
 
-def own_kernel(scale_ref, bias_ref, y_ref, image_ref, mine_ref, sib_ref, coef_mine, coef_sib, cot_ref, sums_ref):
+def own_kernel(
+    scale_ref, bias_ref, y_ref, image_ref, mine_ref, sib_ref, coef_mine, coef_sib, cot_ref, sums_ref, mine_out, sib_out
+):
+    mine_out[...] = mine_ref[...]
+    sib_out[...] = sib_ref[...]
     cot, sums = pairs(scale_ref, bias_ref, image_ref[...], mine_ref, sib_ref, coef_mine, coef_sib, y_ref[0])
     cot_ref[...] = cot
     for k in range(3):
@@ -104,11 +104,10 @@
 def cross_kernel(scale_ref, bias_ref, image_ref, mine_ref, sib_ref, before_ref, coef_mine, coef_sib, cot_ref, sums_ref):
     cot, sums = pairs(scale_ref, bias_ref, image_ref[...], mine_ref, sib_ref, coef_mine, coef_sib)
     cot_ref[...] = cot.astype(BF16)
-    lane = lax.broadcasted_iota(jnp.int32, (1, 128), 1)
-    row = jnp.zeros((1, 128), F32)
     for k in range(3):
-        row = row + jnp.where(lane == k, jnp.sum(sums[k] + before_ref[k]), 0.0)
-    sums_ref[...] = row
+        total = sums[k] + before_ref[k]
+        for peer in range(sums_ref.shape[0]):
+            sums_ref[peer, k * 8 : (k + 1) * 8] = total
 
 
 def text_part(own_ref, cross_ref, image_ref, image_far_ref, block):
@@ -119,30 +118,22 @@
     )
 
 
-def text_sib_kernel(own_ref, cross_ref, image_ref, image_far_ref, sums_ref, out_ref):
-    count = (out_ref.shape[0] - EXTRA) // 128
-    for k in range(count):
-        out_ref[k * 128 : (k + 1) * 128, :] = text_part(own_ref, cross_ref, image_ref, image_far_ref, k).astype(BF16)
-    rest = sums_ref[...]
-    tail = jnp.zeros((EXTRA, 128), F32)
-    row = lax.broadcasted_iota(jnp.int32, (EXTRA, 128), 0)
-    for k in range(3):
-        term = rest.astype(BF16).astype(F32)
-        tail = tail + jnp.where(row == k, term, 0.0)
-        rest = rest - term
-    out_ref[count * 128 :, 0:128] = tail.astype(BF16)
-    out_ref[count * 128 :, 128:] = jnp.zeros((EXTRA, out_ref.shape[1] - 128), BF16)
-
-
-def text_mine_kernel(y_ref, own_ref, cross_ref, image_ref, image_far_ref, sums_ref, got_ref, spread_ref, *out_refs):
+def text_sib_kernel(own_ref, cross_ref, image_ref, image_far_ref, out_ref):
+    for k in range(out_ref.shape[0]):
+        out_ref[k] = text_part(own_ref, cross_ref, image_ref, image_far_ref, k).astype(BF16)
+
+
+def text_mine_kernel(y_ref, own_ref, cross_ref, image_ref, image_far_ref, near_ref, got_ref, spread_ref, *out_refs):
     count = len(out_refs)
     for k in range(count):
         block = lax.rem(y_ref[0] + k, count)
-        got = got_ref[pl.ds(pl.multiple_of(block * 128, 128), 128), :]
-        total = text_part(own_ref, cross_ref, image_ref, image_far_ref, block) + got.astype(F32)
+        total = text_part(own_ref, cross_ref, image_ref, image_far_ref, block) + got_ref[block].astype(F32)
         out_refs[k][...] = total.astype(out_refs[k].dtype)
-    tail = got_ref[count * 128 :, 0:128].astype(F32)
-    row = sums_ref[...] + jnp.sum(tail, axis=0, keepdims=True)
+    near = jnp.sum(near_ref[...], axis=0)
+    lane = lax.broadcasted_iota(jnp.int32, (1, 128), 1)
+    row = jnp.zeros((1, 128), F32)
+    for k in range(3):
+        row = row + jnp.where(lane == k, jnp.sum(near[k * 8 : (k + 1) * 8]), 0.0)
     spread_ref[...] = jnp.broadcast_to(row[None], spread_ref.shape)
 
 
@@ -154,7 +145,7 @@
     return (inverse * cot - (inverse * inverse * inverse * along) * floats).astype(BF16)
 
 
-def last_kernel(scale_ref, image_ref, text_ref, image_cot_ref, far_ref, text_cot_ref, *refs):
+def last_kernel(batch, scale_ref, image_ref, text_ref, image_cot_ref, far_ref, text_cot_ref, *refs):
     *got_refs, totals_ref, image_grad, text_grad, loss_ref, scale_grad, bias_grad = refs
     image_grad[...] = pull(image_ref[...], image_cot_ref[...] + far_ref[...].astype(F32), scale_ref[0])
     cot = text_cot_ref[...]
@@ -163,7 +154,6 @@
     text_grad[...] = pull(text_ref[...], cot, scale_ref[0])
     totals = jnp.sum(totals_ref[...], axis=0)
     lane = lax.broadcasted_iota(jnp.int32, (1, 128), 1)
-    batch = 2 * totals_ref.shape[0] * image_ref.shape[0]
     loss, scale, bias = (jnp.sum(jnp.where(lane == k, totals, 0.0)) for k in range(3))
     loss_ref[0] = loss / batch
     scale_grad[0] = scale
@@ -182,59 +172,52 @@
     inside = y[0] < y_count
     block, blocks = (rows, width), (y_count, rows, width)
     half = (rows, y_count * rows)
-    sum_axes = ("zh", "y", "zl", "x")
-
-    image, text = call(
-        norm_kernel,
-        [(block, BF16), (blocks, BF16)],
-        [HBM] * 2,
-        (image_embeds, text_embeds),
-        [pltpu.VMEM(block, BF16), pltpu.VMEM(block, BF16), pltpu.SemaphoreType.DMA((2,))],
-    )
+
+    (image,) = call(norm_kernel, [(block, BF16)], [VMEM], (image_embeds,))
     image_far = lax.ppermute(image, "zh", SWAP)
 
-    def gather(text):
+    def gather(text_embeds):
+        (text,) = call(norm_kernel, [(blocks, BF16)], [VMEM], (text_embeds,))
         mine = lax.all_to_all(text, "y", 0, 0, tiled=True)
         return mine, lax.ppermute(mine, "c", SWAP)
 
-    mine, sib = region(gather, inside, text)
-    own_mine, own_sib, image_cot, sums = call(
+    mine, sib = region(gather, inside, text_embeds)
+    own_mine, own_sib, image_cot, sums, mine, sib = call(
         own_kernel,
-        [(half, BF16), (half, BF16), (block, F32), ((3, 8, 128), F32)],
+        [(half, BF16), (half, BF16), (block, F32), ((3, 8, 128), F32), (blocks, BF16), (blocks, BF16)],
         [SMEM] * 3 + [VMEM] * 3,
         (log_scale, logit_bias, y, image, mine, sib),
     )
     far_mine, far_sib, far_cot, sums = call(
         cross_kernel,
-        [(half, BF16), (half, BF16), (block, BF16), ((1, 128), F32)],
+        [(half, BF16), (half, BF16), (block, BF16), ((lax.axis_size(("y", "c", "x")), 24, 128), F32)],
         [SMEM] * 2 + [VMEM] * 4,
         (log_scale, logit_bias, image_far, mine, sib, sums),
     )
     far_got = lax.ppermute(far_cot, "zh", SWAP)
 
-    def text_side(own_mine, own_sib, far_mine, far_sib, image, image_far, y, sums):
-        (text_sib,) = call(
-            text_sib_kernel,
-            [((y_count * rows + EXTRA, width), BF16)],
-            [VMEM] * 5,
-            (own_sib, far_sib, image, image_far, sums),
-        )
-        text_got = lax.ppermute(text_sib, "c", SWAP)
+    (text_sib,) = call(text_sib_kernel, [(blocks, BF16)], [VMEM] * 4, (own_sib, far_sib, image, image_far))
+    text_got = lax.ppermute(text_sib, "c", SWAP)
+    near = lax.all_to_all(sums, ("y", "c", "x"), 0, 0, tiled=True)
+
+    def text_side(own_mine, far_mine, image, image_far, y, near, text_got):
+        z_axes = ("zh", "zl")
         spread, text_kept, *text_send = call(
             text_mine_kernel,
-            [((lax.axis_size(sum_axes), 1, 128), F32), (block, F32)] + [(block, BF16)] * (y_count - 1),
+            [((lax.axis_size(z_axes), 1, 128), F32), (block, F32)] + [(block, BF16)] * (y_count - 1),
             [SMEM] + [VMEM] * 6,
-            (y, own_mine, far_mine, image, image_far, sums, text_got),
+            (y, own_mine, far_mine, image, image_far, near, text_got),
         )
         got = [
             lax.ppermute(part, "y", [(i, (i + k) % y_count) for i in range(y_count)])
             for k, part in enumerate(text_send, 1)
         ]
-        return text_kept, *got, lax.all_to_all(spread, sum_axes, 0, 0, tiled=True)
-
-    text_cots = region(text_side, inside, own_mine, own_sib, far_mine, far_sib, image, image_far, y, sums)
+        totals = region(lambda v: lax.all_to_all(v, z_axes, 0, 0, tiled=True), y[0] < y_count, spread)
+        return text_kept, *got, totals
+
+    text_cots = region(text_side, inside, own_mine, far_mine, image, image_far, y, near, text_got)
     image_grad, text_grad, loss, scale_grad, bias_grad = call(
-        last_kernel,
+        functools.partial(last_kernel, rows * lax.axis_size(AXES)),
         [(block, BF16)] * 2 + [((1,), F32)] * 3,
         [SMEM] + [VMEM] * (4 + len(text_cots)),
         (log_scale, image_embeds, text_embeds, image_cot, far_got, *text_cots),

time: 109 us -> 105 us (0.963)
  blocking collectives: 19.1 us -> 36.5 us
  starting transfers between devices: 54.7 us -> 39.1 us
  waiting for transfers between devices: 16.8 us -> 11 us
    all_to_all x0 -> x1, blocking collectives: none -> 17.4 us  [text_side(): lax.all_to_all(v, z_axes, 0, 0, tiled=True)]
    all_to_all x1, starting transfers between devices: 20.3 us -> 5.22 us  [on_device(): near = lax.all_to_all(sums, ('y', 'c', 'x'), 0, 0, tiled=True)]
    ppermute x3, waiting for transfers between devices: 11.5 us -> 0.01 us  [text_side(): lax.ppermute(part, 'y', [(i, (i + k) % y_count) for i in range(y_count)])]
    all_to_all x1, waiting for transfers between devices: 0.01 us -> 8.24 us  [on_device(): near = lax.all_to_all(sums, ('y', 'c', 'x'), 0, 0, tiled=True)]
    ppermute x1, waiting for transfers between devices: 2.5 us -> 0.01 us  [on_device(): text_got = lax.ppermute(text_sib, 'c', SWAP)]
    pallas_call x6 -> x7, Pallas kernels: 13.5 us -> 13.8 us  [call(): pl.pallas_call(kernel, out_shape=[jax.ShapeDtypeStruct(shape, dtype) for...]
  transfers between devices with their start and end apart: 8 -> 8, of which waited for: 5 -> 2; matrix products, arithmetic and copies ran while one was open for 0% -> 0% of each run, Pallas kernels for 6% -> 7%
where the time goes in v3:
time: 105 us; the launch traced here: 104 us
  starting transfers between devices  39.1 us (37%)
  blocking collectives  36.5 us (35%)
  Pallas kernels  13.8 us (13%)
  waiting for transfers between devices  11 us (10%)
  between operations  2.02 us (2%)
  local copies, waits for them, and re-layouts  1.7 us (2%)
    all_to_all x1, blocking collectives, gather(): mine = lax.all_to_all(text, 'y', 0, 0, tiled=True)  19.1 us
    all_to_all x1, blocking collectives, text_side(): lax.all_to_all(v, z_axes, 0, 0, tiled=True)  17.4 us
    ppermute x1, starting transfers between devices, on_device(): image_far = lax.ppermute(image, 'zh', SWAP)  16.3 us
    pallas_call x7, Pallas kernels, call(): pl.pallas_call(kernel, out_shape=[jax.ShapeDtypeStruct(shape, dtype) for...  13.8 us
    ppermute x3, starting transfers between devices, text_side(): lax.ppermute(part, 'y', [(i, (i + k) % y_count) for i in range(y_count)])  9.01 us
    all_to_all x1, waiting for transfers between devices, on_device(): near = lax.all_to_all(sums, ('y', 'c', 'x'), 0, 0, tiled=True)  8.24 us
    all_to_all x1, starting transfers between devices, on_device(): near = lax.all_to_all(sums, ('y', 'c', 'x'), 0, 0, tiled=True)  5.22 us
    ppermute x1, starting transfers between devices, gather(): return (mine, lax.ppermute(mine, 'c', SWAP))  4.35 us
  transfers between devices with their start and end apart: 8, of which 2 were waited for; matrix products, arithmetic and copies ran while one was open for 0% of the time, Pallas kernels for 7%

profile of v3, /device:TPU:1, one launch (start us, length us, event | category | flops | bytes accessed | tf_op | source)
XLA Modules:
  0.0 104.2 jit_solution(3757644952296677908)
XLA Ops:
  0.6 0.0 copy-start
  0.6 1.0 copy-done
  1.6 0.1 shard_map.86.image_ref
  1.7 16.3 %collective-permute-start.4 = (bf16[128,1152]{1,0:T(8,128)(2,1)S(1)}, bf16[128,1152]{1,0:T(8,128)(2,1)S(1)}, u32[]{:S(2)}, u32[]{:S(2)}) collective-permute-start(bf16[128,1152]{1,0:T(8,128)(2,1)S(1)} %shard_map.86.image_ref), channel_id=1, source_target_pairs={{0,256},{256,0},{1,257},{257,1},{2,258},{258,2},{3,259},{259,3},{4... | collective-permute-start | bytes 884744 | tf_op jit(solution)/shard_map/ppermute | solution.py:177
  19.3 27.4 %conditional.3 = (bf16[4,128,1152]{2,1,0:T(8,128)(2,1)}, bf16[4,128,1152]{2,1,0:T(8,128)(2,1)}) conditional(s32[]{:T(128)} %convert_element_type.7, () %tuple.30, bf16[128,1152]{1,0:T(8,128)(2,1)} %text_ref.1), branch_computations={%region_0.0_spmd, %region_1.0_spmd} | conditional | bytes 7077944 | solution.py:165
  19.3 1.1 %branch_1_fun.2 = bf16[4,128,1152]{2,1,0:T(8,128)(2,1)S(1)} custom-call(bf16[128,1152]{1,0:T(8,128)(2,1)} %matrix_ref.1), custom_call_target="tpu_custom_call" | custom-call | tf_op jit(solution)/shard_map/cond/branch_1_fun/pallas_call | solution.py:25
  20.5 19.1 %all_to_all.13 = bf16[4,128,1152]{2,1,0:T(8,128)(2,1)} all-to-all(bf16[4,128,1152]{2,1,0:T(8,128)(2,1)S(1)} %branch_1_fun.2), channel_id=1, replica_groups=mesh['zh'=2,'y'=4,'c'=2,'zl'=8,'x'=4] {'y'}, dimensions={0} | all-to-all | bytes 2359296 | tf_op jit(solution)/shard_map/cond/branch_1_fun/all_to_all | solution.py:181
  39.6 4.4 %collective-permute-start = (bf16[4,128,1152]{2,1,0:T(8,128)(2,1)}, bf16[4,128,1152]{2,1,0:T(8,128)(2,1)}, u32[]{:S(2)}, u32[]{:S(2)}) collective-permute-start(bf16[4,128,1152]{2,1,0:T(8,128)(2,1)} %all_to_all.13), channel_id=1, source_target_pairs={{0,32},{32,0},{1,33},{33,1},{2,34},{34,2},{3,35},{35,3},{4,36},{36... | collective-permute-start | bytes 3538952 | tf_op jit(solution)/shard_map/cond/branch_1_fun/ppermute | solution.py:182
  43.9 2.8 %collective-permute-done = bf16[4,128,1152]{2,1,0:T(8,128)(2,1)} collective-permute-done((bf16[4,128,1152]{2,1,0:T(8,128)(2,1)}, bf16[4,128,1152]{2,1,0:T(8,128)(2,1)}, u32[]{:S(2)}, u32[]{:S(2)}) %collective-permute-start) | collective-permute-done | bytes 1179680 | tf_op jit(solution)/shard_map/cond/branch_1_fun/ppermute | solution.py:182
  46.7 4.0 %shard_map.87 = (bf16[128,512]{1,0:T(8,128)(2,1)}, bf16[128,512]{1,0:T(8,128)(2,1)S(1)}, f32[128,1152]{1,0:T(8,128)S(1)}, f32[3,8,128]{2,1,0:T(8,128)S(1)}, bf16...) custom-call(f32[1]{0:T(128)S(6)} %copy.25.scale_ref, f32[1]{0:T(128)S(6)} %copy.26.bias_ref, ...), custom_call_target="tpu_custom_call" | custom-call | tf_op jit(solution)/shard_map/pallas_call | solution.py:25
  50.8 0.0 collective-permute-done.4.image_ref.image_far_ref
  50.8 2.8 %shard_map.88 = (bf16[128,512]{1,0:T(8,128)(2,1)}, bf16[128,512]{1,0:T(8,128)(2,1)S(1)}, bf16[128,1152]{1,0:T(8,128)(2,1)S(1)}, f32[32,24,128]{2,1,0:T(8,128)}) custom-call(f32[1]{0:T(128)S(6)} %copy.25.scale_ref, f32[1]{0:T(128)S(6)} %copy.26.bias_ref, bf16[128,1152]{1,0:T(8,128)(2,1)S(1)} %collective-permute-done.4.image_ref.image_far_ref, ...), custom_call_target="tpu_custom_call" | custom-call | tf_op jit(solution)/shard_map/pallas_call | solution.py:25
  53.6 0.8 shard_map.89
  54.4 2.3 %collective-permute-start.6 = (bf16[4,128,1152]{2,1,0:T(8,128)(2,1)S(1)}, bf16[4,128,1152]{2,1,0:T(8,128)(2,1)}, u32[]{:S(2)}, u32[]{:S(2)}) collective-permute-start(bf16[4,128,1152]{2,1,0:T(8,128)(2,1)S(1)} %shard_map.89), channel_id=1, source_target_pairs={{0,32},{32,0},{1,33},{33,1},{2,34},{34,2},{3,35},{35,3},{4,36},{36... | collective-permute-start | bytes 3538952 | tf_op jit(solution)/shard_map/ppermute | solution.py:200
  56.7 5.2 %all-to-all-start.2 = ((f32[32,24,128]{2,1,0:T(8,128)}), f32[32,24,128]{2,1,0:T(8,128)S(1)}, u32[]{:S(2)}, u32[]{:S(2)}) async-start(f32[32,24,128]{2,1,0:T(8,128)} %get-tuple-element.70), calls=%async_computation.2 | async-start | bytes 786432 | tf_op jit(solution)/shard_map/all_to_all | solution.py:201
  61.9 1.9 %collective-permute-start.5 = (bf16[128,1152]{1,0:T(8,128)(2,1)S(1)}, bf16[128,1152]{1,0:T(8,128)(2,1)S(1)}, u32[]{:S(2)}, u32[]{:S(2)}) collective-permute-start(bf16[128,1152]{1,0:T(8,128)(2,1)S(1)} %get-tuple-element.67), channel_id=1, source_target_pairs={{0,256},{256,0},{1,257},{257,1},{2,258},{258,2},{3,259},{259,3},{4... | collective-permute-start | bytes 884744 | tf_op jit(solution)/shard_map/ppermute | solution.py:197
  63.8 8.2 %all-to-all-done.2 = f32[32,24,128]{2,1,0:T(8,128)S(1)} async-done(((f32[32,24,128]{2,1,0:T(8,128)}), f32[32,24,128]{2,1,0:T(8,128)S(1)}, u32[]{:S(2)}, u32[]{:S(2)}) %all-to-all-start.2) | async-done | bytes 393248 | tf_op jit(solution)/shard_map/all_to_all | solution.py:201
  72.1 0.0 collective-permute-done.6
  72.1 0.0 copy-start.1
  72.1 29.6 %conditional.4 = (f32[128,1152]{1,0:T(8,128)S(1)}, bf16[128,1152]{1,0:T(8,128)(2,1)}, bf16[128,1152]{1,0:T(8,128)(2,1)}, bf16[128,1152]{1,0:T(8,128)(2,1)}, f32[16,1,128]{2,1,0:T(1,128)}) conditional(s32[]{:T(128)} %convert_element_type.7, () %tuple.31, (s32[1]{0:T(128)}, bf16[128,512]{1,0:T(8,128)(2,1)}, bf16[128,512]{1,0:T(8,128)(2,1)}, ...), branch_computations={%region_2.0_spmd, %region_3.0_spmd} | conditional | flops 2 | bytes 5128402 | solution.py:165
  72.1 0.0 copy-start.2
  72.1 0.7 copy-done.2
  72.8 2.3 %branch_1_fun.3 = (f32[16,1,128]{2,1,0:T(1,128)S(1)}, f32[128,1152]{1,0:T(8,128)S(1)}, bf16[128,1152]{1,0:T(8,128)(2,1)S(1)}, bf16[128,1152]{1,0:T(8,128)(2,1)S(1)}, bf16[128,1152]{1,0:T(8,128)(2,1)S(1)}) custom-call(s32[1]{0:T(128)} %get-tuple-element.21.y_ref, bf16[128,512]{1,0:T(8,128)(2,1)} %get-tuple-element.22.own_ref, ...), custom_call_target="tpu_custom_call" | custom-call | tf_op jit(solution)/shard_map/cond/branch_1_fun/pallas_call | solution.py:25
  75.2 2.3 %collective-permute-start.1 = (bf16[128,1152]{1,0:T(8,128)(2,1)S(1)}, bf16[128,1152]{1,0:T(8,128)(2,1)}, u32[]{:S(2)}, u32[]{:S(2)}) collective-permute-start(bf16[128,1152]{1,0:T(8,128)(2,1)S(1)} %get-tuple-element.29), channel_id=1, source_target_pairs={{0,64},{64,128},{128,192},{192,0},{1,65},{65,129},{129,193},{193,1... | collective-permute-start | bytes 884744 | tf_op jit(solution)/shard_map/cond/branch_1_fun/ppermute | solution.py:212
  77.4 3.6 %collective-permute-start.2 = (bf16[128,1152]{1,0:T(8,128)(2,1)S(1)}, bf16[128,1152]{1,0:T(8,128)(2,1)}, u32[]{:S(2)}, u32[]{:S(2)}) collective-permute-start(bf16[128,1152]{1,0:T(8,128)(2,1)S(1)} %get-tuple-element.30), channel_id=1, source_target_pairs={{0,128},{64,192},{128,0},{192,64},{1,129},{65,193},{129,1},{193,65... | collective-permute-start | bytes 884744 | tf_op jit(solution)/shard_map/cond/branch_1_fun/ppermute | solution.py:212
  81.1 3.1 %collective-permute-start.3 = (bf16[128,1152]{1,0:T(8,128)(2,1)S(1)}, bf16[128,1152]{1,0:T(8,128)(2,1)}, u32[]{:S(2)}, u32[]{:S(2)}) collective-permute-start(bf16[128,1152]{1,0:T(8,128)(2,1)S(1)} %get-tuple-element.31), channel_id=1, source_target_pairs={{0,192},{64,0},{128,64},{192,128},{1,193},{65,1},{129,65},{193,129... | collective-permute-start | bytes 884744 | tf_op jit(solution)/shard_map/cond/branch_1_fun/ppermute | solution.py:212
  84.2 17.4 %conditional = (f32[16,1,128]{2,1,0:T(1,128)}) conditional(s32[]{:T(128)} %convert_element_type.1, () %tuple.23, f32[16,1,128]{2,1,0:T(1,128)S(1)} %get-tuple-element.33), branch_computations={%region_4.0_spmd, %region_5.0_spmd} | conditional | bytes 16392 | solution.py:165
  84.2 17.4 %all_to_all.14 = f32[16,1,128]{2,1,0:T(1,128)} all-to-all(f32[16,1,128]{2,1,0:T(1,128)S(1)} %param.4), channel_id=1, replica_groups=mesh['zh'=2,'y'=4,'c'=2,'zl'=8,'x'=4] {'zh','zl'}, dimensions={0} | all-to-all | bytes 16384 | tf_op jit(solution)/shard_map/cond/branch_1_fun/cond/branch_1_fun/all_to_all | solution.py:215
  101.6 0.0 collective-permute-done.1
  101.6 0.0 collective-permute-done.2
  101.6 0.0 collective-permute-done.3
  101.7 0.0 collective-permute-done.5.far_ref
  101.7 0.0 copy-done.1
  101.7 2.5 %shard_map.90 = (bf16[128,1152]{1,0:T(8,128)(2,1)}, bf16[128,1152]{1,0:T(8,128)(2,1)}, f32[1]{0:T(128)}, f32[1]{0:T(128)}, f32[1]{0:T(128)}) custom-call(f32[1]{0:T(128)S(6)} %copy.25.scale_ref, bf16[128,1152]{1,0:T(8,128)(2,1)S(1)} %copy-done.1, bf16[128,1152]{1,0:T(8,128)(2,1)} %text_ref.1, f32[128,1152]{1,0:T(8,128)S(1)} %get-tuple-element.63.image_cot_ref, ...), custom_call_target="tpu_custom_call" | custom-call | tf_op jit(solution)/shard_map/pallas_call | solution.py:25
Async XLA Ops:
  0.6 1.0 copy-start
  1.7 49.0 %collective-permute-start.4 = (bf16[128,1152]{1,0:T(8,128)(2,1)S(1)}, bf16[128,1152]{1,0:T(8,128)(2,1)S(1)}, u32[]{:S(2)}, u32[]{:S(2)}) collective-permute-start(bf16[128,1152]{1,0:T(8,128)(2,1)S(1)} %shard_map.86.image_ref), channel_id=1, source_target_pairs={{0,256},{256,0},{1,257},{257,1},{2,258},{258,2},{3,259},{259,3},{4... | collective-permute-start | bytes 884744 | tf_op jit(solution)/shard_map/ppermute | solution.py:177
  39.6 7.2 %collective-permute-start = (bf16[4,128,1152]{2,1,0:T(8,128)(2,1)}, bf16[4,128,1152]{2,1,0:T(8,128)(2,1)}, u32[]{:S(2)}, u32[]{:S(2)}) collective-permute-start(bf16[4,128,1152]{2,1,0:T(8,128)(2,1)} %all_to_all.13), channel_id=1, source_target_pairs={{0,32},{32,0},{1,33},{33,1},{2,34},{34,2},{3,35},{35,3},{4,36},{36... | collective-permute-start | bytes 3538952 | tf_op jit(solution)/shard_map/cond/branch_1_fun/ppermute | solution.py:182
  54.4 17.7 %collective-permute-start.6 = (bf16[4,128,1152]{2,1,0:T(8,128)(2,1)S(1)}, bf16[4,128,1152]{2,1,0:T(8,128)(2,1)}, u32[]{:S(2)}, u32[]{:S(2)}) collective-permute-start(bf16[4,128,1152]{2,1,0:T(8,128)(2,1)S(1)} %shard_map.89), channel_id=1, source_target_pairs={{0,32},{32,0},{1,33},{33,1},{2,34},{34,2},{3,35},{35,3},{4,36},{36... | collective-permute-start | bytes 3538952 | tf_op jit(solution)/shard_map/ppermute | solution.py:200
  56.7 15.4 %all-to-all-start.2 = ((f32[32,24,128]{2,1,0:T(8,128)}), f32[32,24,128]{2,1,0:T(8,128)S(1)}, u32[]{:S(2)}, u32[]{:S(2)}) async-start(f32[32,24,128]{2,1,0:T(8,128)} %get-tuple-element.70), calls=%async_computation.2 | async-start | bytes 786432 | tf_op jit(solution)/shard_map/all_to_all | solution.py:201
  61.9 39.8 %collective-permute-start.5 = (bf16[128,1152]{1,0:T(8,128)(2,1)S(1)}, bf16[128,1152]{1,0:T(8,128)(2,1)S(1)}, u32[]{:S(2)}, u32[]{:S(2)}) collective-permute-start(bf16[128,1152]{1,0:T(8,128)(2,1)S(1)} %get-tuple-element.67), channel_id=1, source_target_pairs={{0,256},{256,0},{1,257},{257,1},{2,258},{258,2},{3,259},{259,3},{4... | collective-permute-start | bytes 884744 | tf_op jit(solution)/shard_map/ppermute | solution.py:197
  72.1 29.6 %copy-start.1 = (bf16[128,1152]{1,0:T(8,128)(2,1)S(1)}, bf16[128,1152]{1,0:T(8,128)(2,1)}, u32[]{:S(2)}) copy-start(bf16[128,1152]{1,0:T(8,128)(2,1)} %image_ref.1) | copy-start | bytes 884740
  72.1 0.7 copy-start.2
  75.2 26.5 %collective-permute-start.1 = (bf16[128,1152]{1,0:T(8,128)(2,1)S(1)}, bf16[128,1152]{1,0:T(8,128)(2,1)}, u32[]{:S(2)}, u32[]{:S(2)}) collective-permute-start(bf16[128,1152]{1,0:T(8,128)(2,1)S(1)} %get-tuple-element.29), channel_id=1, source_target_pairs={{0,64},{64,128},{128,192},{192,0},{1,65},{65,129},{129,193},{193,1... | collective-permute-start | bytes 884744 | tf_op jit(solution)/shard_map/cond/branch_1_fun/ppermute | solution.py:212
  77.4 24.2 %collective-permute-start.2 = (bf16[128,1152]{1,0:T(8,128)(2,1)S(1)}, bf16[128,1152]{1,0:T(8,128)(2,1)}, u32[]{:S(2)}, u32[]{:S(2)}) collective-permute-start(bf16[128,1152]{1,0:T(8,128)(2,1)S(1)} %get-tuple-element.30), channel_id=1, source_target_pairs={{0,128},{64,192},{128,0},{192,64},{1,129},{65,193},{129,1},{193,65... | collective-permute-start | bytes 884744 | tf_op jit(solution)/shard_map/cond/branch_1_fun/ppermute | solution.py:212
  81.1 20.6 %collective-permute-start.3 = (bf16[128,1152]{1,0:T(8,128)(2,1)S(1)}, bf16[128,1152]{1,0:T(8,128)(2,1)}, u32[]{:S(2)}, u32[]{:S(2)}) collective-permute-start(bf16[128,1152]{1,0:T(8,128)(2,1)S(1)} %get-tuple-element.31), channel_id=1, source_target_pairs={{0,192},{64,0},{128,64},{192,128},{1,193},{65,1},{129,65},{193,129... | collective-permute-start | bytes 884744 | tf_op jit(solution)/shard_map/cond/branch_1_fun/ppermute | solution.py:212

commit v4 on v3

--- a/solution.py
+++ b/solution.py
@@ -91,23 +91,50 @@
 
 
 def own_kernel(
-    scale_ref, bias_ref, y_ref, image_ref, mine_ref, sib_ref, coef_mine, coef_sib, cot_ref, sums_ref, mine_out, sib_out
+    scale_ref,
+    bias_ref,
+    y_ref,
+    image_ref,
+    mine_ref,
+    sib_ref,
+    coef_mine,
+    coef_sib,
+    cot_ref,
+    sums_ref,
+    mine_out,
+    sib_out,
+    image_out,
 ):
     mine_out[...] = mine_ref[...]
     sib_out[...] = sib_ref[...]
-    cot, sums = pairs(scale_ref, bias_ref, image_ref[...], mine_ref, sib_ref, coef_mine, coef_sib, y_ref[0])
+    image = unit(image_ref[...])
+    image_out[...] = image
+    cot, sums = pairs(scale_ref, bias_ref, image, mine_ref, sib_ref, coef_mine, coef_sib, y_ref[0])
     cot_ref[...] = cot
     for k in range(3):
-        sums_ref[k] = sums[k]
-
-
-def cross_kernel(scale_ref, bias_ref, image_ref, mine_ref, sib_ref, before_ref, coef_mine, coef_sib, cot_ref, sums_ref):
-    cot, sums = pairs(scale_ref, bias_ref, image_ref[...], mine_ref, sib_ref, coef_mine, coef_sib)
+        sums_ref[k * 8 : (k + 1) * 8] = sums[k]
+
+
+def cross_kernel(
+    scale_ref,
+    bias_ref,
+    image_ref,
+    mine_ref,
+    sib_ref,
+    before_ref,
+    coef_mine,
+    coef_sib,
+    cot_ref,
+    sums_ref,
+    image_out,
+):
+    image = unit(image_ref[...])
+    image_out[...] = image
+    cot, sums = pairs(scale_ref, bias_ref, image, mine_ref, sib_ref, coef_mine, coef_sib)
     cot_ref[...] = cot.astype(BF16)
     for k in range(3):
-        total = sums[k] + before_ref[k]
-        for peer in range(sums_ref.shape[0]):
-            sums_ref[peer, k * 8 : (k + 1) * 8] = total
+        rows = slice(k * 8, (k + 1) * 8)
+        sums_ref[rows] = sums[k] + before_ref[rows]
 
 
 def text_part(own_ref, cross_ref, image_ref, image_far_ref, block):
@@ -123,12 +150,16 @@
         out_ref[k] = text_part(own_ref, cross_ref, image_ref, image_far_ref, k).astype(BF16)
 
 
-def text_mine_kernel(y_ref, own_ref, cross_ref, image_ref, image_far_ref, near_ref, got_ref, spread_ref, *out_refs):
+def text_mine_kernel(y_ref, own_ref, cross_ref, image_ref, image_far_ref, got_ref, sums_ref, spread_ref, *out_refs):
+    spread_ref[...] = jnp.broadcast_to(sums_ref[...][None], spread_ref.shape)
     count = len(out_refs)
     for k in range(count):
         block = lax.rem(y_ref[0] + k, count)
         total = text_part(own_ref, cross_ref, image_ref, image_far_ref, block) + got_ref[block].astype(F32)
         out_refs[k][...] = total.astype(out_refs[k].dtype)
+
+
+def sum_kernel(near_ref, spread_ref):
     near = jnp.sum(near_ref[...], axis=0)
     lane = lax.broadcasted_iota(jnp.int32, (1, 128), 1)
     row = jnp.zeros((1, 128), F32)
@@ -145,13 +176,15 @@
     return (inverse * cot - (inverse * inverse * inverse * along) * floats).astype(BF16)
 
 
-def last_kernel(batch, scale_ref, image_ref, text_ref, image_cot_ref, far_ref, text_cot_ref, *refs):
-    *got_refs, totals_ref, image_grad, text_grad, loss_ref, scale_grad, bias_grad = refs
-    image_grad[...] = pull(image_ref[...], image_cot_ref[...] + far_ref[...].astype(F32), scale_ref[0])
-    cot = text_cot_ref[...]
-    for got_ref in got_refs:
+def grad_kernel(scale_ref, embeds_ref, cot_ref, *refs):
+    cot = cot_ref[...]
+    for got_ref in refs[:-1]:
         cot = cot + got_ref[...].astype(F32)
-    text_grad[...] = pull(text_ref[...], cot, scale_ref[0])
+    refs[-1][...] = pull(embeds_ref[...], cot, scale_ref[0])
+
+
+def last_kernel(batch, scale_ref, embeds_ref, cot_ref, got_ref, totals_ref, grad_ref, loss_ref, scale_grad, bias_grad):
+    grad_kernel(scale_ref, embeds_ref, cot_ref, got_ref, grad_ref)
     totals = jnp.sum(totals_ref[...], axis=0)
     lane = lax.broadcasted_iota(jnp.int32, (1, 128), 1)
     loss, scale, bias = (jnp.sum(jnp.where(lane == k, totals, 0.0)) for k in range(3))
@@ -173,24 +206,23 @@
     block, blocks = (rows, width), (y_count, rows, width)
     half = (rows, y_count * rows)
 
-    (image,) = call(norm_kernel, [(block, BF16)], [VMEM], (image_embeds,))
-    image_far = lax.ppermute(image, "zh", SWAP)
-
-    def gather(text_embeds):
-        (text,) = call(norm_kernel, [(blocks, BF16)], [VMEM], (text_embeds,))
+    image_far = lax.ppermute(image_embeds, "zh", SWAP)
+    (text,) = call(norm_kernel, [(blocks, BF16)], [VMEM], (text_embeds,))
+
+    def gather(text):
         mine = lax.all_to_all(text, "y", 0, 0, tiled=True)
         return mine, lax.ppermute(mine, "c", SWAP)
 
-    mine, sib = region(gather, inside, text_embeds)
-    own_mine, own_sib, image_cot, sums, mine, sib = call(
+    mine, sib = region(gather, inside, text)
+    own_mine, own_sib, image_cot, sums, mine, sib, image = call(
         own_kernel,
-        [(half, BF16), (half, BF16), (block, F32), ((3, 8, 128), F32), (blocks, BF16), (blocks, BF16)],
+        [(half, BF16), (half, BF16), (block, F32), ((24, 128), F32), (blocks, BF16), (blocks, BF16), (block, BF16)],
         [SMEM] * 3 + [VMEM] * 3,
-        (log_scale, logit_bias, y, image, mine, sib),
-    )
-    far_mine, far_sib, far_cot, sums = call(
+        (log_scale, logit_bias, y, image_embeds, mine, sib),
+    )
+    far_mine, far_sib, far_cot, sums, image_far = call(
         cross_kernel,
-        [(half, BF16), (half, BF16), (block, BF16), ((lax.axis_size(("y", "c", "x")), 24, 128), F32)],
+        [(half, BF16), (half, BF16), (block, BF16), ((24, 128), F32), (block, BF16)],
         [SMEM] * 2 + [VMEM] * 4,
         (log_scale, logit_bias, image_far, mine, sib, sums),
     )
@@ -198,30 +230,50 @@
 
     (text_sib,) = call(text_sib_kernel, [(blocks, BF16)], [VMEM] * 4, (own_sib, far_sib, image, image_far))
     text_got = lax.ppermute(text_sib, "c", SWAP)
-    near = lax.all_to_all(sums, ("y", "c", "x"), 0, 0, tiled=True)
-
-    def text_side(own_mine, far_mine, image, image_far, y, near, text_got):
-        z_axes = ("zh", "zl")
+
+    def text_side(own_mine, far_mine, image, image_far, text_got, y, sums, text_embeds, log_scale):
+        near_axes = ("y", "c", "x")
         spread, text_kept, *text_send = call(
             text_mine_kernel,
-            [((lax.axis_size(z_axes), 1, 128), F32), (block, F32)] + [(block, BF16)] * (y_count - 1),
+            [((lax.axis_size(near_axes), 24, 128), F32), (block, F32)] + [(block, BF16)] * (y_count - 1),
             [SMEM] + [VMEM] * 6,
-            (y, own_mine, far_mine, image, image_far, near, text_got),
+            (y, own_mine, far_mine, image, image_far, text_got, sums),
         )
+        near = lax.all_to_all(spread, near_axes, 0, 0, tiled=True)
         got = [
             lax.ppermute(part, "y", [(i, (i + k) % y_count) for i in range(y_count)])
             for k, part in enumerate(text_send, 1)
         ]
-        totals = region(lambda v: lax.all_to_all(v, z_axes, 0, 0, tiled=True), y[0] < y_count, spread)
-        return text_kept, *got, totals
-
-    text_cots = region(text_side, inside, own_mine, far_mine, image, image_far, y, near, text_got)
-    image_grad, text_grad, loss, scale_grad, bias_grad = call(
+        z_axes = ("zh", "zl")
+        (spread,) = call(sum_kernel, [((lax.axis_size(z_axes), 1, 128), F32)], [VMEM], (near,))
+        totals = lax.all_to_all(spread, z_axes, 0, 0, tiled=True)
+        (text_grad,) = call(
+            grad_kernel,
+            [(block, BF16)],
+            [SMEM] + [VMEM] * (2 + len(got)),
+            (log_scale, text_embeds, text_kept, *got),
+        )
+        return text_grad, totals
+
+    text_grad, totals = region(
+        text_side,
+        inside,
+        own_mine,
+        far_mine,
+        image,
+        image_far,
+        text_got,
+        y,
+        sums,
+        text_embeds,
+        log_scale,
+    )
+    image_grad, loss, scale_grad, bias_grad = call(
         functools.partial(last_kernel, rows * lax.axis_size(AXES)),
-        [(block, BF16)] * 2 + [((1,), F32)] * 3,
-        [SMEM] + [VMEM] * (4 + len(text_cots)),
-        (log_scale, image_embeds, text_embeds, image_cot, far_got, *text_cots),
-        out_specs=[VMEM] * 2 + [SMEM] * 3,
+        [(block, BF16)] + [((1,), F32)] * 3,
+        [SMEM] + [VMEM] * 4,
+        (log_scale, image_embeds, image_cot, far_got, totals),
+        out_specs=[VMEM] + [SMEM] * 3,
     )
     return loss, image_grad, text_grad, scale_grad, bias_grad
 

time: 105 us -> 103 us (0.981); the launches traced: 104 us -> 101 us
  blocking collectives: 36.5 us -> 19.2 us
  starting transfers between devices: 39.1 us -> 52.1 us
  Pallas kernels: 13.8 us -> 14.9 us
    all_to_all x1 -> x0, blocking collectives: 17.4 us -> none  [text_side(): lax.all_to_all(v, z_axes, 0, 0, tiled=True)]
    all_to_all x1 -> x2, starting transfers between devices: 5.22 us -> 16.6 us  [the longest x1 11.2 us: text_side(): totals = lax.all_to_all(spread, z_axes, 0, 0, tiled=True)]
    ppermute x3, starting transfers between devices: 9.01 us -> 10.7 us  [text_side(): lax.ppermute(part, 'y', [(i, (i + k) % y_count) for i in range(y_count)])]
    pallas_call x7 -> x8, Pallas kernels: 13.8 us -> 14.9 us  [call(): pl.pallas_call(kernel, out_shape=[jax.ShapeDtypeStruct(shape, dtype) for...]
    all_to_all x1 -> x2, waiting for transfers between devices: 8.24 us -> 8.69 us  [the longest x1 8.69 us: text_side(): totals = lax.all_to_all(spread, z_axes, 0, 0, tiled=True)]
  transfers between devices with their start and end apart: 8 -> 9, of which waited for: 2 -> 3; matrix products, arithmetic and copies ran while one was open for 0% -> 0% of each run, Pallas kernels for 7% -> 10%
where the time goes in v4:
time: 103 us; the launch traced here: 101 us
  starting transfers between devices  52.1 us (51%)
  blocking collectives  19.2 us (19%)
  Pallas kernels  14.9 us (14%)
  waiting for transfers between devices  12 us (12%)
  between operations  2 us (2%)
    all_to_all x1, blocking collectives, gather(): mine = lax.all_to_all(text, 'y', 0, 0, tiled=True)  19.2 us
    ppermute x1, starting transfers between devices, on_device(): image_far = lax.ppermute(image_embeds, 'zh', SWAP)  16.3 us
    pallas_call x8, Pallas kernels, call(): pl.pallas_call(kernel, out_shape=[jax.ShapeDtypeStruct(shape, dtype) for...  14.9 us
    all_to_all x1, starting transfers between devices, text_side(): totals = lax.all_to_all(spread, z_axes, 0, 0, tiled=True)  11.2 us
    ppermute x3, starting transfers between devices, text_side(): lax.ppermute(part, 'y', [(i, (i + k) % y_count) for i in range(y_count)])  10.7 us
    all_to_all x1, waiting for transfers between devices, text_side(): totals = lax.all_to_all(spread, z_axes, 0, 0, tiled=True)  8.69 us
    all_to_all x1, starting transfers between devices, text_side(): near = lax.all_to_all(spread, near_axes, 0, 0, tiled=True)  5.43 us
    ppermute x1, starting transfers between devices, gather(): return (mine, lax.ppermute(mine, 'c', SWAP))  4.35 us
  transfers between devices with their start and end apart: 9, of which 3 were waited for; matrix products, arithmetic and copies ran while one was open for 0% of the time, Pallas kernels for 10%

profile of v4, /device:TPU:1, one launch (start us, length us, event | category | flops | bytes accessed | tf_op | source)
XLA Modules:
  0.0 101.0 jit_solution(13957678074640520218)
XLA Ops:
  0.6 16.3 %collective-permute-start.4 = (bf16[128,1152]{1,0:T(8,128)(2,1)}, bf16[128,1152]{1,0:T(8,128)(2,1)S(1)}, u32[]{:S(2)}, u32[]{:S(2)}) collective-permute-start(bf16[128,1152]{1,0:T(8,128)(2,1)} %embeds_ref.1), channel_id=1, source_target_pairs={{0,256},{256,0},{1,257},{257,1},{2,258},{258,2},{3,259},{259,3},{4... | collective-permute-start | bytes 884744 | tf_op jit(solution)/shard_map/ppermute | solution.py:209
  16.9 1.1 %shard_map.83 = bf16[4,128,1152]{2,1,0:T(8,128)(2,1)S(1)} custom-call(bf16[128,1152]{1,0:T(8,128)(2,1)} %matrix_ref.1), custom_call_target="tpu_custom_call" | custom-call | tf_op jit(solution)/shard_map/pallas_call | solution.py:25
  19.4 0.0 copy-start
  19.4 26.4 %conditional.2 = (bf16[4,128,1152]{2,1,0:T(8,128)(2,1)}, bf16[4,128,1152]{2,1,0:T(8,128)(2,1)}) conditional(s32[]{:T(128)} %convert_element_type.4, () %tuple.24, bf16[4,128,1152]{2,1,0:T(8,128)(2,1)S(1)} %shard_map.83), branch_computations={%region_0.0_spmd, %region_1.0_spmd} | conditional | bytes 7077944 | solution.py:198
  19.4 19.2 %all_to_all.12 = bf16[4,128,1152]{2,1,0:T(8,128)(2,1)} all-to-all(bf16[4,128,1152]{2,1,0:T(8,128)(2,1)S(1)} %param.1), channel_id=1, replica_groups=mesh['zh'=2,'y'=4,'c'=2,'zl'=8,'x'=4] {'y'}, dimensions={0} | all-to-all | bytes 2359296 | tf_op jit(solution)/shard_map/cond/branch_1_fun/all_to_all | solution.py:213
  38.6 4.4 %collective-permute-start = (bf16[4,128,1152]{2,1,0:T(8,128)(2,1)}, bf16[4,128,1152]{2,1,0:T(8,128)(2,1)}, u32[]{:S(2)}, u32[]{:S(2)}) collective-permute-start(bf16[4,128,1152]{2,1,0:T(8,128)(2,1)} %all_to_all.12), channel_id=1, source_target_pairs={{0,32},{32,0},{1,33},{33,1},{2,34},{34,2},{3,35},{35,3},{4,36},{36... | collective-permute-start | bytes 3538952 | tf_op jit(solution)/shard_map/cond/branch_1_fun/ppermute | solution.py:214
  43.0 2.8 %collective-permute-done = bf16[4,128,1152]{2,1,0:T(8,128)(2,1)} collective-permute-done((bf16[4,128,1152]{2,1,0:T(8,128)(2,1)}, bf16[4,128,1152]{2,1,0:T(8,128)(2,1)}, u32[]{:S(2)}, u32[]{:S(2)}) %collective-permute-start) | collective-permute-done | bytes 1179680 | tf_op jit(solution)/shard_map/cond/branch_1_fun/ppermute | solution.py:214
  45.8 0.0 copy-done
  45.8 4.0 %shard_map.84 = (bf16[128,512]{1,0:T(8,128)(2,1)S(1)}, bf16[128,512]{1,0:T(8,128)(2,1)S(1)}, f32[128,1152]{1,0:T(8,128)S(1)}, f32[24,128]{1,0:T(8,128)S(1)}, bf1...) custom-call(f32[1]{0:T(128)S(6)} %copy.17.scale_ref, ...), custom_call_target="tpu_custom_call" | custom-call | tf_op jit(solution)/shard_map/pallas_call | solution.py:25
  49.8 0.0 collective-permute-done.4.image_ref
  49.8 2.2 %shard_map.85 = (bf16[128,512]{1,0:T(8,128)(2,1)S(1)}, bf16[128,512]{1,0:T(8,128)(2,1)S(1)}, bf16[128,1152]{1,0:T(8,128)(2,1)S(1)}, f32[24,128]{1,0:T(8,128)S(1)}, bf16[128,1152]{1,0:T(8,128)(2,1)S(1)}) custom-call(f32[1]{0:T(128)S(6)} %copy.17.scale_ref, f32[1]{0:T(128)S(6)} %copy.18.bias_ref, bf16[128,1152]{1,0:T(8,128)(2,1)S(1)} %collective-permute-done.4.image_ref, ...), custom_call_target="tpu_custom_call" | custom-call | tf_op jit(solution)/shard_map/pallas_call | solution.py:25
  52.0 0.8 shard_map.86
  52.9 2.3 %collective-permute-start.6 = (bf16[4,128,1152]{2,1,0:T(8,128)(2,1)S(1)}, bf16[4,128,1152]{2,1,0:T(8,128)(2,1)S(1)}, u32[]{:S(2)}, u32[]{:S(2)}) collective-permute-start(bf16[4,128,1152]{2,1,0:T(8,128)(2,1)S(1)} %shard_map.86), channel_id=1, source_target_pairs={{0,32},{32,0},{1,33},{33,1},{2,34},{34,2},{3,35},{35,3},{4,36},{36... | collective-permute-start | bytes 3538952 | tf_op jit(solution)/shard_map/ppermute | solution.py:232
  55.1 1.9 %collective-permute-start.5 = (bf16[128,1152]{1,0:T(8,128)(2,1)S(1)}, bf16[128,1152]{1,0:T(8,128)(2,1)S(1)}, u32[]{:S(2)}, u32[]{:S(2)}) collective-permute-start(bf16[128,1152]{1,0:T(8,128)(2,1)S(1)} %get-tuple-element.64), channel_id=1, source_target_pairs={{0,256},{256,0},{1,257},{257,1},{2,258},{258,2},{3,259},{259,3},{4... | collective-permute-start | bytes 884744 | tf_op jit(solution)/shard_map/ppermute | solution.py:229
  57.1 0.5 collective-permute-done.6
  57.6 41.8 %conditional.3 = (bf16[128,1152]{1,0:T(8,128)(2,1)}, f32[16,1,128]{2,1,0:T(1,128)}) conditional(s32[]{:T(128)} %convert_element_type.4, () %tuple.25, (s32[1]{0:T(128)}, bf16[128,512]{1,0:T(8,128)(2,1)S(1)}, bf16[128,512]{1,0:T(8,128)(2,1)S(1)}, bf16[128,1152]{1,0:T(8,128)(2,1)S(1)}, bf16[128,1152]{1,0:T(8,128)(2,1)S(1)}, ...), branch_computations={%region_2.0_spmd, %region_3.0_spmd} | conditional | bytes 5923044 | solution.py:198
  57.6 1.6 %branch_1_fun.3 = (f32[32,24,128]{2,1,0:T(8,128)}, f32[128,1152]{1,0:T(8,128)S(1)}, bf16[128,1152]{1,0:T(8,128)(2,1)}, bf16[128,1152]{1,0:T(8,128)(2,1)}, bf16[128,1152]{1,0:T(8,128)(2,1)S(1)}) custom-call(s32[1]{0:T(128)} %get-tuple-element.21.y_ref, bf16[128,512]{1,0:T(8,128)(2,1)S(1)} %get-tuple-element.22.own_ref, ...), custom_call_target="tpu_custom_call" | custom-call | tf_op jit(solution)/shard_map/cond/branch_1_fun/pallas_call | solution.py:25
  59.2 0.0 copy-start.1
  59.2 0.7 copy-done.1
  59.9 5.4 %all-to-all-start.1 = ((f32[32,24,128]{2,1,0:T(8,128)}), f32[32,24,128]{2,1,0:T(8,128)S(1)}, u32[]{:S(2)}, u32[]{:S(2)}) async-start(f32[32,24,128]{2,1,0:T(8,128)} %get-tuple-element.32), calls=%async_computation.1 | async-start | bytes 786432 | tf_op jit(solution)/shard_map/cond/branch_1_fun/all_to_all | solution.py:242
  65.4 3.3 %collective-permute-start.1 = (bf16[128,1152]{1,0:T(8,128)(2,1)}, bf16[128,1152]{1,0:T(8,128)(2,1)S(1)}, u32[]{:S(2)}, u32[]{:S(2)}) collective-permute-start(bf16[128,1152]{1,0:T(8,128)(2,1)} %get-tuple-element.29), channel_id=1, source_target_pairs={{0,64},{64,128},{128,192},{192,0},{1,65},{65,129},{129,193},{193,1... | collective-permute-start | bytes 884744 | tf_op jit(solution)/shard_map/cond/branch_1_fun/ppermute | solution.py:244
  68.7 4.4 %collective-permute-start.2 = (bf16[128,1152]{1,0:T(8,128)(2,1)}, bf16[128,1152]{1,0:T(8,128)(2,1)S(1)}, u32[]{:S(2)}, u32[]{:S(2)}) collective-permute-start(bf16[128,1152]{1,0:T(8,128)(2,1)} %get-tuple-element.30), channel_id=1, source_target_pairs={{0,128},{64,192},{128,0},{192,64},{1,129},{65,193},{129,1},{193,65... | collective-permute-start | bytes 884744 | tf_op jit(solution)/shard_map/cond/branch_1_fun/ppermute | solution.py:244
  73.0 3.0 %collective-permute-start.3 = (bf16[128,1152]{1,0:T(8,128)(2,1)}, bf16[128,1152]{1,0:T(8,128)(2,1)S(1)}, u32[]{:S(2)}, u32[]{:S(2)}) collective-permute-start(bf16[128,1152]{1,0:T(8,128)(2,1)} %copy-done.1), channel_id=1, source_target_pairs={{0,192},{64,0},{128,64},{192,128},{1,193},{65,1},{129,65},{193,129... | collective-permute-start | bytes 884744 | tf_op jit(solution)/shard_map/cond/branch_1_fun/ppermute | solution.py:244
  76.1 0.0 all-to-all-done.1.near_ref
  76.1 0.8 branch_1_fun.5
  76.8 11.2 %all-to-all-start.2 = ((f32[16,1,128]{2,1,0:T(1,128)}), f32[16,1,128]{2,1,0:T(1,128)}, u32[]{:S(2)}, u32[]{:S(2)}) async-start(f32[16,1,128]{2,1,0:T(1,128)} %branch_1_fun.5), calls=%async_computation.2 | async-start | bytes 16384 | tf_op jit(solution)/shard_map/cond/branch_1_fun/all_to_all | solution.py:249
  88.0 0.0 collective-permute-done.1.refs_0_
  88.0 0.0 collective-permute-done.2.refs_1_
  88.0 0.0 collective-permute-done.3.refs_2_
  88.0 2.6 %branch_1_fun.4 = bf16[128,1152]{1,0:T(8,128)(2,1)} custom-call(f32[1]{0:T(128)} %get-tuple-element.19.scale_ref, bf16[128,1152]{1,0:T(8,128)(2,1)} %get-tuple-element.20.embeds_ref, f32[128,1152]{1,0:T(8,128)S(1)} %get-tuple-element.28.cot_ref, bf16[128,1152]{1,0:T(8,128)(2,1)S(1)} %collective-permute-done.1.refs_0_, ...), custom_call_target="tpu_custom_call" | custom-call | tf_op jit(solution)/shard_map/cond/branch_1_fun/pallas_call | solution.py:25
  90.7 8.7 %all-to-all-done.2 = f32[16,1,128]{2,1,0:T(1,128)} async-done(((f32[16,1,128]{2,1,0:T(1,128)}), f32[16,1,128]{2,1,0:T(1,128)}, u32[]{:S(2)}, u32[]{:S(2)}) %all-to-all-start.2) | async-done | bytes 8224 | tf_op jit(solution)/shard_map/cond/branch_1_fun/all_to_all | solution.py:249
  99.4 0.0 collective-permute-done.5.got_ref
  99.4 1.7 %shard_map.87 = (bf16[128,1152]{1,0:T(8,128)(2,1)}, f32[1]{0:T(128)}, f32[1]{0:T(128)}, f32[1]{0:T(128)}) custom-call(f32[1]{0:T(128)S(6)} %copy.17.scale_ref, bf16[128,1152]{1,0:T(8,128)(2,1)S(1)} %copy-done, f32[128,1152]{1,0:T(8,128)S(1)} %get-tuple-element.60.cot_ref, bf16[128,1152]{1,0:T(8,128)(2,1)S(1)} %collective-permute-done.5.got_ref, ...), custom_call_target="tpu_custom_call" | custom-call | tf_op jit(solution)/shard_map/pallas_call | solution.py:25
Async XLA Ops:
  0.6 49.2 %collective-permute-start.4 = (bf16[128,1152]{1,0:T(8,128)(2,1)}, bf16[128,1152]{1,0:T(8,128)(2,1)S(1)}, u32[]{:S(2)}, u32[]{:S(2)}) collective-permute-start(bf16[128,1152]{1,0:T(8,128)(2,1)} %embeds_ref.1), channel_id=1, source_target_pairs={{0,256},{256,0},{1,257},{257,1},{2,258},{258,2},{3,259},{259,3},{4... | collective-permute-start | bytes 884744 | tf_op jit(solution)/shard_map/ppermute | solution.py:209
  19.4 26.4 %copy-start = (bf16[128,1152]{1,0:T(8,128)(2,1)S(1)}, bf16[128,1152]{1,0:T(8,128)(2,1)}, u32[]{:S(2)}) copy-start(bf16[128,1152]{1,0:T(8,128)(2,1)} %embeds_ref.1) | copy-start | bytes 884740
  38.6 7.2 %collective-permute-start = (bf16[4,128,1152]{2,1,0:T(8,128)(2,1)}, bf16[4,128,1152]{2,1,0:T(8,128)(2,1)}, u32[]{:S(2)}, u32[]{:S(2)}) collective-permute-start(bf16[4,128,1152]{2,1,0:T(8,128)(2,1)} %all_to_all.12), channel_id=1, source_target_pairs={{0,32},{32,0},{1,33},{33,1},{2,34},{34,2},{3,35},{35,3},{4,36},{36... | collective-permute-start | bytes 3538952 | tf_op jit(solution)/shard_map/cond/branch_1_fun/ppermute | solution.py:214
  52.9 4.7 %collective-permute-start.6 = (bf16[4,128,1152]{2,1,0:T(8,128)(2,1)S(1)}, bf16[4,128,1152]{2,1,0:T(8,128)(2,1)S(1)}, u32[]{:S(2)}, u32[]{:S(2)}) collective-permute-start(bf16[4,128,1152]{2,1,0:T(8,128)(2,1)S(1)} %shard_map.86), channel_id=1, source_target_pairs={{0,32},{32,0},{1,33},{33,1},{2,34},{34,2},{3,35},{35,3},{4,36},{36... | collective-permute-start | bytes 3538952 | tf_op jit(solution)/shard_map/ppermute | solution.py:232
  55.1 44.2 %collective-permute-start.5 = (bf16[128,1152]{1,0:T(8,128)(2,1)S(1)}, bf16[128,1152]{1,0:T(8,128)(2,1)S(1)}, u32[]{:S(2)}, u32[]{:S(2)}) collective-permute-start(bf16[128,1152]{1,0:T(8,128)(2,1)S(1)} %get-tuple-element.64), channel_id=1, source_target_pairs={{0,256},{256,0},{1,257},{257,1},{2,258},{258,2},{3,259},{259,3},{4... | collective-permute-start | bytes 884744 | tf_op jit(solution)/shard_map/ppermute | solution.py:229
  59.2 0.7 copy-start.1
  59.9 16.2 %all-to-all-start.1 = ((f32[32,24,128]{2,1,0:T(8,128)}), f32[32,24,128]{2,1,0:T(8,128)S(1)}, u32[]{:S(2)}, u32[]{:S(2)}) async-start(f32[32,24,128]{2,1,0:T(8,128)} %get-tuple-element.32), calls=%async_computation.1 | async-start | bytes 786432 | tf_op jit(solution)/shard_map/cond/branch_1_fun/all_to_all | solution.py:242
  65.4 22.6 %collective-permute-start.1 = (bf16[128,1152]{1,0:T(8,128)(2,1)}, bf16[128,1152]{1,0:T(8,128)(2,1)S(1)}, u32[]{:S(2)}, u32[]{:S(2)}) collective-permute-start(bf16[128,1152]{1,0:T(8,128)(2,1)} %get-tuple-element.29), channel_id=1, source_target_pairs={{0,64},{64,128},{128,192},{192,0},{1,65},{65,129},{129,193},{193,1... | collective-permute-start | bytes 884744 | tf_op jit(solution)/shard_map/cond/branch_1_fun/ppermute | solution.py:244
  68.7 19.4 %collective-permute-start.2 = (bf16[128,1152]{1,0:T(8,128)(2,1)}, bf16[128,1152]{1,0:T(8,128)(2,1)S(1)}, u32[]{:S(2)}, u32[]{:S(2)}) collective-permute-start(bf16[128,1152]{1,0:T(8,128)(2,1)} %get-tuple-element.30), channel_id=1, source_target_pairs={{0,128},{64,192},{128,0},{192,64},{1,129},{65,193},{129,1},{193,65... | collective-permute-start | bytes 884744 | tf_op jit(solution)/shard_map/cond/branch_1_fun/ppermute | solution.py:244
  73.0 15.0 %collective-permute-start.3 = (bf16[128,1152]{1,0:T(8,128)(2,1)}, bf16[128,1152]{1,0:T(8,128)(2,1)S(1)}, u32[]{:S(2)}, u32[]{:S(2)}) collective-permute-start(bf16[128,1152]{1,0:T(8,128)(2,1)} %copy-done.1), channel_id=1, source_target_pairs={{0,192},{64,0},{128,64},{192,128},{1,193},{65,1},{129,65},{193,129... | collective-permute-start | bytes 884744 | tf_op jit(solution)/shard_map/cond/branch_1_fun/ppermute | solution.py:244
  76.8 22.5 %all-to-all-start.2 = ((f32[16,1,128]{2,1,0:T(1,128)}), f32[16,1,128]{2,1,0:T(1,128)}, u32[]{:S(2)}, u32[]{:S(2)}) async-start(f32[16,1,128]{2,1,0:T(1,128)} %branch_1_fun.5), calls=%async_computation.2 | async-start | bytes 16384 | tf_op jit(solution)/shard_map/cond/branch_1_fun/all_to_all | solution.py:249

commit v5 on v4

v5 whole, which is shorter than its diff:
```python
import functools

import jax
import jax.numpy as jnp
from jax import lax
from jax.experimental import pallas as pl
from jax.experimental.pallas import tpu as pltpu
from jax.sharding import Mesh, PartitionSpec as P

EPSILON = 1e-06
F32 = jnp.float32
BF16 = jnp.bfloat16
AXES = ("zh", "y", "c", "zl", "x")
SIZES = (2, 4, 2, 8, 4)

VMEM = pl.BlockSpec(memory_space=pltpu.VMEM)
SMEM = pl.BlockSpec(memory_space=pltpu.SMEM)
HBM = pl.BlockSpec(memory_space=pltpu.HBM)
PARAMS = pltpu.CompilerParams(vmem_limit_bytes=16 * 1024 * 1024)
SWAP = ((0, 1), (1, 0))
CHUNK = 256


def call(kernel, outs, in_specs, args, scratch=(), out_specs=None):
    return pl.pallas_call(
        kernel,
        out_shape=[jax.ShapeDtypeStruct(shape, dtype) for shape, dtype in outs],
        in_specs=in_specs,
        out_specs=out_specs or [VMEM] * len(outs),
        scratch_shapes=scratch,
        compiler_params=PARAMS,
    )(*args)


def unit(matrix):
    floats = matrix.astype(F32)
    return (floats * lax.rsqrt(jnp.sum(floats * floats, axis=1, keepdims=True) + EPSILON)).astype(BF16)


def first_kernel(scale_ref, bias_ref, text_ref, text_out, scalars_ref, scale, bias, sems):
    copies = [
        pltpu.make_async_copy(scale_ref, scale, sems.at[0]),
        pltpu.make_async_copy(bias_ref, bias, sems.at[1]),
    ]
    for copy in copies:
        copy.start()
    rows = unit(text_ref[...])
    for k in range(text_out.shape[0]):
        text_out[k] = rows
    for copy in copies:
        copy.wait()
    row = lax.broadcasted_iota(jnp.int32, scalars_ref.shape, 0)
    temper = jnp.exp(jnp.full(scalars_ref.shape, scale[0], F32))
    scalars_ref[...] = jnp.where(row == 0, temper, bias[0])


def fold(values):
    rows, cols = values.shape
    total = jnp.sum(values.reshape(rows // 8, 8, cols), axis=0)
    return sum(total[:, k * 128 : (k + 1) * 128] for k in range(cols // 128))


def pair_chunk(image, text, temper, offset, positive):
    products = lax.dot_general(image, text, (((1,), (1,)), ((), ())), preferred_element_type=F32)
    scaled = temper * products
    logits = scaled + offset
    small = jnp.exp(-jnp.abs(logits))
    part = 1.0 / (1.0 + small)
    coef = jnp.where(logits >= 0.0, 1.0, small) * part
    signed = logits
    if positive is not None:
        coef = coef - jnp.where(positive, 1.0, 0.0)
        signed = jnp.where(positive, -logits, logits)
    losses = jnp.maximum(signed, 0.0) + jnp.log1p(small)
    return coef, (fold(losses), fold(coef * scaled), fold(coef))


def pairs(scalars_ref, image, text_ref, coef_ref, y=None):
    per = CHUNK // 128
    temper = scalars_ref[0:1, 0:1]
    offset = scalars_ref[1:2, 0:1]
    sums, cot = None, None
    for first in range(0, text_ref.shape[0], per):
        text = text_ref[first : first + per].reshape(CHUNK, text_ref.shape[2])
        positive = None
        if y is not None:
            rows = lax.broadcasted_iota(jnp.int32, (128, CHUNK), 0)
            cols = lax.broadcasted_iota(jnp.int32, (128, CHUNK), 1)
            positive = cols + first * 128 == rows + y * 128
        coef, terms = pair_chunk(image, text, temper, offset, positive)
        half = coef.astype(BF16)
        coef_ref[:, first * 128 : first * 128 + CHUNK] = half
        part = jnp.dot(half, text, preferred_element_type=F32)
        cot = part if cot is None else cot + part
        sums = terms if sums is None else tuple(a + b for a, b in zip(sums, terms))
    return cot, jnp.concatenate(sums, axis=0)


def own_mine_kernel(scalars_ref, y_ref, image_ref, text_ref, coef_ref, cot_ref, sums_ref, image_out):
    image = unit(image_ref[...])
    image_out[...] = image
    cot_ref[...], sums_ref[...] = pairs(scalars_ref, image, text_ref, coef_ref, y_ref[0])


def own_sib_kernel(
    scalars_ref,
    image_ref,
    mine_ref,
    sib_ref,
    before_cot,
    before_sums,
    coef_ref,
    cot_ref,
    sums_ref,
    mine_out,
    sib_out,
):
    mine_out[...] = mine_ref[...]
    sib_out[...] = sib_ref[...]
    cot, sums = pairs(scalars_ref, image_ref[...], sib_ref, coef_ref)
    cot_ref[...] = before_cot[...] + cot
    sums_ref[...] = before_sums[...] + sums


def cross_kernel(
    scalars_ref,
    image_ref,
    image_far_ref,
    own_sib,
    mine_ref,
    sib_ref,
    before_sums,
    coef_mine,
    cot_ref,
    sums_ref,
    image_out,
    text_sib,
    coef_sib,
):
    image = unit(image_far_ref[...])
    image_out[...] = image
    cot, sums = pairs(scalars_ref, image, sib_ref, coef_sib)
    for k in range(text_sib.shape[0]):
        text_sib[k] = text_part(own_sib, coef_sib, image_ref, image_out, k).astype(BF16)
    more_cot, more_sums = pairs(scalars_ref, image, mine_ref, coef_mine)
    cot_ref[...] = (cot + more_cot).astype(BF16)
    sums_ref[...] = before_sums[...] + sums + more_sums


def text_part(own_ref, cross_ref, image_ref, image_far_ref, block):
    cols = pl.ds(pl.multiple_of(block * 128, 128), 128)
    dims = (((0,), (0,)), ((), ()))
    return lax.dot_general(own_ref[:, cols], image_ref[...], dims, preferred_element_type=F32) + lax.dot_general(
        cross_ref[:, cols], image_far_ref[...], dims, preferred_element_type=F32
    )


def text_mine_kernel(y_ref, own_ref, cross_ref, image_ref, image_far_ref, got_ref, sums_ref, spread_ref, *out_refs):
    spread_ref[...] = jnp.broadcast_to(sums_ref[...][None], spread_ref.shape)
    count = len(out_refs)
    for k in range(count):
        block = lax.rem(y_ref[0] + k, count)
        total = text_part(own_ref, cross_ref, image_ref, image_far_ref, block) + got_ref[block].astype(F32)
        out_refs[k][...] = total.astype(out_refs[k].dtype)


def sum_kernel(near_ref, spread_ref):
    near = jnp.sum(near_ref[...], axis=0)
    lane = lax.broadcasted_iota(jnp.int32, (1, 128), 1)
    row = jnp.zeros((1, 128), F32)
    for k in range(3):
        row = row + jnp.where(lane == k, jnp.sum(near[k * 8 : (k + 1) * 8]), 0.0)
    spread_ref[...] = jnp.broadcast_to(row[None], spread_ref.shape)


def pull(embeds, cot, temper):
    floats = embeds.astype(F32)
    cot = temper * cot
    inverse = lax.rsqrt(jnp.sum(floats * floats, axis=1, keepdims=True) + EPSILON)
    along = jnp.sum(cot * floats, axis=1, keepdims=True)
    return (inverse * cot - (inverse * inverse * inverse * along) * floats).astype(BF16)


def grad_kernel(scalars_ref, embeds_ref, cot_ref, *refs):
    cot = cot_ref[...]
    for got_ref in refs[:-1]:
        cot = cot + got_ref[...].astype(F32)
    refs[-1][...] = pull(embeds_ref[...], cot, scalars_ref[0:1, 0:1])


def last_kernel(batch, scalars_ref, embeds_ref, cot_ref, got_ref, totals_ref, grad_ref, loss_ref, scale_grad, bias_grad):
    grad_kernel(scalars_ref, embeds_ref, cot_ref, got_ref, grad_ref)
    totals = jnp.sum(totals_ref[...], axis=0)
    lane = lax.broadcasted_iota(jnp.int32, (1, 128), 1)
    loss, scale, bias = (jnp.sum(jnp.where(lane == k, totals, 0.0)) for k in range(3))
    loss_ref[0] = loss / batch
    scale_grad[0] = scale
    bias_grad[0] = bias


def region(body, inside, *args):
    outs = jax.eval_shape(body, *args)
    return lax.cond(inside, body, lambda *_: jax.tree.map(lambda o: jnp.zeros(o.shape, o.dtype), outs), *args)


def on_device(image_embeds, text_embeds, log_scale, logit_bias):
    rows, width = image_embeds.shape
    y_count = lax.axis_size("y")
    y = jnp.reshape(lax.axis_index("y"), (1,))
    inside = y[0] < y_count
    block, blocks = (rows, width), (y_count, rows, width)
    half = (rows, y_count * rows)

    image_far = lax.ppermute(image_embeds, "zh", SWAP)
    text, scalars = call(
        first_kernel,
        [(blocks, BF16), ((8, 128), F32)],
        [HBM, HBM, VMEM],
        (log_scale, logit_bias, text_embeds),
        [pltpu.SMEM((1,), F32), pltpu.SMEM((1,), F32), pltpu.SemaphoreType.DMA((2,))],
    )

    def own_pairs(text, image_embeds, scalars, y):
        mine = lax.all_to_all(text, "y", 0, 0, tiled=True)
        sib = lax.ppermute(mine, "c", SWAP)
        coef, cot, sums, image = call(
            own_mine_kernel,
            [(half, BF16), (block, F32), ((24, 128), F32), (block, BF16)],
            [VMEM, SMEM, VMEM, VMEM],
            (scalars, y, image_embeds, mine),
        )
        return mine, sib, coef, cot, sums, image

    mine, sib, own_mine, image_cot, sums, image = region(
        own_pairs, inside, text, image_embeds, scalars, y
    )
    own_sib, image_cot, sums, mine, sib = call(
        own_sib_kernel,
        [(half, BF16), (block, F32), ((24, 128), F32), (blocks, BF16), (blocks, BF16)],
        [VMEM] * 6,
        (scalars, image, mine, sib, image_cot, sums),
    )
    far_mine, far_cot, sums, image_far, text_sib = call(
        cross_kernel,
        [(half, BF16), (block, BF16), ((24, 128), F32), (block, BF16), (blocks, BF16)],
        [VMEM] * 7,
        (scalars, image, image_far, own_sib, mine, sib, sums),
        [pltpu.VMEM(half, BF16)],
    )
    far_got = lax.ppermute(far_cot, "zh", SWAP)

    text_got = lax.ppermute(text_sib, "c", SWAP)

    def text_side(own_mine, far_mine, image, image_far, text_got, y, sums, text_embeds, scalars):
        near_axes = ("y", "c", "x")
        spread, text_kept, *text_send = call(
            text_mine_kernel,
            [((lax.axis_size(near_axes), 24, 128), F32), (block, F32)] + [(block, BF16)] * (y_count - 1),
            [SMEM] + [VMEM] * 6,
            (y, own_mine, far_mine, image, image_far, text_got, sums),
        )
        near = lax.all_to_all(spread, near_axes, 0, 0, tiled=True)
        got = [
            lax.ppermute(part, "y", [(i, (i + k) % y_count) for i in range(y_count)])
            for k, part in enumerate(text_send, 1)
        ]
        z_axes = ("zh", "zl")
        (spread,) = call(sum_kernel, [((lax.axis_size(z_axes), 1, 128), F32)], [VMEM], (near,))
        totals = lax.all_to_all(spread, z_axes, 0, 0, tiled=True)
        (text_grad,) = call(
            grad_kernel,
            [(block, BF16)],
            [VMEM] * (3 + len(got)),
            (scalars, text_embeds, text_kept, *got),
        )
        return text_grad, totals

    text_grad, totals = region(
        text_side,
        inside,
        own_mine,
        far_mine,
        image,
        image_far,
        text_got,
        y,
        sums,
        text_embeds,
        scalars,
    )
    image_grad, loss, scale_grad, bias_grad = call(
        functools.partial(last_kernel, rows * lax.axis_size(AXES)),
        [(block, BF16)] + [((1,), F32)] * 3,
        [VMEM] * 5,
        (scalars, image_embeds, image_cot, far_got, totals),
        out_specs=[VMEM] + [SMEM] * 3,
    )
    return loss, image_grad, text_grad, scale_grad, bias_grad


def solution(mesh):
    fine = Mesh(mesh.devices.reshape(SIZES), AXES)
    return jax.shard_map(
        on_device,
        mesh=fine,
        in_specs=(P(AXES, None), P(AXES, None), P(), P()),
        out_specs=(P(), P(AXES, None), P(AXES, None), P(), P()),
        check_vma=False,
    )
```

time: 103 us -> 101 us (0.981)
  waiting for transfers between devices: 12 us -> 10.1 us
    ppermute x1, waiting for transfers between devices: 2.79 us -> 0.46 us  [own_pairs(): sib = lax.ppermute(mine, 'c', SWAP)]
  transfers between devices with their start and end apart: 9 -> 9, of which waited for: 3 -> 3; matrix products, arithmetic and copies ran while one was open for 0% -> 0% of each run, Pallas kernels for 10% -> 11%
where the time goes in v5:
time: 101 us; the launch traced here: 98.9 us
  starting transfers between devices  52.1 us (52%)
  blocking collectives  19.2 us (19%)
  Pallas kernels  15.3 us (15%)
  waiting for transfers between devices  10.1 us (10%)
  between operations  1.98 us (2%)
    all_to_all x1, blocking collectives, own_pairs(): mine = lax.all_to_all(text, 'y', 0, 0, tiled=True)  19.2 us
    ppermute x1, starting transfers between devices, on_device(): image_far = lax.ppermute(image_embeds, 'zh', SWAP)  16.3 us
    pallas_call x8, Pallas kernels, call(): pl.pallas_call(kernel, out_shape=[jax.ShapeDtypeStruct(shape, dtype) for...  15.3 us
    all_to_all x1, starting transfers between devices, text_side(): totals = lax.all_to_all(spread, z_axes, 0, 0, tiled=True)  11.2 us
    ppermute x3, starting transfers between devices, text_side(): lax.ppermute(part, 'y', [(i, (i + k) % y_count) for i in range(y_count)])  10.7 us
    all_to_all x1, waiting for transfers between devices, text_side(): totals = lax.all_to_all(spread, z_axes, 0, 0, tiled=True)  9.13 us
    all_to_all x1, starting transfers between devices, text_side(): near = lax.all_to_all(spread, near_axes, 0, 0, tiled=True)  5.44 us
    ppermute x1, starting transfers between devices, own_pairs(): sib = lax.ppermute(mine, 'c', SWAP)  4.35 us
  transfers between devices with their start and end apart: 9, of which 3 were waited for; matrix products, arithmetic and copies ran while one was open for 0% of the time, Pallas kernels for 11%

profile of v5, /device:TPU:1, one launch (start us, length us, event | category | flops | bytes accessed | tf_op | source)
XLA Modules:
  0.0 98.9 jit_solution(467844022009482166)
XLA Ops:
  0.6 16.3 %collective-permute-start.4 = (bf16[128,1152]{1,0:T(8,128)(2,1)}, bf16[128,1152]{1,0:T(8,128)(2,1)S(1)}, u32[]{:S(2)}, u32[]{:S(2)}) collective-permute-start(bf16[128,1152]{1,0:T(8,128)(2,1)} %embeds_ref.1), channel_id=1, source_target_pairs={{0,256},{256,0},{1,257},{257,1},{2,258},{258,2},{3,259},{259,3},{4... | collective-permute-start | bytes 884744 | tf_op jit(solution)/shard_map/ppermute | solution.py:214
  18.2 1.5 %shard_map.83 = (bf16[4,128,1152]{2,1,0:T(8,128)(2,1)S(1)}, f32[8,128]{1,0:T(8,128)S(1)}) custom-call(f32[1]{0:T(128)S(6)} %copy.25.scale_ref, f32[1]{0:T(128)S(6)} %copy.26.bias_ref, bf16[128,1152]{1,0:T(8,128)(2,1)} %text_ref.1), custom_call_target="tpu_custom_call" | custom-call | tf_op jit(solution)/shard_map/pallas_call | solution.py:25
  19.8 26.4 %conditional.2 = (bf16[4,128,1152]{2,1,0:T(8,128)(2,1)}, bf16[4,128,1152]{2,1,0:T(8,128)(2,1)}, bf16[128,512]{1,0:T(8,128)(2,1)S(1)}, f32[128,1152]{1,0:T(8,128)...) conditional(s32[]{:T(128)} %convert_element_type.4, () %tuple.24, ...), branch_computations={%region_0.0_spmd, %region_1.0_spmd} | conditional | bytes 8257652 | solution.py:203
  19.8 0.0 copy-start
  19.8 19.2 %all_to_all.12.text_ref = bf16[4,128,1152]{2,1,0:T(8,128)(2,1)} all-to-all(bf16[4,128,1152]{2,1,0:T(8,128)(2,1)S(1)} %get-tuple-element.26), channel_id=1, replica_groups=mesh['zh'=2,'y'=4,'c'=2,'zl'=8,'x'=4] {'y'}, dimensions={0} | all-to-all | bytes 2359296 | tf_op jit(solution)/shard_map/cond/branch_1_fun/all_to_all | solution.py:224
  39.0 4.4 %collective-permute-start = (bf16[4,128,1152]{2,1,0:T(8,128)(2,1)}, bf16[4,128,1152]{2,1,0:T(8,128)(2,1)}, u32[]{:S(2)}, u32[]{:S(2)}) collective-permute-start(bf16[4,128,1152]{2,1,0:T(8,128)(2,1)} %all_to_all.12.text_ref), channel_id=1, source_target_pairs={{0,32},{32,0},{1,33},{33,1},{2,34},{34,2},{3,35},{35,3},{4,36},{36... | collective-permute-start | bytes 3538952 | tf_op jit(solution)/shard_map/cond/branch_1_fun/ppermute | solution.py:225
  43.4 0.0 copy-done
  43.4 2.3 %branch_1_fun.4 = (bf16[128,512]{1,0:T(8,128)(2,1)S(1)}, f32[128,1152]{1,0:T(8,128)S(1)}, f32[24,128]{1,0:T(8,128)S(1)}, bf16[128,1152]{1,0:T(8,128)(2,1)S(1)}) custom-call(f32[8,128]{1,0:T(8,128)S(1)} %get-tuple-element.27.scalars_ref, s32[1]{0:T(128)} %get-tuple-element.28.y_ref, bf16[128,1152]{1,0:T(8,128)(2,1)S(1)} %copy-done, ...), custom_call_target="tpu_custom_call" | custom-call | tf_op jit(solution)/shard_map/cond/branch_1_fun/pallas_call | solution.py:25
  45.7 0.5 collective-permute-done
  46.2 2.7 %shard_map.84 = (bf16[128,512]{1,0:T(8,128)(2,1)S(1)}, f32[128,1152]{1,0:T(8,128)S(1)}, f32[24,128]{1,0:T(8,128)S(1)}, bf16[4,128,1152]{2,1,0:T(8,128)(2,1)S(1)}, bf16[4,128,1152]{2,1,0:T(8,128)(2,1)S(1)}) custom-call(f32[8,128]{1,0:T(8,128)S(1)} %get-tuple-element.77.scalars_ref, bf16[128,1152]{1,0:T(8,128)(2,1)S(1)} %get-tuple-element.79.image_ref, ...), custom_call_target="tpu_custom_call" | custom-call | tf_op jit(solution)/shard_map/pallas_call | solution.py:25
  48.9 0.0 collective-permute-done.4.image_far_ref
  48.9 2.5 %shard_map.85 = (bf16[128,512]{1,0:T(8,128)(2,1)S(1)}, bf16[128,1152]{1,0:T(8,128)(2,1)S(1)}, f32[24,128]{1,0:T(8,128)S(1)}, bf16[128,1152]{1,0:T(8,128)(2,1)S(1)}, bf16[4,128,1152]{2,1,0:T(8,128)(2,1)S(1)}) custom-call(f32[8,128]{1,0:T(8,128)S(1)} %get-tuple-element.77.scalars_ref, bf16[128,1152]{1,0:T(8,128)(2,1)S(1)} %get-tuple-element.79.image_ref, ...), custom_call_target="tpu_custom_call" | custom-call | tf_op jit(solution)/shard_map/pallas_call | solution.py:25
  51.3 2.3 %collective-permute-start.6 = (bf16[4,128,1152]{2,1,0:T(8,128)(2,1)S(1)}, bf16[4,128,1152]{2,1,0:T(8,128)(2,1)S(1)}, u32[]{:S(2)}, u32[]{:S(2)}) collective-permute-start(bf16[4,128,1152]{2,1,0:T(8,128)(2,1)S(1)} %get-tuple-element.93), channel_id=1, source_target_pairs={{0,32},{32,0},{1,33},{33,1},{2,34},{34,2},{3,35},{35,3},{4,36},{36... | collective-permute-start | bytes 3538952 | tf_op jit(solution)/shard_map/ppermute | solution.py:252
  53.6 1.9 %collective-permute-start.5 = (bf16[128,1152]{1,0:T(8,128)(2,1)S(1)}, bf16[128,1152]{1,0:T(8,128)(2,1)S(1)}, u32[]{:S(2)}, u32[]{:S(2)}) collective-permute-start(bf16[128,1152]{1,0:T(8,128)(2,1)S(1)} %get-tuple-element.89), channel_id=1, source_target_pairs={{0,256},{256,0},{1,257},{257,1},{2,258},{258,2},{3,259},{259,3},{4... | collective-permute-start | bytes 884744 | tf_op jit(solution)/shard_map/ppermute | solution.py:250
  55.6 0.5 collective-permute-done.6
  56.1 40.8 %conditional.3 = (bf16[128,1152]{1,0:T(8,128)(2,1)}, f32[16,1,128]{2,1,0:T(1,128)}) conditional(s32[]{:T(128)} %convert_element_type.4, () %tuple.26, (s32[1]{0:T(128)}, bf16[128,512]{1,0:T(8,128)(2,1)S(1)}, bf16[128,512]{1,0:T(8,128)(2,1)S(1)}, bf16[128,1152]{1,0:T(8,128)(2,1)S(1)}, bf16[128,1152]{1,0:T(8,128)(2,1)S(1)}, ...), branch_computations={%region_2.0_spmd, %region_3.0_spmd} | conditional | bytes 4743368 | solution.py:203
  56.1 1.6 %branch_1_fun.5 = (f32[32,24,128]{2,1,0:T(8,128)}, f32[128,1152]{1,0:T(8,128)S(1)}, bf16[128,1152]{1,0:T(8,128)(2,1)}, bf16[128,1152]{1,0:T(8,128)(2,1)}, bf16[128,1152]{1,0:T(8,128)(2,1)S(1)}) custom-call(s32[1]{0:T(128)} %get-tuple-element.36.y_ref, bf16[128,512]{1,0:T(8,128)(2,1)S(1)} %get-tuple-element.37.own_ref, ...), custom_call_target="tpu_custom_call" | custom-call | tf_op jit(solution)/shard_map/cond/branch_1_fun/pallas_call | solution.py:25
  57.7 5.4 %all-to-all-start.1 = ((f32[32,24,128]{2,1,0:T(8,128)}), f32[32,24,128]{2,1,0:T(8,128)S(1)}, u32[]{:S(2)}, u32[]{:S(2)}) async-start(f32[32,24,128]{2,1,0:T(8,128)} %get-tuple-element.47), calls=%async_computation.1 | async-start | bytes 786432 | tf_op jit(solution)/shard_map/cond/branch_1_fun/all_to_all | solution.py:262
  63.1 3.3 %collective-permute-start.1 = (bf16[128,1152]{1,0:T(8,128)(2,1)}, bf16[128,1152]{1,0:T(8,128)(2,1)S(1)}, u32[]{:S(2)}, u32[]{:S(2)}) collective-permute-start(bf16[128,1152]{1,0:T(8,128)(2,1)} %get-tuple-element.44), channel_id=1, source_target_pairs={{0,64},{64,128},{128,192},{192,0},{1,65},{65,129},{129,193},{193,1... | collective-permute-start | bytes 884744 | tf_op jit(solution)/shard_map/cond/branch_1_fun/ppermute | solution.py:264
  66.4 4.4 %collective-permute-start.2 = (bf16[128,1152]{1,0:T(8,128)(2,1)}, bf16[128,1152]{1,0:T(8,128)(2,1)S(1)}, u32[]{:S(2)}, u32[]{:S(2)}) collective-permute-start(bf16[128,1152]{1,0:T(8,128)(2,1)} %get-tuple-element.45), channel_id=1, source_target_pairs={{0,128},{64,192},{128,0},{192,64},{1,129},{65,193},{129,1},{193,65... | collective-permute-start | bytes 884744 | tf_op jit(solution)/shard_map/cond/branch_1_fun/ppermute | solution.py:264
  70.8 3.0 %collective-permute-start.3 = (bf16[128,1152]{1,0:T(8,128)(2,1)S(1)}, bf16[128,1152]{1,0:T(8,128)(2,1)S(1)}, u32[]{:S(2)}, u32[]{:S(2)}) collective-permute-start(bf16[128,1152]{1,0:T(8,128)(2,1)S(1)} %get-tuple-element.46), channel_id=1, source_target_pairs={{0,192},{64,0},{128,64},{192,128},{1,193},{65,1},{129,65},{193,129... | collective-permute-start | bytes 884744 | tf_op jit(solution)/shard_map/cond/branch_1_fun/ppermute | solution.py:264
  73.8 0.0 all-to-all-done.1.near_ref
  73.8 0.8 branch_1_fun.7
  74.6 11.2 %all-to-all-start.2 = ((f32[16,1,128]{2,1,0:T(1,128)}), f32[16,1,128]{2,1,0:T(1,128)}, u32[]{:S(2)}, u32[]{:S(2)}) async-start(f32[16,1,128]{2,1,0:T(1,128)} %branch_1_fun.7), calls=%async_computation.2 | async-start | bytes 16384 | tf_op jit(solution)/shard_map/cond/branch_1_fun/all_to_all | solution.py:269
  85.8 0.0 collective-permute-done.1.refs_0_
  85.8 0.0 collective-permute-done.2.refs_1_
  85.8 0.0 collective-permute-done.3.refs_2_
  85.8 2.0 %branch_1_fun.6 = bf16[128,1152]{1,0:T(8,128)(2,1)} custom-call(f32[8,128]{1,0:T(8,128)S(1)} %get-tuple-element.34.scalars_ref, bf16[128,1152]{1,0:T(8,128)(2,1)} %get-tuple-element.35.embeds_ref, f32[128,1152]{1,0:T(8,128)S(1)} %get-tuple-element.43.cot_ref, bf16[128,1152]{1,0:T(8,128)(2,1)S(1)} %collective-permute-done.1.refs_0_, ...), custom_call_target="tpu_custom_call" | custom-call | tf_op jit(solution)/shard_map/cond/branch_1_fun/pallas_call | solution.py:25
  87.8 9.1 %all-to-all-done.2 = f32[16,1,128]{2,1,0:T(1,128)} async-done(((f32[16,1,128]{2,1,0:T(1,128)}), f32[16,1,128]{2,1,0:T(1,128)}, u32[]{:S(2)}, u32[]{:S(2)}) %all-to-all-start.2) | async-done | bytes 8224 | tf_op jit(solution)/shard_map/cond/branch_1_fun/all_to_all | solution.py:269
  96.9 0.0 collective-permute-done.5.got_ref
  96.9 1.9 %shard_map.86 = (bf16[128,1152]{1,0:T(8,128)(2,1)}, f32[1]{0:T(128)}, f32[1]{0:T(128)}, f32[1]{0:T(128)}) custom-call(f32[8,128]{1,0:T(8,128)S(1)} %get-tuple-element.77.scalars_ref, bf16[128,1152]{1,0:T(8,128)(2,1)} %embeds_ref.1, f32[128,1152]{1,0:T(8,128)S(1)} %get-tuple-element.84.cot_ref, bf16[128,1152]{1,0:T(8,128)(2,1)S(1)} %collective-permute-done.5.got_ref, ...), custom_call_target="tpu_custom_call" | custom-call | tf_op jit(solution)/shard_map/pallas_call | solution.py:25
Async XLA Ops:
  0.6 48.2 %collective-permute-start.4 = (bf16[128,1152]{1,0:T(8,128)(2,1)}, bf16[128,1152]{1,0:T(8,128)(2,1)S(1)}, u32[]{:S(2)}, u32[]{:S(2)}) collective-permute-start(bf16[128,1152]{1,0:T(8,128)(2,1)} %embeds_ref.1), channel_id=1, source_target_pairs={{0,256},{256,0},{1,257},{257,1},{2,258},{258,2},{3,259},{259,3},{4... | collective-permute-start | bytes 884744 | tf_op jit(solution)/shard_map/ppermute | solution.py:214
  19.8 23.6 %copy-start = (bf16[128,1152]{1,0:T(8,128)(2,1)S(1)}, bf16[128,1152]{1,0:T(8,128)(2,1)}, u32[]{:S(2)}) copy-start(bf16[128,1152]{1,0:T(8,128)(2,1)} %get-tuple-element.29.image_ref) | copy-start | bytes 884740 | tf_op jit(solution)/shard_map/cond
  39.0 7.2 %collective-permute-start = (bf16[4,128,1152]{2,1,0:T(8,128)(2,1)}, bf16[4,128,1152]{2,1,0:T(8,128)(2,1)}, u32[]{:S(2)}, u32[]{:S(2)}) collective-permute-start(bf16[4,128,1152]{2,1,0:T(8,128)(2,1)} %all_to_all.12.text_ref), channel_id=1, source_target_pairs={{0,32},{32,0},{1,33},{33,1},{2,34},{34,2},{3,35},{35,3},{4,36},{36... | collective-permute-start | bytes 3538952 | tf_op jit(solution)/shard_map/cond/branch_1_fun/ppermute | solution.py:225
  51.3 4.8 %collective-permute-start.6 = (bf16[4,128,1152]{2,1,0:T(8,128)(2,1)S(1)}, bf16[4,128,1152]{2,1,0:T(8,128)(2,1)S(1)}, u32[]{:S(2)}, u32[]{:S(2)}) collective-permute-start(bf16[4,128,1152]{2,1,0:T(8,128)(2,1)S(1)} %get-tuple-element.93), channel_id=1, source_target_pairs={{0,32},{32,0},{1,33},{33,1},{2,34},{34,2},{3,35},{35,3},{4,36},{36... | collective-permute-start | bytes 3538952 | tf_op jit(solution)/shard_map/ppermute | solution.py:252
  53.6 43.3 %collective-permute-start.5 = (bf16[128,1152]{1,0:T(8,128)(2,1)S(1)}, bf16[128,1152]{1,0:T(8,128)(2,1)S(1)}, u32[]{:S(2)}, u32[]{:S(2)}) collective-permute-start(bf16[128,1152]{1,0:T(8,128)(2,1)S(1)} %get-tuple-element.89), channel_id=1, source_target_pairs={{0,256},{256,0},{1,257},{257,1},{2,258},{258,2},{3,259},{259,3},{4... | collective-permute-start | bytes 884744 | tf_op jit(solution)/shard_map/ppermute | solution.py:250
  57.7 16.2 %all-to-all-start.1 = ((f32[32,24,128]{2,1,0:T(8,128)}), f32[32,24,128]{2,1,0:T(8,128)S(1)}, u32[]{:S(2)}, u32[]{:S(2)}) async-start(f32[32,24,128]{2,1,0:T(8,128)} %get-tuple-element.47), calls=%async_computation.1 | async-start | bytes 786432 | tf_op jit(solution)/shard_map/cond/branch_1_fun/all_to_all | solution.py:262
  63.1 22.6 %collective-permute-start.1 = (bf16[128,1152]{1,0:T(8,128)(2,1)}, bf16[128,1152]{1,0:T(8,128)(2,1)S(1)}, u32[]{:S(2)}, u32[]{:S(2)}) collective-permute-start(bf16[128,1152]{1,0:T(8,128)(2,1)} %get-tuple-element.44), channel_id=1, source_target_pairs={{0,64},{64,128},{128,192},{192,0},{1,65},{65,129},{129,193},{193,1... | collective-permute-start | bytes 884744 | tf_op jit(solution)/shard_map/cond/branch_1_fun/ppermute | solution.py:264
  66.4 19.4 %collective-permute-start.2 = (bf16[128,1152]{1,0:T(8,128)(2,1)}, bf16[128,1152]{1,0:T(8,128)(2,1)S(1)}, u32[]{:S(2)}, u32[]{:S(2)}) collective-permute-start(bf16[128,1152]{1,0:T(8,128)(2,1)} %get-tuple-element.45), channel_id=1, source_target_pairs={{0,128},{64,192},{128,0},{192,64},{1,129},{65,193},{129,1},{193,65... | collective-permute-start | bytes 884744 | tf_op jit(solution)/shard_map/cond/branch_1_fun/ppermute | solution.py:264
  70.8 15.0 %collective-permute-start.3 = (bf16[128,1152]{1,0:T(8,128)(2,1)S(1)}, bf16[128,1152]{1,0:T(8,128)(2,1)S(1)}, u32[]{:S(2)}, u32[]{:S(2)}) collective-permute-start(bf16[128,1152]{1,0:T(8,128)(2,1)S(1)} %get-tuple-element.46), channel_id=1, source_target_pairs={{0,192},{64,0},{128,64},{192,128},{1,193},{65,1},{129,65},{193,129... | collective-permute-start | bytes 884744 | tf_op jit(solution)/shard_map/cond/branch_1_fun/ppermute | solution.py:264
  74.6 22.3 %all-to-all-start.2 = ((f32[16,1,128]{2,1,0:T(1,128)}), f32[16,1,128]{2,1,0:T(1,128)}, u32[]{:S(2)}, u32[]{:S(2)}) async-start(f32[16,1,128]{2,1,0:T(1,128)} %branch_1_fun.7), calls=%async_computation.2 | async-start | bytes 16384 | tf_op jit(solution)/shard_map/cond/branch_1_fun/all_to_all | solution.py:269

commit v6 on v5

--- a/solution.py
+++ b/solution.py
@@ -15,10 +15,10 @@
 
 VMEM = pl.BlockSpec(memory_space=pltpu.VMEM)
 SMEM = pl.BlockSpec(memory_space=pltpu.SMEM)
-HBM = pl.BlockSpec(memory_space=pltpu.HBM)
 PARAMS = pltpu.CompilerParams(vmem_limit_bytes=16 * 1024 * 1024)
 SWAP = ((0, 1), (1, 0))
 CHUNK = 256
+PART = 16
 
 
 def call(kernel, outs, in_specs, args, scratch=(), out_specs=None):
@@ -37,27 +37,34 @@
     return (floats * lax.rsqrt(jnp.sum(floats * floats, axis=1, keepdims=True) + EPSILON)).astype(BF16)
 
 
-def first_kernel(scale_ref, bias_ref, text_ref, text_out, scalars_ref, scale, bias, sems):
-    copies = [
-        pltpu.make_async_copy(scale_ref, scale, sems.at[0]),
-        pltpu.make_async_copy(bias_ref, bias, sems.at[1]),
-    ]
-    for copy in copies:
-        copy.start()
-    rows = unit(text_ref[...])
-    for k in range(text_out.shape[0]):
-        text_out[k] = rows
-    for copy in copies:
-        copy.wait()
+def norm_kernel(matrix_ref, out_ref):
+    rows = unit(matrix_ref[...])
+    for k in range(out_ref.shape[0]):
+        out_ref[k] = rows
+
+
+def scalars_kernel(scale_ref, bias_ref, scalars_ref):
     row = lax.broadcasted_iota(jnp.int32, scalars_ref.shape, 0)
-    temper = jnp.exp(jnp.full(scalars_ref.shape, scale[0], F32))
-    scalars_ref[...] = jnp.where(row == 0, temper, bias[0])
+    temper = jnp.exp(jnp.full(scalars_ref.shape, scale_ref[0], F32))
+    scalars_ref[...] = jnp.where(row == 0, temper, bias_ref[0])
+
+
+def lanes(values):
+    return sum(values[:, k * 128 : (k + 1) * 128] for k in range(values.shape[1] // 128))
 
 
 def fold(values):
     rows, cols = values.shape
-    total = jnp.sum(values.reshape(rows // 8, 8, cols), axis=0)
-    return sum(total[:, k * 128 : (k + 1) * 128] for k in range(cols // 128))
+    return lanes(jnp.sum(values.reshape(rows // PART, PART, cols), axis=0))
+
+
+def fold_logs(values):
+    rows, cols = values.shape
+    parts = values.reshape(rows // PART, PART, cols)
+    while parts.shape[0] > 1:
+        middle = parts.shape[0] // 2
+        parts = parts[:middle] * parts[middle:]
+    return lanes(jnp.log(parts[0]))
 
 
 def pair_chunk(image, text, temper, offset, positive):
@@ -71,11 +78,11 @@
     if positive is not None:
         coef = coef - jnp.where(positive, 1.0, 0.0)
         signed = jnp.where(positive, -logits, logits)
-    losses = jnp.maximum(signed, 0.0) + jnp.log1p(small)
-    return coef, (fold(losses), fold(coef * scaled), fold(coef))
-
-
-def pairs(scalars_ref, image, text_ref, coef_ref, y=None):
+    loss = fold(jnp.maximum(signed, 0.0)) + fold_logs(1.0 + small)
+    return coef, (loss, fold(coef * scaled), fold(coef))
+
+
+def pairs(scalars_ref, image, text_ref, coef_ref, y=None, pull_back=True):
     per = CHUNK // 128
     temper = scalars_ref[0:1, 0:1]
     offset = scalars_ref[1:2, 0:1]
@@ -90,35 +97,44 @@
         coef, terms = pair_chunk(image, text, temper, offset, positive)
         half = coef.astype(BF16)
         coef_ref[:, first * 128 : first * 128 + CHUNK] = half
-        part = jnp.dot(half, text, preferred_element_type=F32)
-        cot = part if cot is None else cot + part
+        if pull_back:
+            part = jnp.dot(half, text, preferred_element_type=F32)
+            cot = part if cot is None else cot + part
         sums = terms if sums is None else tuple(a + b for a, b in zip(sums, terms))
     return cot, jnp.concatenate(sums, axis=0)
 
 
-def own_mine_kernel(scalars_ref, y_ref, image_ref, text_ref, coef_ref, cot_ref, sums_ref, image_out):
+def own_mine_kernel(
+    scalars_ref, y_ref, image_ref, text_ref, coef_ref, sums_ref, image_out, text_out
+):
+    text_out[...] = text_ref[...]
     image = unit(image_ref[...])
     image_out[...] = image
-    cot_ref[...], sums_ref[...] = pairs(scalars_ref, image, text_ref, coef_ref, y_ref[0])
+    _, sums_ref[...] = pairs(scalars_ref, image, text_ref, coef_ref, y_ref[0], False)
 
 
 def own_sib_kernel(
     scalars_ref,
     image_ref,
+    sib_ref,
     mine_ref,
-    sib_ref,
-    before_cot,
+    coef_mine,
     before_sums,
     coef_ref,
     cot_ref,
     sums_ref,
-    mine_out,
     sib_out,
+    scalars_out,
 ):
-    mine_out[...] = mine_ref[...]
+    scalars_out[...] = scalars_ref[...]
     sib_out[...] = sib_ref[...]
     cot, sums = pairs(scalars_ref, image_ref[...], sib_ref, coef_ref)
-    cot_ref[...] = before_cot[...] + cot
+    per = CHUNK // 128
+    for first in range(0, mine_ref.shape[0], per):
+        text = mine_ref[first : first + per].reshape(CHUNK, mine_ref.shape[2])
+        half = coef_mine[:, first * 128 : first * 128 + CHUNK]
+        cot = cot + jnp.dot(half, text, preferred_element_type=F32)
+    cot_ref[...] = cot
     sums_ref[...] = before_sums[...] + sums
 
 
@@ -140,11 +156,19 @@
     image = unit(image_far_ref[...])
     image_out[...] = image
     cot, sums = pairs(scalars_ref, image, sib_ref, coef_sib)
-    for k in range(text_sib.shape[0]):
-        text_sib[k] = text_part(own_sib, coef_sib, image_ref, image_out, k).astype(BF16)
+    count = text_sib.shape[0] // 128
+    for k in range(count):
+        text_sib[k * 128 : (k + 1) * 128] = text_part(own_sib, coef_sib, image_ref, image_out, k).astype(BF16)
     more_cot, more_sums = pairs(scalars_ref, image, mine_ref, coef_mine)
     cot_ref[...] = (cot + more_cot).astype(BF16)
-    sums_ref[...] = before_sums[...] + sums + more_sums
+    rest = before_sums[...] + sums + more_sums
+    sums_ref[...] = rest
+    for term in range(3):
+        value = rest.astype(BF16)
+        rest = rest - value.astype(F32)
+        for k in range(3):
+            at = (term * 3 + k) * 128
+            text_sib[count * 128 :, at : at + 128] = value[k * PART : (k + 1) * PART]
 
 
 def text_part(own_ref, cross_ref, image_ref, image_far_ref, block):
@@ -156,11 +180,17 @@
 
 
 def text_mine_kernel(y_ref, own_ref, cross_ref, image_ref, image_far_ref, got_ref, sums_ref, spread_ref, *out_refs):
-    spread_ref[...] = jnp.broadcast_to(sums_ref[...][None], spread_ref.shape)
     count = len(out_refs)
+    for k in range(3):
+        total = sums_ref[k * PART : (k + 1) * PART]
+        for term in range(3):
+            at = (term * 3 + k) * 128
+            total = total + got_ref[count * 128 :, at : at + 128].astype(F32)
+        for peer in range(spread_ref.shape[0]):
+            spread_ref[peer, k * PART : (k + 1) * PART] = total
     for k in range(count):
         block = lax.rem(y_ref[0] + k, count)
-        total = text_part(own_ref, cross_ref, image_ref, image_far_ref, block) + got_ref[block].astype(F32)
+        total = text_part(own_ref, cross_ref, image_ref, image_far_ref, block) + got_ref[pl.ds(pl.multiple_of(block * 128, 128), 128), :].astype(F32)
         out_refs[k][...] = total.astype(out_refs[k].dtype)
 
 
@@ -169,7 +199,7 @@
     lane = lax.broadcasted_iota(jnp.int32, (1, 128), 1)
     row = jnp.zeros((1, 128), F32)
     for k in range(3):
-        row = row + jnp.where(lane == k, jnp.sum(near[k * 8 : (k + 1) * 8]), 0.0)
+        row = row + jnp.where(lane == k, jnp.sum(near[k * PART : (k + 1) * PART]), 0.0)
     spread_ref[...] = jnp.broadcast_to(row[None], spread_ref.shape)
 
 
@@ -212,37 +242,37 @@
     half = (rows, y_count * rows)
 
     image_far = lax.ppermute(image_embeds, "zh", SWAP)
-    text, scalars = call(
-        first_kernel,
-        [(blocks, BF16), ((8, 128), F32)],
-        [HBM, HBM, VMEM],
-        (log_scale, logit_bias, text_embeds),
-        [pltpu.SMEM((1,), F32), pltpu.SMEM((1,), F32), pltpu.SemaphoreType.DMA((2,))],
-    )
-
-    def own_pairs(text, image_embeds, scalars, y):
+    def own_pairs(text_embeds, image_embeds, log_scale, logit_bias, y):
+        (text,) = call(norm_kernel, [(blocks, BF16)], [VMEM], (text_embeds,))
+        (scalars,) = call(scalars_kernel, [((8, 128), F32)], [SMEM] * 2, (log_scale, logit_bias))
         mine = lax.all_to_all(text, "y", 0, 0, tiled=True)
         sib = lax.ppermute(mine, "c", SWAP)
-        coef, cot, sums, image = call(
+        coef, sums, image, mine = call(
             own_mine_kernel,
-            [(half, BF16), (block, F32), ((24, 128), F32), (block, BF16)],
+            [(half, BF16), ((3 * PART, 128), F32), (block, BF16), (blocks, BF16)],
             [VMEM, SMEM, VMEM, VMEM],
             (scalars, y, image_embeds, mine),
         )
-        return mine, sib, coef, cot, sums, image
-
-    mine, sib, own_mine, image_cot, sums, image = region(
-        own_pairs, inside, text, image_embeds, scalars, y
-    )
-    own_sib, image_cot, sums, mine, sib = call(
+        return mine, sib, coef, sums, image, scalars
+
+    mine, sib, own_mine, sums, image, scalars = region(
+        own_pairs, inside, text_embeds, image_embeds, log_scale, logit_bias, y
+    )
+    own_sib, image_cot, sums, sib, scalars = call(
         own_sib_kernel,
-        [(half, BF16), (block, F32), ((24, 128), F32), (blocks, BF16), (blocks, BF16)],
+        [(half, BF16), (block, F32), ((3 * PART, 128), F32), (blocks, BF16), ((8, 128), F32)],
         [VMEM] * 6,
-        (scalars, image, mine, sib, image_cot, sums),
+        (scalars, image, sib, mine, own_mine, sums),
     )
     far_mine, far_cot, sums, image_far, text_sib = call(
         cross_kernel,
-        [(half, BF16), (block, BF16), ((24, 128), F32), (block, BF16), (blocks, BF16)],
+        [
+            (half, BF16),
+            (block, BF16),
+            ((3 * PART, 128), F32),
+            (block, BF16),
+            ((y_count * rows + PART, width), BF16),
+        ],
         [VMEM] * 7,
         (scalars, image, image_far, own_sib, mine, sib, sums),
         [pltpu.VMEM(half, BF16)],
@@ -252,10 +282,10 @@
     text_got = lax.ppermute(text_sib, "c", SWAP)
 
     def text_side(own_mine, far_mine, image, image_far, text_got, y, sums, text_embeds, scalars):
-        near_axes = ("y", "c", "x")
+        near_axes = ("y", "x")
         spread, text_kept, *text_send = call(
             text_mine_kernel,
-            [((lax.axis_size(near_axes), 24, 128), F32), (block, F32)] + [(block, BF16)] * (y_count - 1),
+            [((lax.axis_size(near_axes), 3 * PART, 128), F32), (block, F32)] + [(block, BF16)] * (y_count - 1),
             [SMEM] + [VMEM] * 6,
             (y, own_mine, far_mine, image, image_far, text_got, sums),
         )

time: 101 us -> 100 us (0.990)
  the two profiles are of different devices: /device:TPU:1 before, /device:TPU:2 now
where the time goes in v6:
time: 100 us; the launch traced here: 99.4 us
  starting transfers between devices  51.8 us (52%)
  blocking collectives  20.6 us (21%)
  Pallas kernels  15.6 us (16%)
  waiting for transfers between devices  10.6 us (11%)
    all_to_all x1, blocking collectives, own_pairs(): mine = lax.all_to_all(text, 'y', 0, 0, tiled=True)  20.6 us
    ppermute x1, starting transfers between devices, on_device(): image_far = lax.ppermute(image_embeds, 'zh', SWAP)  15.7 us
    pallas_call x9, Pallas kernels, call(): pl.pallas_call(kernel, out_shape=[jax.ShapeDtypeStruct(shape, dtype) for...  15.6 us
    all_to_all x1, starting transfers between devices, text_side(): totals = lax.all_to_all(spread, z_axes, 0, 0, tiled=True)  12.8 us
    ppermute x3, starting transfers between devices, text_side(): lax.ppermute(part, 'y', [(i, (i + k) % y_count) for i in range(y_count)])  11.3 us
    all_to_all x1, waiting for transfers between devices, text_side(): totals = lax.all_to_all(spread, z_axes, 0, 0, tiled=True)  10.3 us
    all_to_all x1, starting transfers between devices, text_side(): near = lax.all_to_all(spread, near_axes, 0, 0, tiled=True)  5.47 us
    ppermute x1, starting transfers between devices, on_device(): text_got = lax.ppermute(text_sib, 'c', SWAP)  2.4 us
  transfers between devices with their start and end apart: 9, of which 2 were waited for; matrix products, arithmetic and copies ran while one was open for 0% of the time, Pallas kernels for 11%

profile of v6, /device:TPU:2, one launch (start us, length us, event | category | flops | bytes accessed | tf_op | source)
XLA Modules:
  0.0 99.4 jit_solution(6834298744670592119)
XLA Ops:
  0.6 15.7 %collective-permute-start.4 = (bf16[128,1152]{1,0:T(8,128)(2,1)}, bf16[128,1152]{1,0:T(8,128)(2,1)S(1)}, u32[]{:S(2)}, u32[]{:S(2)}) collective-permute-start(bf16[128,1152]{1,0:T(8,128)(2,1)} %embeds_ref.1), channel_id=1, source_target_pairs={{0,256},{256,0},{1,257},{257,1},{2,258},{258,2},{3,259},{259,3},{4... | collective-permute-start | bytes 884744 | tf_op jit(solution)/shard_map/ppermute | solution.py:244
  16.4 27.1 %conditional.2 = (bf16[4,128,1152]{2,1,0:T(8,128)(2,1)S(1)}, bf16[4,128,1152]{2,1,0:T(8,128)(2,1)}, bf16[128,512]{1,0:T(8,128)(2,1)S(1)}, f32[48,128]{1,0:T(8,12...) conditional(s32[]{:T(128)} %convert_element_type.4, () %tuple.24, (f32[1]{0:T(128)}, f32[1]{0:T(128)}, ...), branch_computations={%region_0.0_spmd, %region_1.0_spmd} | conditional | bytes 8257652 | solution.py:233
  16.4 1.1 %branch_1_fun.7 = bf16[4,128,1152]{2,1,0:T(8,128)(2,1)S(1)} custom-call(bf16[128,1152]{1,0:T(8,128)(2,1)} %get-tuple-element.32.matrix_ref), custom_call_target="tpu_custom_call" | custom-call | tf_op jit(solution)/shard_map/cond/branch_1_fun/pallas_call | solution.py:25
  17.5 0.0 copy-start
  17.5 20.6 %all_to_all.12.text_ref = bf16[4,128,1152]{2,1,0:T(8,128)(2,1)S(1)} all-to-all(bf16[4,128,1152]{2,1,0:T(8,128)(2,1)S(1)} %branch_1_fun.7), channel_id=1, replica_groups=mesh['zh'=2,'y'=4,'c'=2,'zl'=8,'x'=4] {'y'}, dimensions={0} | all-to-all | bytes 2359296 | tf_op jit(solution)/shard_map/cond/branch_1_fun/all_to_all | solution.py:248
  38.1 1.9 %collective-permute-start = (bf16[4,128,1152]{2,1,0:T(8,128)(2,1)S(1)}, bf16[4,128,1152]{2,1,0:T(8,128)(2,1)}, u32[]{:S(2)}, u32[]{:S(2)}) collective-permute-start(bf16[4,128,1152]{2,1,0:T(8,128)(2,1)S(1)} %all_to_all.12.text_ref), channel_id=1, source_target_pairs={{0,32},{32,0},{1,33},{33,1},{2,34},{34,2},{3,35},{35,3},{4,36},{36... | collective-permute-start | bytes 3538952 | tf_op jit(solution)/shard_map/cond/branch_1_fun/ppermute | solution.py:249
  40.1 1.9 %branch_1_fun.6.scalars_ref = f32[8,128]{1,0:T(8,128)} custom-call(f32[1]{0:T(128)} %get-tuple-element.102.scale_ref, f32[1]{0:T(128)} %get-tuple-element.103.bias_ref), custom_call_target="tpu_custom_call" | custom-call | tf_op jit(solution)/shard_map/cond/branch_1_fun/pallas_call | solution.py:25
  42.0 0.0 copy-done
  42.0 1.5 %branch_1_fun.8 = (bf16[128,512]{1,0:T(8,128)(2,1)S(1)}, f32[48,128]{1,0:T(8,128)S(1)}, bf16[128,1152]{1,0:T(8,128)(2,1)S(1)}, bf16[4,128,1152]{2,1,0:T(8,128)(2,1)S(1)}) custom-call(f32[8,128]{1,0:T(8,128)} %branch_1_fun.6.scalars_ref, s32[1]{0:T(128)} %get-tuple-element.30.y_ref, bf16[128,1152]{1,0:T(8,128)(2,1)S(1)} %copy-done, ...), custom_call_target="tpu_custom_call" | custom-call | tf_op jit(solution)/shard_map/cond/branch_1_fun/pallas_call | solution.py:25
  43.5 0.0 collective-permute-done
  43.5 2.4 %shard_map.85 = (bf16[128,512]{1,0:T(8,128)(2,1)S(1)}, f32[128,1152]{1,0:T(8,128)S(1)}, f32[48,128]{1,0:T(8,128)S(1)}, bf16[4,128,1152]{2,1,0:T(8,128)(2,1)S(1)}, f32[8,128]{1,0:T(8,128)S(1)}) custom-call(f32[8,128]{1,0:T(8,128)} %get-tuple-element.78.scalars_ref, bf16[128,1152]{1,0:T(8,128)(2,1)S(1)} %get-tuple-element.79.image_ref, ...), custom_call_target="tpu_custom_call" | custom-call | tf_op jit(solution)/shard_map/pallas_call | solution.py:25
  45.9 0.0 collective-permute-done.4.image_far_ref
  45.9 2.4 %shard_map.86 = (bf16[128,512]{1,0:T(8,128)(2,1)S(1)}, bf16[128,1152]{1,0:T(8,128)(2,1)S(1)}, f32[48,128]{1,0:T(8,128)S(1)}, bf16[128,1152]{1,0:T(8,128)(2,1)S(1)}, bf16[528,1152]{1,0:T(8,128)(2,1)S(1)}) custom-call(f32[8,128]{1,0:T(8,128)S(1)} %get-tuple-element.84.scalars_ref, bf16[128,1152]{1,0:T(8,128)(2,1)S(1)} %get-tuple-element.79.image_ref, ...), custom_call_target="tpu_custom_call" | custom-call | tf_op jit(solution)/shard_map/pallas_call | solution.py:25
  48.2 2.4 %collective-permute-start.6 = (bf16[528,1152]{1,0:T(8,128)(2,1)S(1)}, bf16[528,1152]{1,0:T(8,128)(2,1)S(1)}, u32[]{:S(2)}, u32[]{:S(2)}) collective-permute-start(bf16[528,1152]{1,0:T(8,128)(2,1)S(1)} %get-tuple-element.92), channel_id=1, source_target_pairs={{0,32},{32,0},{1,33},{33,1},{2,34},{34,2},{3,35},{35,3},{4,36},{36... | collective-permute-start | bytes 3649544 | tf_op jit(solution)/shard_map/ppermute | solution.py:282
  50.7 2.2 %collective-permute-start.5 = (bf16[128,1152]{1,0:T(8,128)(2,1)S(1)}, bf16[128,1152]{1,0:T(8,128)(2,1)S(1)}, u32[]{:S(2)}, u32[]{:S(2)}) collective-permute-start(bf16[128,1152]{1,0:T(8,128)(2,1)S(1)} %get-tuple-element.89), channel_id=1, source_target_pairs={{0,256},{256,0},{1,257},{257,1},{2,258},{258,2},{3,259},{259,3},{4... | collective-permute-start | bytes 884744 | tf_op jit(solution)/shard_map/ppermute | solution.py:280
  52.9 0.3 collective-permute-done.6
  53.2 44.3 %conditional.3 = (bf16[128,1152]{1,0:T(8,128)(2,1)}, f32[16,1,128]{2,1,0:T(1,128)}) conditional(s32[]{:T(128)} %convert_element_type.4, () %tuple.26, (s32[1]{0:T(128)}, bf16[128,512]{1,0:T(8,128)(2,1)S(1)}, bf16[128,512]{1,0:T(8,128)(2,1)S(1)}, bf16[128,1152]{1,0:T(8,128)(2,1)S(1)}, bf16[128,1152]{1,0:T(8,128)(2,1)S(1)}, ...), branch_computations={%region_2.0_spmd, %region_3.0_spmd} | conditional | bytes 4743368 | solution.py:233
  53.2 1.6 %branch_1_fun.9 = (f32[16,48,128]{2,1,0:T(8,128)}, f32[128,1152]{1,0:T(8,128)S(1)}, bf16[128,1152]{1,0:T(8,128)(2,1)}, bf16[128,1152]{1,0:T(8,128)(2,1)}, bf16[128,1152]{1,0:T(8,128)(2,1)S(1)}) custom-call(s32[1]{0:T(128)} %get-tuple-element.39.y_ref, bf16[128,512]{1,0:T(8,128)(2,1)S(1)} %get-tuple-element.40.own_ref, ...), custom_call_target="tpu_custom_call" | custom-call | tf_op jit(solution)/shard_map/cond/branch_1_fun/pallas_call | solution.py:25
  54.8 5.5 %all-to-all-start.1 = ((f32[16,48,128]{2,1,0:T(8,128)}), f32[16,48,128]{2,1,0:T(8,128)S(1)}, u32[]{:S(2)}, u32[]{:S(2)}) async-start(f32[16,48,128]{2,1,0:T(8,128)} %get-tuple-element.50), calls=%async_computation.1 | async-start | bytes 786432 | tf_op jit(solution)/shard_map/cond/branch_1_fun/all_to_all | solution.py:292
  60.2 3.4 %collective-permute-start.1 = (bf16[128,1152]{1,0:T(8,128)(2,1)}, bf16[128,1152]{1,0:T(8,128)(2,1)S(1)}, u32[]{:S(2)}, u32[]{:S(2)}) collective-permute-start(bf16[128,1152]{1,0:T(8,128)(2,1)} %get-tuple-element.47), channel_id=1, source_target_pairs={{0,64},{64,128},{128,192},{192,0},{1,65},{65,129},{129,193},{193,1... | collective-permute-start | bytes 884744 | tf_op jit(solution)/shard_map/cond/branch_1_fun/ppermute | solution.py:294
  63.6 4.6 %collective-permute-start.2 = (bf16[128,1152]{1,0:T(8,128)(2,1)}, bf16[128,1152]{1,0:T(8,128)(2,1)S(1)}, u32[]{:S(2)}, u32[]{:S(2)}) collective-permute-start(bf16[128,1152]{1,0:T(8,128)(2,1)} %get-tuple-element.48), channel_id=1, source_target_pairs={{0,128},{64,192},{128,0},{192,64},{1,129},{65,193},{129,1},{193,65... | collective-permute-start | bytes 884744 | tf_op jit(solution)/shard_map/cond/branch_1_fun/ppermute | solution.py:294
  68.2 3.4 %collective-permute-start.3 = (bf16[128,1152]{1,0:T(8,128)(2,1)S(1)}, bf16[128,1152]{1,0:T(8,128)(2,1)S(1)}, u32[]{:S(2)}, u32[]{:S(2)}) collective-permute-start(bf16[128,1152]{1,0:T(8,128)(2,1)S(1)} %get-tuple-element.49), channel_id=1, source_target_pairs={{0,192},{64,0},{128,64},{192,128},{1,193},{65,1},{129,65},{193,129... | collective-permute-start | bytes 884744 | tf_op jit(solution)/shard_map/cond/branch_1_fun/ppermute | solution.py:294
  71.6 0.0 all-to-all-done.1.near_ref
  71.6 0.7 branch_1_fun.11
  72.3 12.8 %all-to-all-start.2 = ((f32[16,1,128]{2,1,0:T(1,128)}), f32[16,1,128]{2,1,0:T(1,128)}, u32[]{:S(2)}, u32[]{:S(2)}) async-start(f32[16,1,128]{2,1,0:T(1,128)} %branch_1_fun.11), calls=%async_computation.2 | async-start | bytes 16384 | tf_op jit(solution)/shard_map/cond/branch_1_fun/all_to_all | solution.py:299
  85.1 0.0 collective-permute-done.1.refs_0_
  85.1 0.0 collective-permute-done.2.refs_1_
  85.2 0.0 collective-permute-done.3.refs_2_
  85.2 2.0 %branch_1_fun.10 = bf16[128,1152]{1,0:T(8,128)(2,1)} custom-call(f32[8,128]{1,0:T(8,128)S(1)} %get-tuple-element.37.scalars_ref, bf16[128,1152]{1,0:T(8,128)(2,1)} %get-tuple-element.38.embeds_ref, f32[128,1152]{1,0:T(8,128)S(1)} %get-tuple-element.46.cot_ref, bf16[128,1152]{1,0:T(8,128)(2,1)S(1)} %collective-permute-done.1.refs_0_, ...), custom_call_target="tpu_custom_call" | custom-call | tf_op jit(solution)/shard_map/cond/branch_1_fun/pallas_call | solution.py:25
  87.2 10.3 %all-to-all-done.2 = f32[16,1,128]{2,1,0:T(1,128)} async-done(((f32[16,1,128]{2,1,0:T(1,128)}), f32[16,1,128]{2,1,0:T(1,128)}, u32[]{:S(2)}, u32[]{:S(2)}) %all-to-all-start.2) | async-done | bytes 8224 | tf_op jit(solution)/shard_map/cond/branch_1_fun/all_to_all | solution.py:299
  97.5 0.0 collective-permute-done.5.got_ref
  97.5 1.9 %shard_map.87 = (bf16[128,1152]{1,0:T(8,128)(2,1)}, f32[1]{0:T(128)}, f32[1]{0:T(128)}, f32[1]{0:T(128)}) custom-call(f32[8,128]{1,0:T(8,128)S(1)} %get-tuple-element.84.scalars_ref, bf16[128,1152]{1,0:T(8,128)(2,1)} %embeds_ref.1, f32[128,1152]{1,0:T(8,128)S(1)} %get-tuple-element.85.cot_ref, bf16[128,1152]{1,0:T(8,128)(2,1)S(1)} %collective-permute-done.5.got_ref, ...), custom_call_target="tpu_custom_call" | custom-call | tf_op jit(solution)/shard_map/pallas_call | solution.py:25
Async XLA Ops:
  0.6 45.2 %collective-permute-start.4 = (bf16[128,1152]{1,0:T(8,128)(2,1)}, bf16[128,1152]{1,0:T(8,128)(2,1)S(1)}, u32[]{:S(2)}, u32[]{:S(2)}) collective-permute-start(bf16[128,1152]{1,0:T(8,128)(2,1)} %embeds_ref.1), channel_id=1, source_target_pairs={{0,256},{256,0},{1,257},{257,1},{2,258},{258,2},{3,259},{259,3},{4... | collective-permute-start | bytes 884744 | tf_op jit(solution)/shard_map/ppermute | solution.py:244
  17.5 24.4 %copy-start = (bf16[128,1152]{1,0:T(8,128)(2,1)S(1)}, bf16[128,1152]{1,0:T(8,128)(2,1)}, u32[]{:S(2)}) copy-start(bf16[128,1152]{1,0:T(8,128)(2,1)} %get-tuple-element.31.image_ref) | copy-start | bytes 884740 | tf_op jit(solution)/shard_map/cond
  38.1 5.3 %collective-permute-start = (bf16[4,128,1152]{2,1,0:T(8,128)(2,1)S(1)}, bf16[4,128,1152]{2,1,0:T(8,128)(2,1)}, u32[]{:S(2)}, u32[]{:S(2)}) collective-permute-start(bf16[4,128,1152]{2,1,0:T(8,128)(2,1)S(1)} %all_to_all.12.text_ref), channel_id=1, source_target_pairs={{0,32},{32,0},{1,33},{33,1},{2,34},{34,2},{3,35},{35,3},{4,36},{36... | collective-permute-start | bytes 3538952 | tf_op jit(solution)/shard_map/cond/branch_1_fun/ppermute | solution.py:249
  48.2 4.9 %collective-permute-start.6 = (bf16[528,1152]{1,0:T(8,128)(2,1)S(1)}, bf16[528,1152]{1,0:T(8,128)(2,1)S(1)}, u32[]{:S(2)}, u32[]{:S(2)}) collective-permute-start(bf16[528,1152]{1,0:T(8,128)(2,1)S(1)} %get-tuple-element.92), channel_id=1, source_target_pairs={{0,32},{32,0},{1,33},{33,1},{2,34},{34,2},{3,35},{35,3},{4,36},{36... | collective-permute-start | bytes 3649544 | tf_op jit(solution)/shard_map/ppermute | solution.py:282
  50.7 46.8 %collective-permute-start.5 = (bf16[128,1152]{1,0:T(8,128)(2,1)S(1)}, bf16[128,1152]{1,0:T(8,128)(2,1)S(1)}, u32[]{:S(2)}, u32[]{:S(2)}) collective-permute-start(bf16[128,1152]{1,0:T(8,128)(2,1)S(1)} %get-tuple-element.89), channel_id=1, source_target_pairs={{0,256},{256,0},{1,257},{257,1},{2,258},{258,2},{3,259},{259,3},{4... | collective-permute-start | bytes 884744 | tf_op jit(solution)/shard_map/ppermute | solution.py:280
  54.8 16.8 %all-to-all-start.1 = ((f32[16,48,128]{2,1,0:T(8,128)}), f32[16,48,128]{2,1,0:T(8,128)S(1)}, u32[]{:S(2)}, u32[]{:S(2)}) async-start(f32[16,48,128]{2,1,0:T(8,128)} %get-tuple-element.50), calls=%async_computation.1 | async-start | bytes 786432 | tf_op jit(solution)/shard_map/cond/branch_1_fun/all_to_all | solution.py:292
  60.2 24.9 %collective-permute-start.1 = (bf16[128,1152]{1,0:T(8,128)(2,1)}, bf16[128,1152]{1,0:T(8,128)(2,1)S(1)}, u32[]{:S(2)}, u32[]{:S(2)}) collective-permute-start(bf16[128,1152]{1,0:T(8,128)(2,1)} %get-tuple-element.47), channel_id=1, source_target_pairs={{0,64},{64,128},{128,192},{192,0},{1,65},{65,129},{129,193},{193,1... | collective-permute-start | bytes 884744 | tf_op jit(solution)/shard_map/cond/branch_1_fun/ppermute | solution.py:294
  63.6 21.5 %collective-permute-start.2 = (bf16[128,1152]{1,0:T(8,128)(2,1)}, bf16[128,1152]{1,0:T(8,128)(2,1)S(1)}, u32[]{:S(2)}, u32[]{:S(2)}) collective-permute-start(bf16[128,1152]{1,0:T(8,128)(2,1)} %get-tuple-element.48), channel_id=1, source_target_pairs={{0,128},{64,192},{128,0},{192,64},{1,129},{65,193},{129,1},{193,65... | collective-permute-start | bytes 884744 | tf_op jit(solution)/shard_map/cond/branch_1_fun/ppermute | solution.py:294
  68.2 17.0 %collective-permute-start.3 = (bf16[128,1152]{1,0:T(8,128)(2,1)S(1)}, bf16[128,1152]{1,0:T(8,128)(2,1)S(1)}, u32[]{:S(2)}, u32[]{:S(2)}) collective-permute-start(bf16[128,1152]{1,0:T(8,128)(2,1)S(1)} %get-tuple-element.49), channel_id=1, source_target_pairs={{0,192},{64,0},{128,64},{192,128},{1,193},{65,1},{129,65},{193,129... | collective-permute-start | bytes 884744 | tf_op jit(solution)/shard_map/cond/branch_1_fun/ppermute | solution.py:294
  72.3 25.2 %all-to-all-start.2 = ((f32[16,1,128]{2,1,0:T(1,128)}), f32[16,1,128]{2,1,0:T(1,128)}, u32[]{:S(2)}, u32[]{:S(2)}) async-start(f32[16,1,128]{2,1,0:T(1,128)} %branch_1_fun.11), calls=%async_computation.2 | async-start | bytes 16384 | tf_op jit(solution)/shard_map/cond/branch_1_fun/all_to_all | solution.py:299

commit v7 on v6

--- a/solution.py
+++ b/solution.py
@@ -290,13 +290,15 @@
             (y, own_mine, far_mine, image, image_far, text_got, sums),
         )
         near = lax.all_to_all(spread, near_axes, 0, 0, tiled=True)
-        got = [
-            lax.ppermute(part, "y", [(i, (i + k) % y_count) for i in range(y_count)])
-            for k, part in enumerate(text_send, 1)
-        ]
+        def shift(k):
+            return lambda part: lax.ppermute(part, "y", [(i, (i + k) % y_count) for i in range(y_count)])
+
+        order = sorted(range(1, y_count), key=lambda k: -min(k, y_count - k))
+        got = [shift(k)(text_send[k - 1]) for k in order[:-1]]
         z_axes = ("zh", "zl")
         (spread,) = call(sum_kernel, [((lax.axis_size(z_axes), 1, 128), F32)], [VMEM], (near,))
         totals = lax.all_to_all(spread, z_axes, 0, 0, tiled=True)
+        got.append(region(shift(order[-1]), y[0] < y_count, text_send[order[-1] - 1]))
         (text_grad,) = call(
             grad_kernel,
             [(block, BF16)],

time: 100 us -> 98.2 us (0.982)
  the two profiles are of different devices: /device:TPU:2 before, /device:TPU:1 now
where the time goes in v7:
time: 98.2 us; the launch traced here: 96.7 us
  starting transfers between devices  50.9 us (52%)
  blocking collectives  19.1 us (19%)
  Pallas kernels  15.7 us (16%)
  waiting for transfers between devices  10.3 us (10%)
    all_to_all x1, blocking collectives, own_pairs(): mine = lax.all_to_all(text, 'y', 0, 0, tiled=True)  19.1 us
    ppermute x1, starting transfers between devices, on_device(): image_far = lax.ppermute(image_embeds, 'zh', SWAP)  16.3 us
    pallas_call x9, Pallas kernels, call(): pl.pallas_call(kernel, out_shape=[jax.ShapeDtypeStruct(shape, dtype) for...  15.7 us
    all_to_all x1, starting transfers between devices, text_side(): totals = lax.all_to_all(spread, z_axes, 0, 0, tiled=True)  12.2 us
    ppermute x3, starting transfers between devices, shift(): lax.ppermute(part, 'y', [(i, (i + k) % y_count) for i in range(y_count)])  9.45 us
    ppermute x3, waiting for transfers between devices, shift(): lax.ppermute(part, 'y', [(i, (i + k) % y_count) for i in range(y_count)])  6.22 us
    all_to_all x1, starting transfers between devices, text_side(): near = lax.all_to_all(spread, near_axes, 0, 0, tiled=True)  4.73 us
    ppermute x1, starting transfers between devices, own_pairs(): sib = lax.ppermute(mine, 'c', SWAP)  4.35 us
  transfers between devices with their start and end apart: 9, of which 4 were waited for; matrix products, arithmetic and copies ran while one was open for 0% of the time, Pallas kernels for 12%

profile of v7, /device:TPU:1, one launch (start us, length us, event | category | flops | bytes accessed | tf_op | source)
XLA Modules:
  0.0 96.7 jit_solution(6468208782268577574)
XLA Ops:
  0.6 16.3 %collective-permute-start.4 = (bf16[128,1152]{1,0:T(8,128)(2,1)}, bf16[128,1152]{1,0:T(8,128)(2,1)S(1)}, u32[]{:S(2)}, u32[]{:S(2)}) collective-permute-start(bf16[128,1152]{1,0:T(8,128)(2,1)} %embeds_ref.1), channel_id=1, source_target_pairs={{0,256},{256,0},{1,257},{257,1},{2,258},{258,2},{3,259},{259,3},{4... | collective-permute-start | bytes 884744 | tf_op jit(solution)/shard_map/ppermute | solution.py:244
  16.9 28.0 %conditional.3 = (bf16[4,128,1152]{2,1,0:T(8,128)(2,1)S(1)}, bf16[4,128,1152]{2,1,0:T(8,128)(2,1)}, bf16[128,512]{1,0:T(8,128)(2,1)S(1)}, f32[48,128]{1,0:T(8,12...) conditional(s32[]{:T(128)} %convert_element_type.7, () %tuple.30, (f32[1]{0:T(128)}, f32[1]{0:T(128)}, ...), branch_computations={%region_0.0_spmd, %region_1.0_spmd} | conditional | bytes 8257652 | solution.py:233
  16.9 1.1 %branch_1_fun.7 = bf16[4,128,1152]{2,1,0:T(8,128)(2,1)S(1)} custom-call(bf16[128,1152]{1,0:T(8,128)(2,1)} %get-tuple-element.38.matrix_ref), custom_call_target="tpu_custom_call" | custom-call | tf_op jit(solution)/shard_map/cond/branch_1_fun/pallas_call | solution.py:25
  18.1 0.0 copy-start
  18.1 19.1 %all_to_all.12.text_ref = bf16[4,128,1152]{2,1,0:T(8,128)(2,1)S(1)} all-to-all(bf16[4,128,1152]{2,1,0:T(8,128)(2,1)S(1)} %branch_1_fun.7), channel_id=1, replica_groups=mesh['zh'=2,'y'=4,'c'=2,'zl'=8,'x'=4] {'y'}, dimensions={0} | all-to-all | bytes 2359296 | tf_op jit(solution)/shard_map/cond/branch_1_fun/all_to_all | solution.py:248
  37.2 4.4 %collective-permute-start = (bf16[4,128,1152]{2,1,0:T(8,128)(2,1)S(1)}, bf16[4,128,1152]{2,1,0:T(8,128)(2,1)}, u32[]{:S(2)}, u32[]{:S(2)}) collective-permute-start(bf16[4,128,1152]{2,1,0:T(8,128)(2,1)S(1)} %all_to_all.12.text_ref), channel_id=1, source_target_pairs={{0,32},{32,0},{1,33},{33,1},{2,34},{34,2},{3,35},{35,3},{4,36},{36... | collective-permute-start | bytes 3538952 | tf_op jit(solution)/shard_map/cond/branch_1_fun/ppermute | solution.py:249
  41.6 1.9 %branch_1_fun.6.scalars_ref = f32[8,128]{1,0:T(8,128)} custom-call(f32[1]{0:T(128)} %get-tuple-element.109.scale_ref, f32[1]{0:T(128)} %get-tuple-element.110.bias_ref), custom_call_target="tpu_custom_call" | custom-call | tf_op jit(solution)/shard_map/cond/branch_1_fun/pallas_call | solution.py:25
  43.5 0.0 copy-done
  43.5 1.5 %branch_1_fun.8 = (bf16[128,512]{1,0:T(8,128)(2,1)S(1)}, f32[48,128]{1,0:T(8,128)S(1)}, bf16[128,1152]{1,0:T(8,128)(2,1)S(1)}, bf16[4,128,1152]{2,1,0:T(8,128)(2,1)S(1)}) custom-call(f32[8,128]{1,0:T(8,128)} %branch_1_fun.6.scalars_ref, s32[1]{0:T(128)} %get-tuple-element.36.y_ref, bf16[128,1152]{1,0:T(8,128)(2,1)S(1)} %copy-done, ...), custom_call_target="tpu_custom_call" | custom-call | tf_op jit(solution)/shard_map/cond/branch_1_fun/pallas_call | solution.py:25
  45.0 0.0 collective-permute-done
  45.0 2.4 %shard_map.85 = (bf16[128,512]{1,0:T(8,128)(2,1)S(1)}, f32[128,1152]{1,0:T(8,128)S(1)}, f32[48,128]{1,0:T(8,128)S(1)}, bf16[4,128,1152]{2,1,0:T(8,128)(2,1)S(1)}, f32[8,128]{1,0:T(8,128)S(1)}) custom-call(f32[8,128]{1,0:T(8,128)} %get-tuple-element.85.scalars_ref, bf16[128,1152]{1,0:T(8,128)(2,1)S(1)} %get-tuple-element.86.image_ref, ...), custom_call_target="tpu_custom_call" | custom-call | tf_op jit(solution)/shard_map/pallas_call | solution.py:25
  47.4 0.0 collective-permute-done.4.image_far_ref
  47.4 2.4 %shard_map.86 = (bf16[128,512]{1,0:T(8,128)(2,1)S(1)}, bf16[128,1152]{1,0:T(8,128)(2,1)S(1)}, f32[48,128]{1,0:T(8,128)S(1)}, bf16[128,1152]{1,0:T(8,128)(2,1)S(1)}, bf16[528,1152]{1,0:T(8,128)(2,1)S(1)}) custom-call(f32[8,128]{1,0:T(8,128)S(1)} %get-tuple-element.91.scalars_ref, bf16[128,1152]{1,0:T(8,128)(2,1)S(1)} %get-tuple-element.86.image_ref, ...), custom_call_target="tpu_custom_call" | custom-call | tf_op jit(solution)/shard_map/pallas_call | solution.py:25
  49.7 1.9 %collective-permute-start.6 = (bf16[528,1152]{1,0:T(8,128)(2,1)S(1)}, bf16[528,1152]{1,0:T(8,128)(2,1)S(1)}, u32[]{:S(2)}, u32[]{:S(2)}) collective-permute-start(bf16[528,1152]{1,0:T(8,128)(2,1)S(1)} %get-tuple-element.99), channel_id=1, source_target_pairs={{0,32},{32,0},{1,33},{33,1},{2,34},{34,2},{3,35},{35,3},{4,36},{36... | collective-permute-start | bytes 3649544 | tf_op jit(solution)/shard_map/ppermute | solution.py:282
  51.7 1.9 %collective-permute-start.5 = (bf16[128,1152]{1,0:T(8,128)(2,1)S(1)}, bf16[128,1152]{1,0:T(8,128)(2,1)S(1)}, u32[]{:S(2)}, u32[]{:S(2)}) collective-permute-start(bf16[128,1152]{1,0:T(8,128)(2,1)S(1)} %get-tuple-element.96), channel_id=1, source_target_pairs={{0,256},{256,0},{1,257},{257,1},{2,258},{258,2},{3,259},{259,3},{4... | collective-permute-start | bytes 884744 | tf_op jit(solution)/shard_map/ppermute | solution.py:280
  53.6 0.9 collective-permute-done.6
  54.5 40.2 %conditional.4 = (bf16[128,1152]{1,0:T(8,128)(2,1)}, f32[16,1,128]{2,1,0:T(1,128)}) conditional(s32[]{:T(128)} %convert_element_type.7, () %tuple.32, (s32[1]{0:T(128)}, bf16[128,512]{1,0:T(8,128)(2,1)S(1)}, bf16[128,512]{1,0:T(8,128)(2,1)S(1)}, bf16[128,1152]{1,0:T(8,128)(2,1)S(1)}, bf16[128,1152]{1,0:T(8,128)(2,1)S(1)}, ...), branch_computations={%region_2.0_spmd, %region_3.0_spmd} | conditional | flops 2 | bytes 4743390 | solution.py:233
  54.5 1.6 %branch_1_fun.9 = (f32[16,48,128]{2,1,0:T(8,128)}, f32[128,1152]{1,0:T(8,128)S(1)}, bf16[128,1152]{1,0:T(8,128)(2,1)S(1)}, bf16[128,1152]{1,0:T(8,128)(2,1)S(1)}, bf16[128,1152]{1,0:T(8,128)(2,1)}) custom-call(s32[1]{0:T(128)} %get-tuple-element.45.y_ref, bf16[128,512]{1,0:T(8,128)(2,1)S(1)} %get-tuple-element.46.own_ref, ...), custom_call_target="tpu_custom_call" | custom-call | tf_op jit(solution)/shard_map/cond/branch_1_fun/pallas_call | solution.py:25
  56.1 4.7 %all-to-all-start.1 = ((f32[16,48,128]{2,1,0:T(8,128)}), f32[16,48,128]{2,1,0:T(8,128)S(1)}, u32[]{:S(2)}, u32[]{:S(2)}) async-start(f32[16,48,128]{2,1,0:T(8,128)} %get-tuple-element.57), calls=%async_computation.1 | async-start | bytes 786432 | tf_op jit(solution)/shard_map/cond/branch_1_fun/all_to_all | solution.py:292
  60.9 4.8 %collective-permute-start.2 = (bf16[128,1152]{1,0:T(8,128)(2,1)S(1)}, bf16[128,1152]{1,0:T(8,128)(2,1)S(1)}, u32[]{:S(2)}, u32[]{:S(2)}) collective-permute-start(bf16[128,1152]{1,0:T(8,128)(2,1)S(1)} %get-tuple-element.53), channel_id=1, source_target_pairs={{0,128},{64,192},{128,0},{192,64},{1,129},{65,193},{129,1},{193,65... | collective-permute-start | bytes 884744 | tf_op jit(solution)/shard_map/cond/branch_1_fun/ppermute | solution.py:294
  65.7 2.2 %collective-permute-start.3 = (bf16[128,1152]{1,0:T(8,128)(2,1)S(1)}, bf16[128,1152]{1,0:T(8,128)(2,1)S(1)}, u32[]{:S(2)}, u32[]{:S(2)}) collective-permute-start(bf16[128,1152]{1,0:T(8,128)(2,1)S(1)} %get-tuple-element.54), channel_id=1, source_target_pairs={{0,64},{64,128},{128,192},{192,0},{1,65},{65,129},{129,193},{193,1... | collective-permute-start | bytes 884744 | tf_op jit(solution)/shard_map/cond/branch_1_fun/ppermute | solution.py:294
  67.9 2.8 %all-to-all-done.1.near_ref = f32[16,48,128]{2,1,0:T(8,128)S(1)} async-done(((f32[16,48,128]{2,1,0:T(8,128)}), f32[16,48,128]{2,1,0:T(8,128)S(1)}, u32[]{:S(2)}, u32[]{:S(2)}) %all-to-all-start.1) | async-done | bytes 393248 | tf_op jit(solution)/shard_map/cond/branch_1_fun/all_to_all | solution.py:292
  70.6 0.7 branch_1_fun.11
  71.4 12.2 %all-to-all-start.2 = ((f32[16,1,128]{2,1,0:T(1,128)}), f32[16,1,128]{2,1,0:T(1,128)}, u32[]{:S(2)}, u32[]{:S(2)}) async-start(f32[16,1,128]{2,1,0:T(1,128)} %branch_1_fun.11), calls=%async_computation.2 | async-start | bytes 16384 | tf_op jit(solution)/shard_map/cond/branch_1_fun/all_to_all | solution.py:300
  83.6 8.7 %conditional = (bf16[128,1152]{1,0:T(8,128)(2,1)}) conditional(s32[]{:T(128)} %convert_element_type.1, () %tuple.22, bf16[128,1152]{1,0:T(8,128)(2,1)} %get-tuple-element.56), branch_computations={%region_4.0_spmd, %region_5.0_spmd} | conditional | bytes 1179696 | solution.py:233
  83.6 2.5 %collective-permute-start.1 = (bf16[128,1152]{1,0:T(8,128)(2,1)}, bf16[128,1152]{1,0:T(8,128)(2,1)}, u32[]{:S(2)}, u32[]{:S(2)}) collective-permute-start(bf16[128,1152]{1,0:T(8,128)(2,1)} %param.4), channel_id=1, source_target_pairs={{0,192},{64,0},{128,64},{192,128},{1,193},{65,1},{129,65},{193,129... | collective-permute-start | bytes 884744 | tf_op jit(solution)/shard_map/cond/branch_1_fun/cond/branch_1_fun/ppermute | solution.py:294
  86.1 6.2 %collective-permute-done.1 = bf16[128,1152]{1,0:T(8,128)(2,1)} collective-permute-done((bf16[128,1152]{1,0:T(8,128)(2,1)}, bf16[128,1152]{1,0:T(8,128)(2,1)}, u32[]{:S(2)}, u32[]{:S(2)}) %collective-permute-start.1) | collective-permute-done | bytes 294944 | tf_op jit(solution)/shard_map/cond/branch_1_fun/cond/branch_1_fun/ppermute | solution.py:294
  92.3 0.0 collective-permute-done.2.refs_0_
  92.3 0.0 collective-permute-done.3.refs_1_
  92.3 2.1 %branch_1_fun.10 = bf16[128,1152]{1,0:T(8,128)(2,1)} custom-call(f32[8,128]{1,0:T(8,128)S(1)} %get-tuple-element.43.scalars_ref, bf16[128,1152]{1,0:T(8,128)(2,1)} %get-tuple-element.44.embeds_ref, f32[128,1152]{1,0:T(8,128)S(1)} %get-tuple-element.52.cot_ref, bf16[128,1152]{1,0:T(8,128)(2,1)S(1)} %collective-permute-done.2.refs_0_, ...), custom_call_target="tpu_custom_call" | custom-call | tf_op jit(solution)/shard_map/cond/branch_1_fun/pallas_call | solution.py:25
  94.4 0.3 all-to-all-done.2
  94.7 0.0 collective-permute-done.5.got_ref
  94.7 2.0 %shard_map.87 = (bf16[128,1152]{1,0:T(8,128)(2,1)}, f32[1]{0:T(128)}, f32[1]{0:T(128)}, f32[1]{0:T(128)}) custom-call(f32[8,128]{1,0:T(8,128)S(1)} %get-tuple-element.91.scalars_ref, bf16[128,1152]{1,0:T(8,128)(2,1)} %embeds_ref.1, f32[128,1152]{1,0:T(8,128)S(1)} %get-tuple-element.92.cot_ref, bf16[128,1152]{1,0:T(8,128)(2,1)S(1)} %collective-permute-done.5.got_ref, ...), custom_call_target="tpu_custom_call" | custom-call | tf_op jit(solution)/shard_map/pallas_call | solution.py:25
Async XLA Ops:
  0.6 46.7 %collective-permute-start.4 = (bf16[128,1152]{1,0:T(8,128)(2,1)}, bf16[128,1152]{1,0:T(8,128)(2,1)S(1)}, u32[]{:S(2)}, u32[]{:S(2)}) collective-permute-start(bf16[128,1152]{1,0:T(8,128)(2,1)} %embeds_ref.1), channel_id=1, source_target_pairs={{0,256},{256,0},{1,257},{257,1},{2,258},{258,2},{3,259},{259,3},{4... | collective-permute-start | bytes 884744 | tf_op jit(solution)/shard_map/ppermute | solution.py:244
  18.1 25.4 %copy-start = (bf16[128,1152]{1,0:T(8,128)(2,1)S(1)}, bf16[128,1152]{1,0:T(8,128)(2,1)}, u32[]{:S(2)}) copy-start(bf16[128,1152]{1,0:T(8,128)(2,1)} %get-tuple-element.37.image_ref) | copy-start | bytes 884740 | tf_op jit(solution)/shard_map/cond
  37.2 7.8 %collective-permute-start = (bf16[4,128,1152]{2,1,0:T(8,128)(2,1)S(1)}, bf16[4,128,1152]{2,1,0:T(8,128)(2,1)}, u32[]{:S(2)}, u32[]{:S(2)}) collective-permute-start(bf16[4,128,1152]{2,1,0:T(8,128)(2,1)S(1)} %all_to_all.12.text_ref), channel_id=1, source_target_pairs={{0,32},{32,0},{1,33},{33,1},{2,34},{34,2},{3,35},{35,3},{4,36},{36... | collective-permute-start | bytes 3538952 | tf_op jit(solution)/shard_map/cond/branch_1_fun/ppermute | solution.py:249
  49.7 4.8 %collective-permute-start.6 = (bf16[528,1152]{1,0:T(8,128)(2,1)S(1)}, bf16[528,1152]{1,0:T(8,128)(2,1)S(1)}, u32[]{:S(2)}, u32[]{:S(2)}) collective-permute-start(bf16[528,1152]{1,0:T(8,128)(2,1)S(1)} %get-tuple-element.99), channel_id=1, source_target_pairs={{0,32},{32,0},{1,33},{33,1},{2,34},{34,2},{3,35},{35,3},{4,36},{36... | collective-permute-start | bytes 3649544 | tf_op jit(solution)/shard_map/ppermute | solution.py:282
  51.7 43.1 %collective-permute-start.5 = (bf16[128,1152]{1,0:T(8,128)(2,1)S(1)}, bf16[128,1152]{1,0:T(8,128)(2,1)S(1)}, u32[]{:S(2)}, u32[]{:S(2)}) collective-permute-start(bf16[128,1152]{1,0:T(8,128)(2,1)S(1)} %get-tuple-element.96), channel_id=1, source_target_pairs={{0,256},{256,0},{1,257},{257,1},{2,258},{258,2},{3,259},{259,3},{4... | collective-permute-start | bytes 884744 | tf_op jit(solution)/shard_map/ppermute | solution.py:280
  56.1 14.5 %all-to-all-start.1 = ((f32[16,48,128]{2,1,0:T(8,128)}), f32[16,48,128]{2,1,0:T(8,128)S(1)}, u32[]{:S(2)}, u32[]{:S(2)}) async-start(f32[16,48,128]{2,1,0:T(8,128)} %get-tuple-element.57), calls=%async_computation.1 | async-start | bytes 786432 | tf_op jit(solution)/shard_map/cond/branch_1_fun/all_to_all | solution.py:292
  60.9 31.4 %collective-permute-start.2 = (bf16[128,1152]{1,0:T(8,128)(2,1)S(1)}, bf16[128,1152]{1,0:T(8,128)(2,1)S(1)}, u32[]{:S(2)}, u32[]{:S(2)}) collective-permute-start(bf16[128,1152]{1,0:T(8,128)(2,1)S(1)} %get-tuple-element.53), channel_id=1, source_target_pairs={{0,128},{64,192},{128,0},{192,64},{1,129},{65,193},{129,1},{193,65... | collective-permute-start | bytes 884744 | tf_op jit(solution)/shard_map/cond/branch_1_fun/ppermute | solution.py:294
  65.7 26.7 %collective-permute-start.3 = (bf16[128,1152]{1,0:T(8,128)(2,1)S(1)}, bf16[128,1152]{1,0:T(8,128)(2,1)S(1)}, u32[]{:S(2)}, u32[]{:S(2)}) collective-permute-start(bf16[128,1152]{1,0:T(8,128)(2,1)S(1)} %get-tuple-element.54), channel_id=1, source_target_pairs={{0,64},{64,128},{128,192},{192,0},{1,65},{65,129},{129,193},{193,1... | collective-permute-start | bytes 884744 | tf_op jit(solution)/shard_map/cond/branch_1_fun/ppermute | solution.py:294
  71.4 23.4 %all-to-all-start.2 = ((f32[16,1,128]{2,1,0:T(1,128)}), f32[16,1,128]{2,1,0:T(1,128)}, u32[]{:S(2)}, u32[]{:S(2)}) async-start(f32[16,1,128]{2,1,0:T(1,128)} %branch_1_fun.11), calls=%async_computation.2 | async-start | bytes 16384 | tf_op jit(solution)/shard_map/cond/branch_1_fun/all_to_all | solution.py:300
  83.6 8.7 %collective-permute-start.1 = (bf16[128,1152]{1,0:T(8,128)(2,1)}, bf16[128,1152]{1,0:T(8,128)(2,1)}, u32[]{:S(2)}, u32[]{:S(2)}) collective-permute-start(bf16[128,1152]{1,0:T(8,128)(2,1)} %param.4), channel_id=1, source_target_pairs={{0,192},{64,0},{128,64},{192,128},{1,193},{65,1},{129,65},{193,129... | collective-permute-start | bytes 884744 | tf_op jit(solution)/shard_map/cond/branch_1_fun/cond/branch_1_fun/ppermute | solution.py:294

commit v8 on v7

--- a/solution.py
+++ b/solution.py
@@ -17,7 +17,7 @@
 SMEM = pl.BlockSpec(memory_space=pltpu.SMEM)
 PARAMS = pltpu.CompilerParams(vmem_limit_bytes=16 * 1024 * 1024)
 SWAP = ((0, 1), (1, 0))
-CHUNK = 256
+CHUNK = 512
 PART = 16
 
 

time: 98.2 us -> 98.3 us (level)
  no operation moved by 1% of the time
where the time goes in v8:
time: 98.3 us; the launch traced here: 96.7 us
  starting transfers between devices  51 us (52%)
  blocking collectives  19.1 us (19%)
  Pallas kernels  15.6 us (16%)
  waiting for transfers between devices  10.3 us (10%)
    all_to_all x1, blocking collectives, own_pairs(): mine = lax.all_to_all(text, 'y', 0, 0, tiled=True)  19.1 us
    ppermute x1, starting transfers between devices, on_device(): image_far = lax.ppermute(image_embeds, 'zh', SWAP)  16.3 us
    pallas_call x9, Pallas kernels, call(): pl.pallas_call(kernel, out_shape=[jax.ShapeDtypeStruct(shape, dtype) for...  15.6 us
    all_to_all x1, starting transfers between devices, text_side(): totals = lax.all_to_all(spread, z_axes, 0, 0, tiled=True)  12.4 us
    ppermute x3, starting transfers between devices, shift(): lax.ppermute(part, 'y', [(i, (i + k) % y_count) for i in range(y_count)])  9.45 us
    ppermute x3, waiting for transfers between devices, shift(): lax.ppermute(part, 'y', [(i, (i + k) % y_count) for i in range(y_count)])  6.22 us
    all_to_all x1, starting transfers between devices, text_side(): near = lax.all_to_all(spread, near_axes, 0, 0, tiled=True)  4.73 us
    ppermute x1, starting transfers between devices, own_pairs(): sib = lax.ppermute(mine, 'c', SWAP)  4.35 us
  transfers between devices with their start and end apart: 9, of which 4 were waited for; matrix products, arithmetic and copies ran while one was open for 0% of the time, Pallas kernels for 12%

profile of v8, /device:TPU:1, one launch (start us, length us, event | category | flops | bytes accessed | tf_op | source)
XLA Modules:
  0.0 96.7 jit_solution(18048858541252238600)
XLA Ops:
  0.6 16.3 %collective-permute-start.4 = (bf16[128,1152]{1,0:T(8,128)(2,1)}, bf16[128,1152]{1,0:T(8,128)(2,1)S(1)}, u32[]{:S(2)}, u32[]{:S(2)}) collective-permute-start(bf16[128,1152]{1,0:T(8,128)(2,1)} %embeds_ref.1), channel_id=1, source_target_pairs={{0,256},{256,0},{1,257},{257,1},{2,258},{258,2},{3,259},{259,3},{4... | collective-permute-start | bytes 884744 | tf_op jit(solution)/shard_map/ppermute | solution.py:244
  16.9 28.0 %conditional.3 = (bf16[4,128,1152]{2,1,0:T(8,128)(2,1)S(1)}, bf16[4,128,1152]{2,1,0:T(8,128)(2,1)}, bf16[128,512]{1,0:T(8,128)(2,1)S(1)}, f32[48,128]{1,0:T(8,12...) conditional(s32[]{:T(128)} %convert_element_type.7, () %tuple.30, (f32[1]{0:T(128)}, f32[1]{0:T(128)}, ...), branch_computations={%region_0.0_spmd, %region_1.0_spmd} | conditional | bytes 8257652 | solution.py:233
  16.9 1.1 %branch_1_fun.7 = bf16[4,128,1152]{2,1,0:T(8,128)(2,1)S(1)} custom-call(bf16[128,1152]{1,0:T(8,128)(2,1)} %get-tuple-element.38.matrix_ref), custom_call_target="tpu_custom_call" | custom-call | tf_op jit(solution)/shard_map/cond/branch_1_fun/pallas_call | solution.py:25
  18.1 0.0 copy-start
  18.1 19.1 %all_to_all.12.text_ref = bf16[4,128,1152]{2,1,0:T(8,128)(2,1)S(1)} all-to-all(bf16[4,128,1152]{2,1,0:T(8,128)(2,1)S(1)} %branch_1_fun.7), channel_id=1, replica_groups=mesh['zh'=2,'y'=4,'c'=2,'zl'=8,'x'=4] {'y'}, dimensions={0} | all-to-all | bytes 2359296 | tf_op jit(solution)/shard_map/cond/branch_1_fun/all_to_all | solution.py:248
  37.2 4.4 %collective-permute-start = (bf16[4,128,1152]{2,1,0:T(8,128)(2,1)S(1)}, bf16[4,128,1152]{2,1,0:T(8,128)(2,1)}, u32[]{:S(2)}, u32[]{:S(2)}) collective-permute-start(bf16[4,128,1152]{2,1,0:T(8,128)(2,1)S(1)} %all_to_all.12.text_ref), channel_id=1, source_target_pairs={{0,32},{32,0},{1,33},{33,1},{2,34},{34,2},{3,35},{35,3},{4,36},{36... | collective-permute-start | bytes 3538952 | tf_op jit(solution)/shard_map/cond/branch_1_fun/ppermute | solution.py:249
  41.6 1.9 %branch_1_fun.6.scalars_ref = f32[8,128]{1,0:T(8,128)} custom-call(f32[1]{0:T(128)} %get-tuple-element.109.scale_ref, f32[1]{0:T(128)} %get-tuple-element.110.bias_ref), custom_call_target="tpu_custom_call" | custom-call | tf_op jit(solution)/shard_map/cond/branch_1_fun/pallas_call | solution.py:25
  43.5 0.0 copy-done
  43.5 1.5 %branch_1_fun.8 = (bf16[128,512]{1,0:T(8,128)(2,1)S(1)}, f32[48,128]{1,0:T(8,128)S(1)}, bf16[128,1152]{1,0:T(8,128)(2,1)S(1)}, bf16[4,128,1152]{2,1,0:T(8,128)(2,1)S(1)}) custom-call(f32[8,128]{1,0:T(8,128)} %branch_1_fun.6.scalars_ref, s32[1]{0:T(128)} %get-tuple-element.36.y_ref, bf16[128,1152]{1,0:T(8,128)(2,1)S(1)} %copy-done, ...), custom_call_target="tpu_custom_call" | custom-call | tf_op jit(solution)/shard_map/cond/branch_1_fun/pallas_call | solution.py:25
  45.0 0.0 collective-permute-done
  45.0 2.3 %shard_map.85 = (bf16[128,512]{1,0:T(8,128)(2,1)S(1)}, f32[128,1152]{1,0:T(8,128)S(1)}, f32[48,128]{1,0:T(8,128)S(1)}, bf16[4,128,1152]{2,1,0:T(8,128)(2,1)S(1)}, f32[8,128]{1,0:T(8,128)S(1)}) custom-call(f32[8,128]{1,0:T(8,128)} %get-tuple-element.85.scalars_ref, bf16[128,1152]{1,0:T(8,128)(2,1)S(1)} %get-tuple-element.86.image_ref, ...), custom_call_target="tpu_custom_call" | custom-call | tf_op jit(solution)/shard_map/pallas_call | solution.py:25
  47.2 0.0 collective-permute-done.4.image_far_ref
  47.2 2.4 %shard_map.86 = (bf16[128,512]{1,0:T(8,128)(2,1)S(1)}, bf16[128,1152]{1,0:T(8,128)(2,1)S(1)}, f32[48,128]{1,0:T(8,128)S(1)}, bf16[128,1152]{1,0:T(8,128)(2,1)S(1)}, bf16[528,1152]{1,0:T(8,128)(2,1)S(1)}) custom-call(f32[8,128]{1,0:T(8,128)S(1)} %get-tuple-element.91.scalars_ref, bf16[128,1152]{1,0:T(8,128)(2,1)S(1)} %get-tuple-element.86.image_ref, ...), custom_call_target="tpu_custom_call" | custom-call | tf_op jit(solution)/shard_map/pallas_call | solution.py:25
  49.6 1.9 %collective-permute-start.6 = (bf16[528,1152]{1,0:T(8,128)(2,1)S(1)}, bf16[528,1152]{1,0:T(8,128)(2,1)S(1)}, u32[]{:S(2)}, u32[]{:S(2)}) collective-permute-start(bf16[528,1152]{1,0:T(8,128)(2,1)S(1)} %get-tuple-element.99), channel_id=1, source_target_pairs={{0,32},{32,0},{1,33},{33,1},{2,34},{34,2},{3,35},{35,3},{4,36},{36... | collective-permute-start | bytes 3649544 | tf_op jit(solution)/shard_map/ppermute | solution.py:282
  51.6 1.9 %collective-permute-start.5 = (bf16[128,1152]{1,0:T(8,128)(2,1)S(1)}, bf16[128,1152]{1,0:T(8,128)(2,1)S(1)}, u32[]{:S(2)}, u32[]{:S(2)}) collective-permute-start(bf16[128,1152]{1,0:T(8,128)(2,1)S(1)} %get-tuple-element.96), channel_id=1, source_target_pairs={{0,256},{256,0},{1,257},{257,1},{2,258},{258,2},{3,259},{259,3},{4... | collective-permute-start | bytes 884744 | tf_op jit(solution)/shard_map/ppermute | solution.py:280
  53.5 0.9 collective-permute-done.6
  54.4 40.3 %conditional.4 = (bf16[128,1152]{1,0:T(8,128)(2,1)}, f32[16,1,128]{2,1,0:T(1,128)}) conditional(s32[]{:T(128)} %convert_element_type.7, () %tuple.32, (s32[1]{0:T(128)}, bf16[128,512]{1,0:T(8,128)(2,1)S(1)}, bf16[128,512]{1,0:T(8,128)(2,1)S(1)}, bf16[128,1152]{1,0:T(8,128)(2,1)S(1)}, bf16[128,1152]{1,0:T(8,128)(2,1)S(1)}, ...), branch_computations={%region_2.0_spmd, %region_3.0_spmd} | conditional | flops 2 | bytes 4743390 | solution.py:233
  54.4 1.6 %branch_1_fun.9 = (f32[16,48,128]{2,1,0:T(8,128)}, f32[128,1152]{1,0:T(8,128)S(1)}, bf16[128,1152]{1,0:T(8,128)(2,1)S(1)}, bf16[128,1152]{1,0:T(8,128)(2,1)S(1)}, bf16[128,1152]{1,0:T(8,128)(2,1)}) custom-call(s32[1]{0:T(128)} %get-tuple-element.45.y_ref, bf16[128,512]{1,0:T(8,128)(2,1)S(1)} %get-tuple-element.46.own_ref, ...), custom_call_target="tpu_custom_call" | custom-call | tf_op jit(solution)/shard_map/cond/branch_1_fun/pallas_call | solution.py:25
  56.0 4.7 %all-to-all-start.1 = ((f32[16,48,128]{2,1,0:T(8,128)}), f32[16,48,128]{2,1,0:T(8,128)S(1)}, u32[]{:S(2)}, u32[]{:S(2)}) async-start(f32[16,48,128]{2,1,0:T(8,128)} %get-tuple-element.57), calls=%async_computation.1 | async-start | bytes 786432 | tf_op jit(solution)/shard_map/cond/branch_1_fun/all_to_all | solution.py:292
  60.8 4.8 %collective-permute-start.2 = (bf16[128,1152]{1,0:T(8,128)(2,1)S(1)}, bf16[128,1152]{1,0:T(8,128)(2,1)S(1)}, u32[]{:S(2)}, u32[]{:S(2)}) collective-permute-start(bf16[128,1152]{1,0:T(8,128)(2,1)S(1)} %get-tuple-element.53), channel_id=1, source_target_pairs={{0,128},{64,192},{128,0},{192,64},{1,129},{65,193},{129,1},{193,65... | collective-permute-start | bytes 884744 | tf_op jit(solution)/shard_map/cond/branch_1_fun/ppermute | solution.py:294
  65.6 2.2 %collective-permute-start.3 = (bf16[128,1152]{1,0:T(8,128)(2,1)S(1)}, bf16[128,1152]{1,0:T(8,128)(2,1)S(1)}, u32[]{:S(2)}, u32[]{:S(2)}) collective-permute-start(bf16[128,1152]{1,0:T(8,128)(2,1)S(1)} %get-tuple-element.54), channel_id=1, source_target_pairs={{0,64},{64,128},{128,192},{192,0},{1,65},{65,129},{129,193},{193,1... | collective-permute-start | bytes 884744 | tf_op jit(solution)/shard_map/cond/branch_1_fun/ppermute | solution.py:294
  67.8 2.8 %all-to-all-done.1.near_ref = f32[16,48,128]{2,1,0:T(8,128)S(1)} async-done(((f32[16,48,128]{2,1,0:T(8,128)}), f32[16,48,128]{2,1,0:T(8,128)S(1)}, u32[]{:S(2)}, u32[]{:S(2)}) %all-to-all-start.1) | async-done | bytes 393248 | tf_op jit(solution)/shard_map/cond/branch_1_fun/all_to_all | solution.py:292
  70.6 0.7 branch_1_fun.11
  71.3 12.4 %all-to-all-start.2 = ((f32[16,1,128]{2,1,0:T(1,128)}), f32[16,1,128]{2,1,0:T(1,128)}, u32[]{:S(2)}, u32[]{:S(2)}) async-start(f32[16,1,128]{2,1,0:T(1,128)} %branch_1_fun.11), calls=%async_computation.2 | async-start | bytes 16384 | tf_op jit(solution)/shard_map/cond/branch_1_fun/all_to_all | solution.py:300
  83.6 8.7 %conditional = (bf16[128,1152]{1,0:T(8,128)(2,1)}) conditional(s32[]{:T(128)} %convert_element_type.1, () %tuple.22, bf16[128,1152]{1,0:T(8,128)(2,1)} %get-tuple-element.56), branch_computations={%region_4.0_spmd, %region_5.0_spmd} | conditional | bytes 1179696 | solution.py:233
  83.6 2.5 %collective-permute-start.1 = (bf16[128,1152]{1,0:T(8,128)(2,1)}, bf16[128,1152]{1,0:T(8,128)(2,1)}, u32[]{:S(2)}, u32[]{:S(2)}) collective-permute-start(bf16[128,1152]{1,0:T(8,128)(2,1)} %param.4), channel_id=1, source_target_pairs={{0,192},{64,0},{128,64},{192,128},{1,193},{65,1},{129,65},{193,129... | collective-permute-start | bytes 884744 | tf_op jit(solution)/shard_map/cond/branch_1_fun/cond/branch_1_fun/ppermute | solution.py:294
  86.1 6.2 %collective-permute-done.1 = bf16[128,1152]{1,0:T(8,128)(2,1)} collective-permute-done((bf16[128,1152]{1,0:T(8,128)(2,1)}, bf16[128,1152]{1,0:T(8,128)(2,1)}, u32[]{:S(2)}, u32[]{:S(2)}) %collective-permute-start.1) | collective-permute-done | bytes 294944 | tf_op jit(solution)/shard_map/cond/branch_1_fun/cond/branch_1_fun/ppermute | solution.py:294
  92.4 0.0 collective-permute-done.2.refs_0_
  92.4 0.0 collective-permute-done.3.refs_1_
  92.4 2.1 %branch_1_fun.10 = bf16[128,1152]{1,0:T(8,128)(2,1)} custom-call(f32[8,128]{1,0:T(8,128)S(1)} %get-tuple-element.43.scalars_ref, bf16[128,1152]{1,0:T(8,128)(2,1)} %get-tuple-element.44.embeds_ref, f32[128,1152]{1,0:T(8,128)S(1)} %get-tuple-element.52.cot_ref, bf16[128,1152]{1,0:T(8,128)(2,1)S(1)} %collective-permute-done.2.refs_0_, ...), custom_call_target="tpu_custom_call" | custom-call | tf_op jit(solution)/shard_map/cond/branch_1_fun/pallas_call | solution.py:25
  94.5 0.3 all-to-all-done.2
  94.8 0.0 collective-permute-done.5.got_ref
  94.8 2.0 %shard_map.87 = (bf16[128,1152]{1,0:T(8,128)(2,1)}, f32[1]{0:T(128)}, f32[1]{0:T(128)}, f32[1]{0:T(128)}) custom-call(f32[8,128]{1,0:T(8,128)S(1)} %get-tuple-element.91.scalars_ref, bf16[128,1152]{1,0:T(8,128)(2,1)} %embeds_ref.1, f32[128,1152]{1,0:T(8,128)S(1)} %get-tuple-element.92.cot_ref, bf16[128,1152]{1,0:T(8,128)(2,1)S(1)} %collective-permute-done.5.got_ref, ...), custom_call_target="tpu_custom_call" | custom-call | tf_op jit(solution)/shard_map/pallas_call | solution.py:25
Async XLA Ops:
  0.6 46.6 %collective-permute-start.4 = (bf16[128,1152]{1,0:T(8,128)(2,1)}, bf16[128,1152]{1,0:T(8,128)(2,1)S(1)}, u32[]{:S(2)}, u32[]{:S(2)}) collective-permute-start(bf16[128,1152]{1,0:T(8,128)(2,1)} %embeds_ref.1), channel_id=1, source_target_pairs={{0,256},{256,0},{1,257},{257,1},{2,258},{258,2},{3,259},{259,3},{4... | collective-permute-start | bytes 884744 | tf_op jit(solution)/shard_map/ppermute | solution.py:244
  18.1 25.4 %copy-start = (bf16[128,1152]{1,0:T(8,128)(2,1)S(1)}, bf16[128,1152]{1,0:T(8,128)(2,1)}, u32[]{:S(2)}) copy-start(bf16[128,1152]{1,0:T(8,128)(2,1)} %get-tuple-element.37.image_ref) | copy-start | bytes 884740 | tf_op jit(solution)/shard_map/cond
  37.2 7.8 %collective-permute-start = (bf16[4,128,1152]{2,1,0:T(8,128)(2,1)S(1)}, bf16[4,128,1152]{2,1,0:T(8,128)(2,1)}, u32[]{:S(2)}, u32[]{:S(2)}) collective-permute-start(bf16[4,128,1152]{2,1,0:T(8,128)(2,1)S(1)} %all_to_all.12.text_ref), channel_id=1, source_target_pairs={{0,32},{32,0},{1,33},{33,1},{2,34},{34,2},{3,35},{35,3},{4,36},{36... | collective-permute-start | bytes 3538952 | tf_op jit(solution)/shard_map/cond/branch_1_fun/ppermute | solution.py:249
  49.6 4.8 %collective-permute-start.6 = (bf16[528,1152]{1,0:T(8,128)(2,1)S(1)}, bf16[528,1152]{1,0:T(8,128)(2,1)S(1)}, u32[]{:S(2)}, u32[]{:S(2)}) collective-permute-start(bf16[528,1152]{1,0:T(8,128)(2,1)S(1)} %get-tuple-element.99), channel_id=1, source_target_pairs={{0,32},{32,0},{1,33},{33,1},{2,34},{34,2},{3,35},{35,3},{4,36},{36... | collective-permute-start | bytes 3649544 | tf_op jit(solution)/shard_map/ppermute | solution.py:282
  51.6 43.2 %collective-permute-start.5 = (bf16[128,1152]{1,0:T(8,128)(2,1)S(1)}, bf16[128,1152]{1,0:T(8,128)(2,1)S(1)}, u32[]{:S(2)}, u32[]{:S(2)}) collective-permute-start(bf16[128,1152]{1,0:T(8,128)(2,1)S(1)} %get-tuple-element.96), channel_id=1, source_target_pairs={{0,256},{256,0},{1,257},{257,1},{2,258},{258,2},{3,259},{259,3},{4... | collective-permute-start | bytes 884744 | tf_op jit(solution)/shard_map/ppermute | solution.py:280
  56.0 14.5 %all-to-all-start.1 = ((f32[16,48,128]{2,1,0:T(8,128)}), f32[16,48,128]{2,1,0:T(8,128)S(1)}, u32[]{:S(2)}, u32[]{:S(2)}) async-start(f32[16,48,128]{2,1,0:T(8,128)} %get-tuple-element.57), calls=%async_computation.1 | async-start | bytes 786432 | tf_op jit(solution)/shard_map/cond/branch_1_fun/all_to_all | solution.py:292
  60.8 31.6 %collective-permute-start.2 = (bf16[128,1152]{1,0:T(8,128)(2,1)S(1)}, bf16[128,1152]{1,0:T(8,128)(2,1)S(1)}, u32[]{:S(2)}, u32[]{:S(2)}) collective-permute-start(bf16[128,1152]{1,0:T(8,128)(2,1)S(1)} %get-tuple-element.53), channel_id=1, source_target_pairs={{0,128},{64,192},{128,0},{192,64},{1,129},{65,193},{129,1},{193,65... | collective-permute-start | bytes 884744 | tf_op jit(solution)/shard_map/cond/branch_1_fun/ppermute | solution.py:294
  65.6 26.8 %collective-permute-start.3 = (bf16[128,1152]{1,0:T(8,128)(2,1)S(1)}, bf16[128,1152]{1,0:T(8,128)(2,1)S(1)}, u32[]{:S(2)}, u32[]{:S(2)}) collective-permute-start(bf16[128,1152]{1,0:T(8,128)(2,1)S(1)} %get-tuple-element.54), channel_id=1, source_target_pairs={{0,64},{64,128},{128,192},{192,0},{1,65},{65,129},{129,193},{193,1... | collective-permute-start | bytes 884744 | tf_op jit(solution)/shard_map/cond/branch_1_fun/ppermute | solution.py:294
  71.3 23.5 %all-to-all-start.2 = ((f32[16,1,128]{2,1,0:T(1,128)}), f32[16,1,128]{2,1,0:T(1,128)}, u32[]{:S(2)}, u32[]{:S(2)}) async-start(f32[16,1,128]{2,1,0:T(1,128)} %branch_1_fun.11), calls=%async_computation.2 | async-start | bytes 16384 | tf_op jit(solution)/shard_map/cond/branch_1_fun/all_to_all | solution.py:300
  83.6 8.7 %collective-permute-start.1 = (bf16[128,1152]{1,0:T(8,128)(2,1)}, bf16[128,1152]{1,0:T(8,128)(2,1)}, u32[]{:S(2)}, u32[]{:S(2)}) collective-permute-start(bf16[128,1152]{1,0:T(8,128)(2,1)} %param.4), channel_id=1, source_target_pairs={{0,192},{64,0},{128,64},{192,128},{1,193},{65,1},{129,65},{193,129... | collective-permute-start | bytes 884744 | tf_op jit(solution)/shard_map/cond/branch_1_fun/cond/branch_1_fun/ppermute | solution.py:294
